TPU v7x, 32 devices: a whole 2x2x4 slice. The times are simulated.
32 devices in a mesh: energy: 4 (over y, core), space: 8 (over z, x).
Axes of the slice: x: 2, y: 2, z: 4, core: 2. Of those that a mesh axis runs over, the one named last changes fastest.
Arguments:
- green_blocks: float32 [4, 16, 2, 1024, 1024], P('energy', 'space'), may hold values from -0.078125 to 0.078125
- injection: float32 [4, 16, 2, 1024], P('energy', 'space'), may hold values from 0.3 to 27
- mesh_state_choice: int32 [256, 64, 128], P('space'), may hold values from 0 to 1023
- regions: int32 [256, 64, 128], P('space', 'energy'), may hold values from 0 to 2
- dopant_charge_field: float32 [256, 64, 128], P('space', 'energy'), may hold values from -18 to 32
- earlier_voltage: float32 [256, 64, 128], P('space'), may hold values from -3 to 3
Outputs:
- potential: float32 [256, 64, 128], P('space')
All inputs are finite; a program needn't handle non-finite values. Where the computation divides by a largest or mean magnitude, that divisor is 1e-20 or more.
Results may differ from a plain program's by a relative error of at most 0.00007.
Values sent between devices are 32-bit elements; how exact they have to be, the bound alone decides.
No kernel may reach another device: no remote copies, remote signals or barrier semaphores. Data moves between devices by JAX's collectives and lax.ppermute only.
A program may use at most 320 MiB of HBM per device.

v0:
```python
import jax
import jax.numpy as jnp
from jax import lax
from jax.sharding import PartitionSpec as P

ATOMIC_STATES = 1024
PL = 16
SWEEPS = 4


def with_halo(block, sides, width):
    for axis, dim in sides:
        count = lax.axis_size(axis)
        forward = [(i, i + 1) for i in range(count - 1)]
        backward = [(target, source) for source, target in forward]
        low = lax.ppermute(
            lax.slice_in_dim(block, block.shape[dim] - width, None, axis=dim), axis, forward
        )
        high = lax.ppermute(lax.slice_in_dim(block, 0, width, axis=dim), axis, backward)
        block = jnp.concatenate([low, block, high], axis=dim)
    return block


def permittivity(regions):
    return jnp.where(regions == 0, 1.0, jnp.where(regions == 1, 0.33, 1.7)).astype(jnp.float32)


def smoothed_voxels(
    haloed_voltage, dielectric_mesh, dopant_charge_field, electrons, hole_density, old_field
):
    center = haloed_voltage[1:-1, 1:-1, :]
    along_z = jnp.pad(center, ((0, 0), (0, 0), (1, 1)))
    neighbours = haloed_voltage[2:, 1:-1, :] + haloed_voltage[:-2, 1:-1, :]
    neighbours = neighbours + haloed_voltage[1:-1, 2:, :] + haloed_voltage[1:-1, :-2, :]
    neighbours = neighbours + along_z[:, :, 2:] + along_z[:, :, :-2]
    raised = jnp.exp(center - old_field)
    lowered = jnp.exp(old_field - center)
    mismatch = dielectric_mesh * (6.0 * center - neighbours) - (
        dopant_charge_field + hole_density * lowered - electrons * raised
    )
    jacobian = 6.0 * dielectric_mesh + electrons * raised + hole_density * lowered
    return center - mismatch / jacobian


def deposit_occupation(species_occupations, state_lines, wire_layers):
    slab_of = (jnp.arange(wire_layers, dtype=jnp.int32) // PL)[:, None, None]
    linear_offset = (slab_of * ATOMIC_STATES + state_lines).reshape(-1)
    deposited = jnp.take(species_occupations, linear_offset, axis=1)
    return deposited.reshape(2, wire_layers, state_lines.shape[1], state_lines.shape[2])


def on_device(
    green_blocks, injection, mesh_state_choice, regions, dopant_charge_field, earlier_voltage
):
    squared = (
        green_blocks[:, :, 0] * green_blocks[:, :, 0]
        + green_blocks[:, :, 1] * green_blocks[:, :, 1]
    )
    interim_amount = jnp.einsum(
        "esij,espj->spi", squared, injection, precision=lax.Precision.HIGHEST
    )
    number_of_layers = green_blocks.shape[1]
    wire_layers = number_of_layers * PL
    row_count = regions.shape[1]
    row_start = lax.axis_index("energy") * row_count
    species_occupations = jnp.transpose(interim_amount, (1, 0, 2)).reshape(
        2, number_of_layers * ATOMIC_STATES
    )
    whole_mesh = deposit_occupation(species_occupations, mesh_state_choice, wire_layers)
    owned_density = lax.psum_scatter(whole_mesh, "energy", scatter_dimension=2, tiled=True)
    electrons = owned_density[0]
    hole_density = owned_density[1]
    dielectric_mesh = permittivity(regions)
    old_rows = lax.dynamic_slice_in_dim(earlier_voltage, row_start, row_count, 1)
    electrostatic_sweep = old_rows
    for sweep_step in range(SWEEPS):
        haloed_voltage = with_halo(electrostatic_sweep, (("energy", 1), ("space", 0)), 1)
        electrostatic_sweep = smoothed_voxels(
            haloed_voltage, dielectric_mesh, dopant_charge_field, electrons, hole_density, old_rows
        )
    change = electrostatic_sweep - old_rows
    largest = lax.pmax(jnp.max(jnp.abs(change)), ("energy", "space"))
    settled = old_rows + change / (1.0 + largest)
    return lax.all_gather(settled, "energy", axis=1, tiled=True)


def solution(mesh):
    placed = (
        P("energy", "space", None, None, None),
        P("energy", "space", None, None),
        P("space", None, None),
        P("space", "energy", None),
        P("space", "energy", None),
        P("space", None, None),
    )
    return jax.shard_map(
        on_device, mesh=mesh, in_specs=placed, out_specs=P("space", None, None), check_vma=False
    )
```

profile of v0, /device:TPU:0, one launch (start us, length us, event | category | flops | bytes accessed | tf_op | source)
XLA Modules:
  0.0 1119.7 jit_solution(1621448208171723392)
XLA Ops:
  6.5 0.7 copy-done
  7.3 11.5 %fusion = f32[2,1024,2]{1,2,0:T(2,128)S(1)} fusion(f32[1,2,2,1024,1024]{4,3,2,1,0:T(8,128)} %param.6, f32[1,2,2,1024]{3,2,1,0:T(2,128)S(1)} %copy-done), kind=kOutput, calls=%fused_computation.1 | convolution fusion | flops 56623104 | bytes 16809984 | tf_op jit(solution)/shard_map/esij,espj->spi/dot_general | solution.py:59
  18.7 0.4 copy.8
  19.1 1.1 compare_and_fusion
  20.2 1.1 compare_select_fusion
  21.3 0.1 broadcast_clamp_fusion
  21.5 865.6 %gather_fusion = f32[262144,2]{1,0:T(8,128)} fusion(f32[2,2048]{0,1:T(8,128)S(1)} %copy.8, s32[262144]{0:T(1024)S(1)} %broadcast_clamp_fusion), kind=kCustom, calls=%fused_computation | custom fusion | bytes 5242880 | tf_op jit(solution)/shard_map/jit(_take)/gather | solution.py:48
  887.1 72.7 %copy.9 = f32[2,32,64,128]{3,2,1,0:T(8,128)S(1)} copy(f32[2,32,64,128]{0,3,2,1:T(8,128)} %bitcast.7) | data formatting | bytes 4194304 | tf_op jit(solution)/shard_map/jit(_take)/gather | solution.py:48
  959.7 2.6 broadcast_select_fusion
  962.3 0.0 reduce-scatter.2.cloned.1.call-update
  962.3 0.0 all-gather.2.cloned.1.call-start
  962.5 1.3 collective-permute-start.1
  963.8 3.0 collective-permute-start
  966.8 0.8 collective-permute-done
  967.6 1.3 collective-permute-start.2
  968.9 5.5 collective-permute-start.3
  974.4 0.0 collective-permute-done.2
  974.4 1.4 collective-permute-done.3
  975.8 20.9 %reduce-scatter.2.cloned.1.call-done = f32[2,32,16,128]{3,2,1,0:T(8,128)} async-done(((f32[2,32,64,128]{3,2,1,0:T(8,128)}), f32[2,32,16,128]{3,2,1,0:T(8,128)}) %reduce-scatter.2.cloned.1.call-update) | async-done | bytes 524304 | tf_op jit(solution)/shard_map/reduce_scatter | solution.py:70
  996.6 1.5 fusion.13
  998.2 1.3 collective-permute-start.5
  999.5 3.0 collective-permute-start.4
  1002.5 0.0 collective-permute-done.5
  1002.5 0.8 collective-permute-done.4
  1003.3 1.3 collective-permute-start.6
  1004.6 4.5 collective-permute-start.7
  1009.2 1.4 collective-permute-done.7
  1010.6 1.4 fusion.20
  1012.0 1.3 collective-permute-start.9
  1013.3 3.0 collective-permute-start.8
  1016.4 0.0 collective-permute-done.9
  1016.4 0.8 collective-permute-done.8
  1017.2 1.3 collective-permute-start.10
  1018.5 4.9 collective-permute-start.11
  1023.4 1.4 collective-permute-done.11
  1024.8 1.4 fusion.27
  1026.2 1.3 collective-permute-start.13
  1027.5 4.6 collective-permute-start.12
  1032.2 0.8 collective-permute-done.12
  1033.0 1.3 collective-permute-start.14
  1034.3 5.7 collective-permute-start.15
  1040.0 1.4 collective-permute-done.15
  1041.4 2.0 abs_reduce_fusion
  1043.4 47.4 %pmax.7 = f32[]{:T(128)} all-reduce(f32[]{:T(128)} %get-tuple-element.5), channel_id=1, replica_groups=mesh['energy'=4,'space'=8] {'energy','space'}, use_global_device_ids=true, to_apply=%region_2.3 | all-reduce | flops 1 | bytes 8 | tf_op jit(solution)/shard_map/pmax | solution.py:82
  1091.5 0.7 divide_add_fusion
  1092.3 0.0 all-gather.2.cloned.1.call-update
  1092.3 18.2 %all-gather.2.cloned.1.call-done = f32[32,64,128]{2,1,0:T(8,128)} async-done(((f32[32,16,128]{2,1,0:T(8,128)}), f32[32,64,128]{2,1,0:T(8,128)}) %all-gather.2.cloned.1.call-update) | async-done | bytes 1048592 | tf_op jit(solution)/shard_map/all_gather | solution.py:84
  1110.5 2.3 copy.11
  (23 shorter events, 0.2 us)
Async XLA Ops:
  6.5 0.7 copy-start
  6.5 12.6 %copy-start.3 = (s32[32,64,128]{2,1,0:T(8,128)S(1)}, s32[32,64,128]{2,1,0:T(8,128)}, u32[]{:S(2)}) copy-start(s32[32,64,128]{2,1,0:T(8,128)} %param.8) | copy-start | bytes 3145732
  6.5 990.1 %reduce-scatter.2.cloned.1.call-start = ((), (), s32[]{:S(2)}) async-start(), calls=%async_computation.1 | async-start | bytes 2621440 | tf_op jit(solution)/shard_map/reduce_scatter | solution.py:70
  887.1 75.3 %copy-start.2 = (f32[32,64,128]{2,1,0:T(8,128)S(1)}, f32[32,64,128]{2,1,0:T(8,128)}, u32[]{:S(2)}) copy-start(f32[32,64,128]{2,1,0:T(8,128)} %param.11) | copy-start | bytes 3145732
  887.1 109.6 %copy-start.1 = (f32[32,16,128]{2,1,0:T(8,128)S(1)}, f32[32,16,128]{2,1,0:T(8,128)}, u32[]{:S(2)}) copy-start(f32[32,16,128]{2,1,0:T(8,128)} %param.10) | copy-start | bytes 786436
  962.3 148.2 %all-gather.2.cloned.1.call-start = ((), (), s32[]{:S(2)}) async-start(), calls=%async_computation.2 | async-start | bytes 1310720 | tf_op jit(solution)/shard_map/all_gather | solution.py:84
  962.5 4.4 collective-permute-start.1
  963.8 3.9 collective-permute-start
  967.6 6.8 collective-permute-start.2
  968.9 6.9 collective-permute-start.3
  998.2 4.3 collective-permute-start.5
  999.5 3.9 collective-permute-start.4
  1003.3 5.8 collective-permute-start.6
  1004.6 5.9 collective-permute-start.7
  1012.0 4.3 collective-permute-start.9
  1013.3 3.9 collective-permute-start.8
  1017.2 6.2 collective-permute-start.10
  1018.5 6.3 collective-permute-start.11
  1026.2 5.9 collective-permute-start.13
  1027.5 5.5 collective-permute-start.12
  1033.0 7.0 collective-permute-start.14
  1034.3 7.1 collective-permute-start.15
Sparse Core Ops, SparseCore 0:
  962.5 34.1 reduce-scatter.1
  1092.4 18.0 all-gather.1
where the time goes:
time: 1120 us
  local copies, waits for them, and re-layouts  942 us (84%)
  waiting for transfers between devices  47.9 us (4%)
  blocking collectives  47.4 us (4%)
  starting transfers between devices  44.7 us (4%)
  between operations  14.4 us (1%)
  other arithmetic  12.1 us (1%)
  matrix products  11.5 us (1%)
    gather x2, local copies, waits for them, and re-layouts, deposit_occupation(): deposited = jnp.take(species_occupations, linear_offset, axis=1)  938 us
    pmax x1, blocking collectives, on_device(): largest = lax.pmax(jnp.max(jnp.abs(change)), ('energy', 'space'))  47.4 us
    ppermute x8, starting transfers between devices, with_halo(): lax.ppermute(lax.slice_in_dim(block, block.shape[dim] - width, None, axis...  34.4 us
  transfers between devices with their start and end apart: 18, of which 10 were waited for; matrix products, arithmetic and copies ran while one was open for 0% of the time, Pallas kernels for 0%

commit v1 on v0

v1 whole, which is shorter than its diff:
```python
import functools

import jax
import jax.numpy as jnp
from jax import lax
from jax.experimental import pallas as pl
from jax.experimental.pallas import tpu as pltpu
from jax.sharding import PartitionSpec as P

PL = 16
SWEEPS = 4
HALO = 4
PAD = 8
LANES = 128
SUB = 8
MIB = 1 << 20


def merge(parts, width):
    lane = lax.broadcasted_iota(jnp.int32, (SUB, LANES), 1)
    while len(parts) > 1:
        low = (lane & width) == 0
        merged = []
        for a, b in zip(parts[::2], parts[1::2]):
            merged.append(jnp.where(low, a, b) + pltpu.roll(jnp.where(low, b, a), width, 1))
        parts = merged
        width *= 2
    return parts[0]


def table_kernel(green_ref, inject_ref, out_ref, part_ref):
    rows = green_ref.shape[1]
    columns = green_ref.shape[2]
    groups = rows // SUB
    block = pl.program_id(1)
    chunks = columns // LANES
    weights = [
        [
            jnp.broadcast_to(inject_ref[c : c + 1, k * LANES : (k + 1) * LANES], (SUB, LANES))
            for k in range(chunks)
        ]
        for c in range(2)
    ]
    sums = [[], []]
    for g in range(groups):
        total = [None, None]
        for k in range(chunks):
            cols = slice(k * LANES, (k + 1) * LANES)
            re = green_ref[0, g * SUB : (g + 1) * SUB, cols]
            im = green_ref[1, g * SUB : (g + 1) * SUB, cols]
            squared = re * re + im * im
            for c in range(2):
                term = squared * weights[c][k]
                total[c] = term if total[c] is None else total[c] + term
        for c in range(2):
            sums[c].append(total[c])
    for c in range(2):
        part_ref[c, block] = merge(sums[c], 1)

    @pl.when(block == pl.num_programs(1) - 1)
    def _():
        count = part_ref.shape[1]
        for c in range(2):
            out_ref[c] = merge([part_ref[c, b] for b in range(count)], groups)


def orbital_table(green, inject):
    slabs, _, states, _ = green.shape
    rows = 128
    return pl.pallas_call(
        table_kernel,
        grid=(slabs, states // rows),
        in_specs=[
            pl.BlockSpec((None, 2, rows, states), lambda s, b: (s, 0, b, 0)),
            pl.BlockSpec((None, 2, states), lambda s, b: (s, 0, 0)),
        ],
        out_specs=pl.BlockSpec((None, 2, SUB, LANES), lambda s, b: (s, 0, 0, 0)),
        out_shape=jax.ShapeDtypeStruct((slabs, 2, SUB, LANES), jnp.float32),
        scratch_shapes=[pltpu.VMEM((2, states // rows, SUB, LANES), jnp.float32)],
        compiler_params=pltpu.CompilerParams(vmem_limit_bytes=32 * MIB),
        name="table",
    )(green, inject)


def lookup(tables, choice):
    lane = choice >> 3
    group = choice & (SUB - 1)
    bits = [(group & (1 << b)) != 0 for b in range(3)]
    out = []
    for table in tables:
        found = [jnp.take_along_axis(t, lane, axis=1, mode="promise_in_bounds") for t in table]
        for bit in bits:
            found = [jnp.where(bit, found[2 * k + 1], found[2 * k]) for k in range(len(found) // 2)]
        out.append(found[0])
    return out


def permittivity(regions):
    return jnp.where(regions == 0, 1.0, jnp.where(regions == 1, 0.33, 1.7)).astype(jnp.float32)


def sweep_kernel(
    place_ref, tables_ref, beside1_ref, beside2_ref,
    mesh_ref, old_ref, regions_ref, dopant_ref,
    rows1_ref, rows2_ref, planes1_ref, planes2_ref,
    change_ref, most_ref,
    mesh_s, before_s, permit_s, dopant_s, electron_s, hole_s, now_s, next_s,
):
    e, s, ne, ns = (place_ref[k] for k in range(4))
    odd_e, odd_s = (e & 1) == 1, (s & 1) == 1
    planes, own, _ = regions_ref.shape
    slabs = tables_ref.shape[0]
    span = own + 2 * HALO
    row0 = e * own
    first, last = PAD, PAD + span
    full_rows = mesh_ref.shape[1]

    up_in, down_in = e > 0, e < ne - 1
    mid = slice(PAD + HALO, PAD + HALO + own)
    up = slice(PAD, PAD + HALO)
    down = slice(PAD + HALO + own, PAD + span)
    body = slice(HALO, HALO + planes)
    up_from = pl.multiple_of(jnp.maximum(row0 - SUB, 0), SUB)
    down_from = pl.multiple_of(jnp.minimum(row0 + own, full_rows - SUB), SUB)

    def lay(p, _):
        q = p + HALO
        mesh_s[q, mid] = mesh_ref[p, pl.ds(row0, own)]
        mesh_s[q, up] = mesh_ref[p, pl.ds(up_from, SUB)][SUB - HALO :]
        mesh_s[q, down] = mesh_ref[p, pl.ds(down_from, SUB)][:HALO]
        before_s[q, mid] = old_ref[p, pl.ds(row0, own)]
        before_s[q, up] = jnp.where(up_in, old_ref[p, pl.ds(up_from, SUB)][SUB - HALO :], 0.0)
        before_s[q, down] = jnp.where(down_in, old_ref[p, pl.ds(down_from, SUB)][:HALO], 0.0)
        permit_s[q, mid] = permittivity(regions_ref[p])
        dopant_s[q, mid] = dopant_ref[p]
        permit_s[q, up] = jnp.where(odd_e, rows1_ref[0, p], rows2_ref[0, p])
        permit_s[q, down] = jnp.where(odd_e, rows2_ref[0, p], rows1_ref[0, p])
        dopant_s[q, up] = jnp.where(odd_e, rows1_ref[1, p], rows2_ref[1, p])
        dopant_s[q, down] = jnp.where(odd_e, rows2_ref[1, p], rows1_ref[1, p])
        return _

    lax.fori_loop(0, planes, lay, None)
    whole = slice(PAD, PAD + span)
    for k in range(HALO):
        for q, a, b in ((k, planes1_ref, planes2_ref), (HALO + planes + k, planes2_ref, planes1_ref)):
            mesh_s[q, whole] = jnp.where(odd_s, a[0, k], b[0, k]).astype(jnp.int32)
            before_s[q, whole] = jnp.where(odd_s, a[1, k], b[1, k])
            permit_s[q, whole] = jnp.where(odd_s, a[2, k], b[2, k])
            dopant_s[q, whole] = jnp.where(odd_s, a[3, k], b[3, k])

    def table_of(slab_value):
        return [
            [jnp.broadcast_to(slab_value[c, g : g + 1], (SUB, LANES)) for g in range(SUB)]
            for c in range(2)
        ]

    def densities(q, tables):
        for r in range(PAD, PAD + span, SUB):
            found = lookup(tables, mesh_s[q, r : r + SUB])
            electron_s[q, r : r + SUB] = found[0]
            hole_s[q, r : r + SUB] = found[1]

    low_table = table_of(jnp.where(odd_s, beside1_ref[...], beside2_ref[...]))
    for q in range(1, HALO):
        densities(q, low_table)
    for slab in range(slabs):
        table = table_of(tables_ref[slab])

        def one(p, _, table=table):
            densities(p, table)
            return _

        lax.fori_loop(HALO + slab * PL, HALO + (slab + 1) * PL, one, None)
    high_table = table_of(jnp.where(odd_s, beside2_ref[...], beside1_ref[...]))
    for q in range(HALO + planes, HALO + planes + HALO - 1):
        densities(q, high_table)

    lane = lax.broadcasted_iota(jnp.int32, (SUB, LANES), 1)
    not_first, not_last = lane > 0, lane < LANES - 1
    row = lax.broadcasted_iota(jnp.int32, (SUB, LANES), 0)
    for buffer in (now_s, next_s):
        for q in (0, 1, 2, 3, planes + 4, planes + 5, planes + 6, planes + 7):
            buffer[q] = jnp.zeros(buffer.shape[1:], jnp.float32)
    low_plane = jnp.where(s > 0, 0, HALO)
    high_plane = jnp.where(s < ns - 1, planes + 2 * HALO, planes + HALO)
    most_ref[...] = jnp.zeros(most_ref.shape, jnp.float32)
    source = before_s
    for sweep in range(SWEEPS):
        final = sweep == SWEEPS - 1
        target = next_s if source is now_s else now_s
        starts = range(PAD + HALO, PAD + HALO + own, SUB) if final else range(PAD, PAD + span, SUB)

        def step(q, most, sweep=sweep, source=source, target=target, starts=starts, final=final):
            for r in starts:
                rows = slice(r, r + SUB)
                center = source[q, rows]
                neighbours = source[q + 1, rows] + source[q - 1, rows]
                neighbours = neighbours + source[q, r + 1 : r + 1 + SUB] + source[q, r - 1 : r - 1 + SUB]
                after = jnp.where(not_last, pltpu.roll(center, LANES - 1, 1), 0.0)
                ahead = jnp.where(not_first, pltpu.roll(center, 1, 1), 0.0)
                neighbours = neighbours + after + ahead
                permit = permit_s[q, rows]
                electrons = electron_s[q, rows]
                holes = hole_s[q, rows]
                if sweep:
                    moved = center - before_s[q, rows]
                    electrons = electrons * jnp.exp(moved)
                    holes = holes * jnp.exp(-moved)
                mismatch = permit * (6.0 * center - neighbours) - (dopant_s[q, rows] + holes - electrons)
                jacobian = 6.0 * permit + electrons + holes
                fresh = center - mismatch / jacobian
                if final:
                    change = fresh - before_s[q, rows]
                    change_ref[q - HALO, r - PAD - HALO : r - PAD - HALO + SUB] = change
                    most = jnp.maximum(most, jnp.abs(change))
                else:
                    if r == PAD:
                        fresh = jnp.where((row >= HALO) | up_in, fresh, 0.0)
                    elif r == PAD + span - SUB:
                        fresh = jnp.where((row < HALO) | down_in, fresh, 0.0)
                    target[q, rows] = fresh
            return most

        begin = jnp.maximum(low_plane, 1 + sweep)
        end = jnp.minimum(high_plane, planes + 2 * HALO - 1 - sweep)
        most = lax.fori_loop(begin, end, step, jnp.zeros((SUB, LANES), jnp.float32))
        if final:
            most_ref[...] = jnp.max(most, axis=0, keepdims=True)
        source = target


def swept(place, tables, beside, mesh, old, regions, dopant, rows, edge_planes):
    planes, own, lanes = regions.shape
    deep = (planes + 2 * HALO, own + 2 * HALO + 2 * PAD, lanes)
    vmem = pl.BlockSpec(memory_space=pltpu.VMEM)
    return pl.pallas_call(
        sweep_kernel,
        in_specs=[pl.BlockSpec(memory_space=pltpu.SMEM)] + [vmem] * 11,
        out_specs=[vmem, vmem],
        out_shape=[
            jax.ShapeDtypeStruct(regions.shape, jnp.float32),
            jax.ShapeDtypeStruct((1, lanes), jnp.float32),
        ],
        scratch_shapes=[pltpu.VMEM(deep, jnp.int32)] + [pltpu.VMEM(deep, jnp.float32)] * 7,
        compiler_params=pltpu.CompilerParams(vmem_limit_bytes=40 * MIB),
        name="sweeps",
    )(place, tables, *beside, mesh, old, regions, dopant, *rows, *edge_planes)


def settle_kernel(place_ref, most_ref, old_ref, *rest):
    parts, out_ref = rest[:-1], rest[-1]
    e = place_ref[0]
    own = parts[0].shape[1]
    largest = jnp.max(most_ref[...])
    for k, part in enumerate(parts):
        rows = pl.ds(pl.multiple_of((e ^ k) * own, SUB), own)
        out_ref[:, rows] = old_ref[:, rows] + part[...] / (1.0 + largest)


def settled(place, most, old, parts):
    vmem = pl.BlockSpec(memory_space=pltpu.VMEM)
    return pl.pallas_call(
        settle_kernel,
        in_specs=[pl.BlockSpec(memory_space=pltpu.SMEM)] + [vmem] * (2 + len(parts)),
        out_specs=vmem,
        out_shape=jax.ShapeDtypeStruct(old.shape, jnp.float32),
        compiler_params=pltpu.CompilerParams(vmem_limit_bytes=32 * MIB),
        name="settle",
    )(place, most, old, *parts)


def pairs(axis, odd_first):
    count = lax.axis_size(axis)
    out = []
    for low in range(1 if odd_first else 0, count - 1, 2):
        out += [(low, low + 1), (low + 1, low)]
    return out


def toggled(x, axis, mask):
    return lax.ppermute(x, axis, [(i, i ^ mask) for i in range(lax.axis_size(axis))])


def on_device(green_blocks, injection, mesh_state_choice, regions, dopant_charge_field, earlier_voltage):
    ne, ns = lax.axis_size("energy"), lax.axis_size("space")
    e, s = lax.axis_index("energy"), lax.axis_index("space")
    planes, own, lanes = regions.shape
    odd_e, odd_s = e & 1, s & 1
    place = jnp.stack([e, s, jnp.int32(ne), jnp.int32(ns)]).astype(jnp.int32)

    permit = permittivity(regions)
    fields = jnp.stack([permit, dopant_charge_field])
    rows = []
    for odd_first in (False, True):
        at_top = odd_e if not odd_first else 1 - odd_e
        edge = lax.dynamic_slice_in_dim(fields, (1 - at_top) * (own - HALO), HALO, 2)
        rows.append(lax.ppermute(edge, "energy", pairs("energy", odd_first)))
    above = jnp.where(odd_e == 1, rows[0], rows[1])
    below = jnp.where(odd_e == 1, rows[1], rows[0])
    edge_planes = []
    for odd_first in (False, True):
        at_low = odd_s if not odd_first else 1 - odd_s
        start = (1 - at_low) * (planes - HALO)
        cut = functools.partial(lax.dynamic_slice_in_dim, start_index=start, slice_size=HALO)
        taken = []
        for field in (mesh_state_choice, earlier_voltage):
            tall = jnp.pad(cut(field, axis=0), ((0, 0), (HALO, HALO), (0, 0)))
            taken.append(lax.dynamic_slice_in_dim(tall, e * own, own + 2 * HALO, 1).astype(jnp.float32))
        stacked = jnp.stack(taken)
        both = jnp.concatenate([cut(above, axis=1), cut(fields, axis=1), cut(below, axis=1)], axis=2)
        edge_planes.append(
            lax.ppermute(jnp.concatenate([stacked, both]), "space", pairs("space", odd_first))
        )

    tables = orbital_table(green_blocks[0], injection[0])
    terms = [tables] + [toggled(tables, "energy", k) for k in range(1, ne)]
    while len(terms) > 1:
        terms = [terms[2 * k] + terms[2 * k + 1] for k in range(len(terms) // 2)]
    tables = terms[0]
    beside = []
    for odd_first in (False, True):
        at_low = odd_s if not odd_first else 1 - odd_s
        edge = jnp.where(at_low == 1, tables[0], tables[-1])
        beside.append(lax.ppermute(edge, "space", pairs("space", odd_first)))

    change, most = swept(
        place, tables, beside, mesh_state_choice, earlier_voltage, regions, dopant_charge_field,
        rows, edge_planes,
    )
    parts = [change] + [toggled(change, "energy", k) for k in range(1, ne)]
    spread = jnp.broadcast_to(most[None], (ne * ns, 1, lanes))
    most = lax.all_to_all(spread, ("energy", "space"), 0, 0)
    return settled(place, most.reshape(ne * ns, lanes), earlier_voltage, parts)


def solution(mesh):
    placed = (
        P("energy", "space", None, None, None),
        P("energy", "space", None, None),
        P("space", None, None),
        P("space", "energy", None),
        P("space", "energy", None),
        P("space", None, None),
    )
    return jax.shard_map(
        on_device, mesh=mesh, in_specs=placed, out_specs=P("space", None, None), check_vma=False
    )
```

time: 1120 us -> 71.1 us (0.06)
  local copies, waits for them, and re-layouts: 942 us -> 6.62 us
  waiting for transfers between devices: 47.9 us -> 4.87 us
  blocking collectives: 47.4 us -> 12.6 us
  Pallas kernels: 0 us -> 26.5 us
  starting transfers between devices: 44.7 us -> 18.9 us
  between operations: 14.4 us -> 0.21 us
  matrix products: 11.5 us -> 0 us
    gather x2 -> x0, local copies, waits for them, and re-layouts: 938 us -> none  [deposit_occupation(): deposited = jnp.take(species_occupations, linear_offset, axis=1)]
    pmax x1 -> x0, blocking collectives: 47.4 us -> none  [on_device(): largest = lax.pmax(jnp.max(jnp.abs(change)), ('energy', 'space'))]
    pallas_call x0 -> x3, Pallas kernels: none -> 26.5 us  [the longest x1 16.7 us: swept(): pl.pallas_call(sweep_kernel, in_specs=[pl.BlockSpec(memory_space=pltpu.SM...]
    ppermute x16 -> x12, starting transfers between devices: 44.7 us -> 18.9 us  [the longest x6 5.03 us: toggled(): lax.ppermute(x, axis, [(i, i ^ mask) for i in range(lax.axis_size(axis))])]
    reduce_scatter x1 -> x0, waiting for transfers between devices: 20.9 us -> none  [on_device(): lax.psum_scatter(whole_mesh, 'energy', scatter_dimension=2, tiled=True)]
    all_gather x1 -> x0, waiting for transfers between devices: 18.2 us -> none  [on_device(): return lax.all_gather(settled, 'energy', axis=1, tiled=True)]
    all_to_all x0 -> x1, blocking collectives: none -> 12.6 us  [on_device(): most = lax.all_to_all(spread, ('energy', 'space'), 0, 0)]
    dot_general x1 -> x0, matrix products: 11.5 us -> none  [on_device(): jnp.einsum('esij,espj->spi', squared, injection, precision=lax.Precision....]
  transfers between devices with their start and end apart: 18 -> 12, of which waited for: 10 -> 2; matrix products, arithmetic and copies ran while one was open for 0% -> 1% of each run, Pallas kernels for 0% -> 0%
where the time goes in v1:
time: 71.1 us; the launch traced here: 70.6 us
  Pallas kernels  26.5 us (37%)
  starting transfers between devices  18.9 us (27%)
  blocking collectives  12.6 us (18%)
  local copies, waits for them, and re-layouts  6.62 us (9%)
  waiting for transfers between devices  4.87 us (7%)
  other arithmetic  1 us (1%)
    pallas_call x1, Pallas kernels, swept(): pl.pallas_call(sweep_kernel, in_specs=[pl.BlockSpec(memory_space=pltpu.SM...  16.7 us
    all_to_all x1, blocking collectives, on_device(): most = lax.all_to_all(spread, ('energy', 'space'), 0, 0)  12.6 us
    pallas_call x1, Pallas kernels, orbital_table(): pl.pallas_call(table_kernel, grid=(slabs, states // rows), in_specs=[pl.B...  7.98 us
    unnamed x12, local copies, waits for them, and re-layouts  6.5 us
    ppermute x6, starting transfers between devices, toggled(): lax.ppermute(x, axis, [(i, i ^ mask) for i in range(lax.axis_size(axis))])  5.03 us
    ppermute x2, starting transfers between devices, on_device(): lax.ppermute(jnp.concatenate([stacked, both]), 'space', pairs('space', od...  5.01 us
    ppermute x2, starting transfers between devices, on_device(): beside.append(lax.ppermute(edge, 'space', pairs('space', odd_first)))  5 us
    ppermute x2, waiting for transfers between devices, on_device(): beside.append(lax.ppermute(edge, 'space', pairs('space', odd_first)))  3.93 us
  transfers between devices with their start and end apart: 12, of which 2 were waited for; matrix products, arithmetic and copies ran while one was open for 1% of the time, Pallas kernels for 0%

profile of v1, /device:TPU:0, one launch (start us, length us, event | category | flops | bytes accessed | tf_op | source)
XLA Modules:
  0.0 70.6 jit_solution(566703995160763443)
XLA Ops:
  0.0 0.0 copy-start
  0.0 5.8 %copy-done = f32[1,2,2,1024,1024]{4,3,2,1,0:T(8,128)S(1)} copy-done((f32[1,2,2,1024,1024]{4,3,2,1,0:T(8,128)S(1)}, f32[1,2,2,1024,1024]{4,3,2,1,0:T(8,128)}, u32[]{:S(2)}) %copy-start) | copy-done | bytes 16777240
  5.8 0.0 copy-start.5
  5.8 0.7 %copy-done.5 = f32[1,2,2,1024]{3,2,1,0:T(2,128)S(1)} copy-done((f32[1,2,2,1024]{3,2,1,0:T(2,128)S(1)}, f32[1,2,2,1024]{3,2,1,0:T(2,128)}, u32[]{:S(2)}) %copy-start.5) | copy-done | bytes 16408
  6.5 0.0 copy-start.4
  6.5 0.0 copy-start.2
  6.5 0.0 copy-start.3
  6.5 0.0 copy-start.1
  6.5 8.0 %table.1 = f32[2,2,8,128]{3,2,1,0:T(8,128)S(1)} custom-call(f32[2,2,1024,1024]{3,2,1,0:T(8,128)S(1)} %bitcast.25, f32[2,2,1024]{2,1,0:T(2,128)S(1)} %bitcast.31), custom_call_target="tpu_custom_call" | custom-call | tf_op jit(solution)/shard_map/table/pallas_call | solution.py:70
  14.5 2.4 %collective-permute-start.2 = (f32[2,2,8,128]{3,2,1,0:T(8,128)S(1)}, f32[2,2,8,128]{3,2,1,0:T(8,128)S(1)}, u32[]{:S(2)}, u32[]{:S(2)}) collective-permute-start(f32[2,2,8,128]{3,2,1,0:T(8,128)S(1)} %table.1), channel_id=1, source_target_pairs={{0,24},{8,16},{16,8},{24,0},{1,25},{9,17},{17,9},{25,1},{2,26},{10... | collective-permute-start | bytes 49160 | tf_op jit(solution)/shard_map/ppermute | solution.py:281
  16.9 0.6 collective-permute-start.1
  17.5 0.1 collective-permute-start
  17.6 0.0 copy-done.4
  17.6 0.0 copy-done.2
  17.6 0.7 %fusion.1 = (f32[2,32,4,128]{3,2,1,0:T(4,128)}, f32[2,32,4,128]{3,2,1,0:T(4,128)}) fusion(s32[]{:T(128)S(6)} %select_n.75, f32[1,32,16,128]{3,2,1,0:T(8,128)S(1)} %select_bitcast_fusion, f32[1,32,16,128]{3,2,1,0:T(8,128)S(1)} %bitcast.26, s32[]{:T(128)S(6)} %select_n.74), kind=kLoop, calls=%fused_computation.16 | loop fusion | flops 65536 | bytes 786440 | tf_op jit(solution)/shard_map/stack | solution.py:292
  18.4 0.7 collective-permute-start.6
  19.0 3.2 %collective-permute-start.5 = (f32[2,32,4,128]{3,2,1,0:T(4,128)}, f32[2,32,4,128]{3,2,1,0:T(4,128)S(1)}, u32[]{:S(2)}, u32[]{:S(2)}) collective-permute-start(f32[2,32,4,128]{3,2,1,0:T(4,128)} %get-tuple-element.16), channel_id=1, source_target_pairs={{0,8},{8,0},{16,24},{24,16},{1,9},{9,1},{17,25},{25,17},{2,10},{10... | collective-permute-start | bytes 393224 | tf_op jit(solution)/shard_map/ppermute | solution.py:297
  22.2 0.0 copy-done.3
  22.3 0.0 copy-done.1
  22.4 0.0 collective-permute-done.2
  22.4 0.0 collective-permute-done.1
  22.4 0.0 collective-permute-done
  22.5 0.0 collective-permute-done.6.rows2_ref
  22.5 0.9 %collective-permute-done.5.rows1_ref = f32[2,32,4,128]{3,2,1,0:T(4,128)S(1)} collective-permute-done((f32[2,32,4,128]{3,2,1,0:T(4,128)}, f32[2,32,4,128]{3,2,1,0:T(4,128)S(1)}, u32[]{:S(2)}, u32[]{:S(2)}) %collective-permute-start.5) | collective-permute-done | bytes 131104 | tf_op jit(solution)/shard_map/ppermute | solution.py:297
  23.5 0.7 collective-permute-start.8
  24.2 4.3 %collective-permute-start.7 = (f32[4,4,24,128]{3,2,1,0:T(8,128)S(1)}, f32[4,4,24,128]{3,2,1,0:T(8,128)S(1)}, u32[]{:S(2)}, u32[]{:S(2)}) collective-permute-start(f32[4,4,24,128]{3,2,1,0:T(8,128)S(1)} %maximum_maximum_fusion), channel_id=1, source_target_pairs={{0,1},{1,0},{2,3},{3,2},{4,5},{5,4},{6,7},{7,6},{8,9},{9,8},{10,11... | collective-permute-start | bytes 589832 | tf_op jit(solution)/shard_map/ppermute | solution.py:312
  28.5 0.6 collective-permute-start.4
  29.2 4.4 %collective-permute-start.3 = (f32[2,8,128]{2,1,0:T(8,128)S(1)}, f32[2,8,128]{2,1,0:T(8,128)S(1)}, u32[]{:S(2)}, u32[]{:S(2)}) collective-permute-start(f32[2,8,128]{2,1,0:T(8,128)S(1)} %get-tuple-element.24), channel_id=1, source_target_pairs={{0,1},{1,0},{2,3},{3,2},{4,5},{5,4},{6,7},{7,6},{8,9},{9,8},{10,11... | collective-permute-start | bytes 24584 | tf_op jit(solution)/shard_map/ppermute | solution.py:324
  33.5 0.1 pad_add_fusion.place_ref
  33.6 0.0 collective-permute-done.4.beside2_ref
  33.6 3.9 %collective-permute-done.3.beside1_ref = f32[2,8,128]{2,1,0:T(8,128)S(1)} collective-permute-done((f32[2,8,128]{2,1,0:T(8,128)S(1)}, f32[2,8,128]{2,1,0:T(8,128)S(1)}, u32[]{:S(2)}, u32[]{:S(2)}) %collective-permute-start.3) | collective-permute-done | bytes 8224 | tf_op jit(solution)/shard_map/ppermute | solution.py:324
  37.6 0.0 collective-permute-done.8.planes2_ref
  37.6 0.0 collective-permute-done.7.planes1_ref
  37.6 16.7 %sweeps.1 = (f32[32,16,128]{2,1,0:T(8,128)S(1)}, f32[1,128]{1,0:T(1,128)S(1)}) custom-call(s32[4]{0:T(128)S(1)} %pad_add_fusion.place_ref, f32[2,2,8,128]{3,2,1,0:T(8,128)S(1)} %add_add_fusion.tables_ref, f32[2,8,128]{2,1,0:T(8,128)S(1)} %collective-permute-done.3.beside1_ref, f32[2,8,128]{2,1,0:T(8,128)S(1)} %collective-permute-done.4.beside2_ref, ...), custom_call_target="tpu_custom_call" | custom-call | tf_op jit(solution)/shard_map/sweeps/pallas_call | solution.py:236
  54.2 0.1 collective-permute-start.11
  54.3 1.9 %collective-permute-start.10 = (f32[32,16,128]{2,1,0:T(8,128)S(1)}, f32[32,16,128]{2,1,0:T(8,128)S(1)}, u32[]{:S(2)}, u32[]{:S(2)}) collective-permute-start(f32[32,16,128]{2,1,0:T(8,128)S(1)} %get-tuple-element.8.rest_0_), channel_id=1, source_target_pairs={{0,16},{8,24},{16,0},{24,8},{1,17},{9,25},{17,1},{25,9},{2,18},{10... | collective-permute-start | bytes 786440 | tf_op jit(solution)/shard_map/ppermute | solution.py:281
  56.2 0.0 collective-permute-start.9
  56.2 12.6 %all_to_all.5 = f32[32,1,128]{2,1,0:T(1,128)S(1)} all-to-all(f32[32,1,128]{2,1,0:T(1,128)S(1)} %broadcast_in_dim.24), channel_id=1, replica_groups=mesh['energy'=4,'space'=8] {'energy','space'}, dimensions={0} | all-to-all | bytes 32768 | tf_op jit(solution)/shard_map/all_to_all | solution.py:332
  68.8 0.0 collective-permute-done.11.rest_3_
  68.8 0.0 collective-permute-done.10.rest_2_
  68.8 0.0 collective-permute-done.9.rest_1_
  68.8 1.8 %settle.1 = f32[32,64,128]{2,1,0:T(8,128)} custom-call(s32[4]{0:T(128)S(1)} %pad_add_fusion.place_ref, f32[32,128]{1,0:T(8,128)S(1)} %bitcast.30, f32[32,64,128]{2,1,0:T(8,128)S(1)} %copy-done.1, f32[32,16,128]{2,1,0:T(8,128)S(1)} %get-tuple-element.8.rest_0_, f32[32,16,128]{2,1,0:T(8,128)S(1)} %collective-permute-done.9.rest_1_, ...), custom_call_target="tpu_custom_call" | custom-call | tf_op jit(solution)/shard_map/settle/pallas_call | solution.py:262
  (15 shorter events, 0.3 us)
Async XLA Ops:
  0.0 5.8 %copy-start = (f32[1,2,2,1024,1024]{4,3,2,1,0:T(8,128)S(1)}, f32[1,2,2,1024,1024]{4,3,2,1,0:T(8,128)}, u32[]{:S(2)}) copy-start(f32[1,2,2,1024,1024]{4,3,2,1,0:T(8,128)} %param.6) | copy-start | bytes 50331652
  5.8 0.7 %copy-start.5 = (f32[1,2,2,1024]{3,2,1,0:T(2,128)S(1)}, f32[1,2,2,1024]{3,2,1,0:T(2,128)}, u32[]{:S(2)}) copy-start(f32[1,2,2,1024]{3,2,1,0:T(2,128)} %param.7) | copy-start | bytes 49156
  6.5 11.1 %copy-start.4 = (s32[32,16,128]{2,1,0:T(8,128)S(1)}, s32[32,16,128]{2,1,0:T(8,128)}, u32[]{:S(2)}) copy-start(s32[32,16,128]{2,1,0:T(8,128)} %regions_ref.1) | copy-start | bytes 786436
  6.5 11.1 %copy-start.2 = (f32[32,16,128]{2,1,0:T(8,128)S(1)}, f32[32,16,128]{2,1,0:T(8,128)}, u32[]{:S(2)}) copy-start(f32[32,16,128]{2,1,0:T(8,128)} %dopant_ref.1) | copy-start | bytes 786436
  6.5 15.7 %copy-start.3 = (s32[32,64,128]{2,1,0:T(8,128)S(1)}, s32[32,64,128]{2,1,0:T(8,128)}, u32[]{:S(2)}) copy-start(s32[32,64,128]{2,1,0:T(8,128)} %mesh_ref.1) | copy-start | bytes 3145732
  6.5 15.8 %copy-start.1 = (f32[32,64,128]{2,1,0:T(8,128)S(1)}, f32[32,64,128]{2,1,0:T(8,128)}, u32[]{:S(2)}) copy-start(f32[32,64,128]{2,1,0:T(8,128)} %old_ref.3) | copy-start | bytes 3145732
  14.5 7.9 %collective-permute-start.2 = (f32[2,2,8,128]{3,2,1,0:T(8,128)S(1)}, f32[2,2,8,128]{3,2,1,0:T(8,128)S(1)}, u32[]{:S(2)}, u32[]{:S(2)}) collective-permute-start(f32[2,2,8,128]{3,2,1,0:T(8,128)S(1)} %table.1), channel_id=1, source_target_pairs={{0,24},{8,16},{16,8},{24,0},{1,25},{9,17},{17,9},{25,1},{2,26},{10... | collective-permute-start | bytes 49160 | tf_op jit(solution)/shard_map/ppermute | solution.py:281
  16.9 5.5 %collective-permute-start.1 = (f32[2,2,8,128]{3,2,1,0:T(8,128)S(1)}, f32[2,2,8,128]{3,2,1,0:T(8,128)S(1)}, u32[]{:S(2)}, u32[]{:S(2)}) collective-permute-start(f32[2,2,8,128]{3,2,1,0:T(8,128)S(1)} %table.1), channel_id=1, source_target_pairs={{0,16},{8,24},{16,0},{24,8},{1,17},{9,25},{17,1},{25,9},{2,18},{10... | collective-permute-start | bytes 49160 | tf_op jit(solution)/shard_map/ppermute | solution.py:281
  17.5 4.9 %collective-permute-start = (f32[2,2,8,128]{3,2,1,0:T(8,128)S(1)}, f32[2,2,8,128]{3,2,1,0:T(8,128)S(1)}, u32[]{:S(2)}, u32[]{:S(2)}) collective-permute-start(f32[2,2,8,128]{3,2,1,0:T(8,128)S(1)} %table.1), channel_id=1, source_target_pairs={{0,8},{8,0},{16,24},{24,16},{1,9},{9,1},{17,25},{25,17},{2,10},{10... | collective-permute-start | bytes 49160 | tf_op jit(solution)/shard_map/ppermute | solution.py:281
  18.4 4.1 %collective-permute-start.6 = (f32[2,32,4,128]{3,2,1,0:T(4,128)}, f32[2,32,4,128]{3,2,1,0:T(4,128)S(1)}, u32[]{:S(2)}, u32[]{:S(2)}) collective-permute-start(f32[2,32,4,128]{3,2,1,0:T(4,128)} %get-tuple-element.15), channel_id=1, source_target_pairs={{8,16},{16,8},{9,17},{17,9},{10,18},{18,10},{11,19},{19,11},{12,20... | collective-permute-start | bytes 393224 | tf_op jit(solution)/shard_map/ppermute | solution.py:297
  19.0 4.4 %collective-permute-start.5 = (f32[2,32,4,128]{3,2,1,0:T(4,128)}, f32[2,32,4,128]{3,2,1,0:T(4,128)S(1)}, u32[]{:S(2)}, u32[]{:S(2)}) collective-permute-start(f32[2,32,4,128]{3,2,1,0:T(4,128)} %get-tuple-element.16), channel_id=1, source_target_pairs={{0,8},{8,0},{16,24},{24,16},{1,9},{9,1},{17,25},{25,17},{2,10},{10... | collective-permute-start | bytes 393224 | tf_op jit(solution)/shard_map/ppermute | solution.py:297
  23.5 14.1 %collective-permute-start.8 = (f32[4,4,24,128]{3,2,1,0:T(8,128)S(1)}, f32[4,4,24,128]{3,2,1,0:T(8,128)S(1)}, u32[]{:S(2)}, u32[]{:S(2)}) collective-permute-start(f32[4,4,24,128]{3,2,1,0:T(8,128)S(1)} %maximum_maximum_fusion.1), channel_id=1, source_target_pairs={{1,2},{2,1},{3,4},{4,3},{5,6},{6,5},{9,10},{10,9},{11,12},{12,11},... | collective-permute-start | bytes 589832 | tf_op jit(solution)/shard_map/ppermute | solution.py:312
  24.2 13.4 %collective-permute-start.7 = (f32[4,4,24,128]{3,2,1,0:T(8,128)S(1)}, f32[4,4,24,128]{3,2,1,0:T(8,128)S(1)}, u32[]{:S(2)}, u32[]{:S(2)}) collective-permute-start(f32[4,4,24,128]{3,2,1,0:T(8,128)S(1)} %maximum_maximum_fusion), channel_id=1, source_target_pairs={{0,1},{1,0},{2,3},{3,2},{4,5},{5,4},{6,7},{7,6},{8,9},{9,8},{10,11... | collective-permute-start | bytes 589832 | tf_op jit(solution)/shard_map/ppermute | solution.py:312
  28.5 5.1 %collective-permute-start.4 = (f32[2,8,128]{2,1,0:T(8,128)S(1)}, f32[2,8,128]{2,1,0:T(8,128)S(1)}, u32[]{:S(2)}, u32[]{:S(2)}) collective-permute-start(f32[2,8,128]{2,1,0:T(8,128)S(1)} %get-tuple-element.23), channel_id=1, source_target_pairs={{1,2},{2,1},{3,4},{4,3},{5,6},{6,5},{9,10},{10,9},{11,12},{12,11},... | collective-permute-start | bytes 24584 | tf_op jit(solution)/shard_map/ppermute | solution.py:324
  29.2 8.4 %collective-permute-start.3 = (f32[2,8,128]{2,1,0:T(8,128)S(1)}, f32[2,8,128]{2,1,0:T(8,128)S(1)}, u32[]{:S(2)}, u32[]{:S(2)}) collective-permute-start(f32[2,8,128]{2,1,0:T(8,128)S(1)} %get-tuple-element.24), channel_id=1, source_target_pairs={{0,1},{1,0},{2,3},{3,2},{4,5},{5,4},{6,7},{7,6},{8,9},{9,8},{10,11... | collective-permute-start | bytes 24584 | tf_op jit(solution)/shard_map/ppermute | solution.py:324
  54.2 14.5 %collective-permute-start.11 = (f32[32,16,128]{2,1,0:T(8,128)S(1)}, f32[32,16,128]{2,1,0:T(8,128)S(1)}, u32[]{:S(2)}, u32[]{:S(2)}) collective-permute-start(f32[32,16,128]{2,1,0:T(8,128)S(1)} %get-tuple-element.8.rest_0_), channel_id=1, source_target_pairs={{0,24},{8,16},{16,8},{24,0},{1,25},{9,17},{17,9},{25,1},{2,26},{10... | collective-permute-start | bytes 786440 | tf_op jit(solution)/shard_map/ppermute | solution.py:281
  54.3 14.4 %collective-permute-start.10 = (f32[32,16,128]{2,1,0:T(8,128)S(1)}, f32[32,16,128]{2,1,0:T(8,128)S(1)}, u32[]{:S(2)}, u32[]{:S(2)}) collective-permute-start(f32[32,16,128]{2,1,0:T(8,128)S(1)} %get-tuple-element.8.rest_0_), channel_id=1, source_target_pairs={{0,16},{8,24},{16,0},{24,8},{1,17},{9,25},{17,1},{25,9},{2,18},{10... | collective-permute-start | bytes 786440 | tf_op jit(solution)/shard_map/ppermute | solution.py:281
  56.2 12.6 %collective-permute-start.9 = (f32[32,16,128]{2,1,0:T(8,128)S(1)}, f32[32,16,128]{2,1,0:T(8,128)S(1)}, u32[]{:S(2)}, u32[]{:S(2)}) collective-permute-start(f32[32,16,128]{2,1,0:T(8,128)S(1)} %get-tuple-element.8.rest_0_), channel_id=1, source_target_pairs={{0,8},{8,0},{16,24},{24,16},{1,9},{9,1},{17,25},{25,17},{2,10},{10... | collective-permute-start | bytes 786440 | tf_op jit(solution)/shard_map/ppermute | solution.py:281

commit v2 on v0

v2 whole, which is shorter than its diff:
```python
import functools

import jax
import jax.numpy as jnp
from jax import lax
from jax.experimental import pallas as pl
from jax.experimental.pallas import tpu as pltpu
from jax.sharding import PartitionSpec as P

PL = 16
SWEEPS = 4
HALO = 4
PAD = 8
LANES = 128
SUB = 8
MIB = 1 << 20
BLOCK = 8
LOOK = 4
LAY = 4
SETTLE = 4
EDGE_COST = 10 * MIB
TABLE_COST = 10 * MIB
LAY_COST = 3 * MIB
LATER = pl.ANY
PAIRS = 16


def merge(parts, width):
    lane = lax.broadcasted_iota(jnp.int32, (SUB, LANES), 1)
    while len(parts) > 1:
        low = (lane & width) == 0
        merged = []
        for a, b in zip(parts[::2], parts[1::2]):
            merged.append(jnp.where(low, a, b) + pltpu.roll(jnp.where(low, b, a), width, 1))
        parts = merged
        width *= 2
    return parts[0]


def table_kernel(green_ref, inject_ref, out_ref, part_ref):
    slabs, _, states, columns = green_ref.shape
    chunks = columns // LANES
    groups = states // SUB
    for slab in range(slabs):
        weights = [
            [
                jnp.broadcast_to(inject_ref[slab, c : c + 1, k * LANES : (k + 1) * LANES], (SUB, LANES))
                for k in range(chunks)
            ]
            for c in range(2)
        ]

        def some_groups(i, _, slab=slab, weights=weights):
            for pair in range(PAIRS):
                sums = [[], []]
                for g in range(2):
                    rows = pl.ds(pl.multiple_of((i * (2 * PAIRS) + 2 * pair + g) * SUB, SUB), SUB)
                    total = [None, None]
                    for k in range(chunks):
                        cols = slice(k * LANES, (k + 1) * LANES)
                        re = green_ref[slab, 0, rows, cols]
                        im = green_ref[slab, 1, rows, cols]
                        squared = re * re + im * im
                        for c in range(2):
                            term = squared * weights[c][k]
                            total[c] = term if total[c] is None else total[c] + term
                    for c in range(2):
                        sums[c].append(total[c])
                for c in range(2):
                    part_ref[slab, c, i * PAIRS + pair] = merge(sums[c], 1)
            return _

        lax.fori_loop(0, groups // (2 * PAIRS), some_groups, None)
    lane = lax.broadcasted_iota(jnp.int32, (SUB, LANES), 1)
    count, width = groups // 2, 2
    while count > 1:
        low = (lane & width) == 0
        count //= 2
        for slab in range(slabs):
            for c in range(2):
                for k in range(count):
                    a, b = part_ref[slab, c, 2 * k], part_ref[slab, c, 2 * k + 1]
                    both = jnp.where(low, a, b) + pltpu.roll(jnp.where(low, b, a), width, 1)
                    if count > 1:
                        part_ref[slab, c, k] = both
                    else:
                        out_ref[slab, c] = both
        width *= 2


def orbital_table(green, inject):
    slabs, _, states, _ = green.shape
    vmem = pl.BlockSpec(memory_space=pltpu.VMEM)
    return pl.pallas_call(
        table_kernel,
        in_specs=[vmem, vmem],
        out_specs=vmem,
        out_shape=jax.ShapeDtypeStruct((slabs, 2, SUB, LANES), jnp.float32),
        scratch_shapes=[pltpu.VMEM((slabs, 2, states // SUB // 2, SUB, LANES), jnp.float32)],
        compiler_params=pltpu.CompilerParams(vmem_limit_bytes=20 * MIB),
        cost_estimate=pl.CostEstimate(flops=0, bytes_accessed=TABLE_COST, transcendentals=0),
        name="table",
    )(green, inject)


def lookup(tables, choice):
    lane = choice >> 3
    group = choice & (SUB - 1)
    bits = [(group & (1 << b)) != 0 for b in range(3)]
    out = []
    for table in tables:
        found = [jnp.take_along_axis(t, lane, axis=1, mode="promise_in_bounds") for t in table]
        for bit in bits:
            found = [jnp.where(bit, found[2 * k + 1], found[2 * k]) for k in range(len(found) // 2)]
        out.append(found[0])
    return out


def permittivity(regions):
    return jnp.where(regions == 0, 1.0, jnp.where(regions == 1, 0.33, 1.7)).astype(jnp.float32)


def grouped(count, size, step, carry):
    odd = count % size
    if odd:
        carry = step(0, odd, carry)
    return lax.fori_loop(0, count // size, lambda i, c: step(odd + i * size, size, c), carry)


def around(center, below, above, left, right):
    lane = lax.broadcasted_iota(jnp.int32, (SUB, LANES), 1)
    after = jnp.where(lane < LANES - 1, pltpu.roll(center, LANES - 1, 1), 0.0)
    ahead = jnp.where(lane > 0, pltpu.roll(center, 1, 1), 0.0)
    return above + below + right + left + after + ahead


def position():
    return lax.axis_index("energy"), lax.axis_index("space"), lax.axis_size("energy"), lax.axis_size("space")


def edge_rows_kernel(regions_ref, dopant_ref, green_ref, inject_ref, mesh_ref, old_ref, first_ref, second_ref):
    odd = (lax.axis_index("energy") & 1) == 1
    planes, own, _ = regions_ref.shape
    top, bottom = slice(0, HALO), slice(own - HALO, own)

    def pack(first, count, _):
        for k in range(count):
            p = first + k
            permit = permittivity(regions_ref[p])
            dopant = dopant_ref[p]
            for field, values in ((0, permit), (1, dopant)):
                first_ref[field, p] = jnp.where(odd, values[top], values[bottom])
                second_ref[field, p] = jnp.where(odd, values[bottom], values[top])
        return _

    grouped(planes, LAY, pack, None)


def edge_rows(regions, dopant, *later):
    planes, _, lanes = regions.shape
    vmem = pl.BlockSpec(memory_space=pltpu.VMEM)
    return pl.pallas_call(
        edge_rows_kernel,
        in_specs=[vmem] * 2 + [pl.BlockSpec(memory_space=LATER)] * len(later),
        out_specs=[vmem] * 2,
        out_shape=[jax.ShapeDtypeStruct((2, planes, HALO, lanes), jnp.float32)] * 2,
        compiler_params=pltpu.CompilerParams(vmem_limit_bytes=4 * MIB),
        cost_estimate=pl.CostEstimate(flops=0, bytes_accessed=EDGE_COST, transcendentals=0),
        name="edge_rows",
    )(regions, dopant, *(pltpu.with_memory_space_constraint(x, pltpu.HBM) for x in later))


def edge_planes_kernel(mesh_ref, old_ref, regions_ref, dopant_ref, rows1_ref, rows2_ref, first_ref, second_ref):
    e, s, ne, _ = position()
    odd_e, odd_s = (e & 1) == 1, (s & 1) == 1
    planes, own, _ = regions_ref.shape
    row0 = pl.multiple_of(e * own, SUB)
    full_rows = mesh_ref.shape[1]
    up_from = pl.multiple_of(jnp.maximum(row0 - SUB, 0), SUB)
    down_from = pl.multiple_of(jnp.minimum(row0 + own, full_rows - SUB), SUB)
    up, mid, down = slice(0, HALO), slice(HALO, HALO + own), slice(HALO + own, own + 2 * HALO)
    near = HALO - 1
    for out_ref, at_low in ((first_ref, odd_s), (second_ref, jnp.logical_not(odd_s))):
        for k in range(HALO):
            p = jnp.where(at_low, k, planes - HALO + k)
            out_ref[3 * near + k, up] = jnp.where(e > 0, old_ref[p, pl.ds(up_from, SUB)][SUB - HALO :], 0.0)
            out_ref[3 * near + k, mid] = old_ref[p, pl.ds(row0, own)]
            out_ref[3 * near + k, down] = jnp.where(e < ne - 1, old_ref[p, pl.ds(down_from, SUB)][:HALO], 0.0)
        for k in range(near):
            p = jnp.where(at_low, k, planes - near + k)
            out_ref[k, up] = mesh_ref[p, pl.ds(up_from, SUB)][SUB - HALO :].astype(jnp.float32)
            out_ref[k, mid] = mesh_ref[p, pl.ds(row0, own)].astype(jnp.float32)
            out_ref[k, down] = mesh_ref[p, pl.ds(down_from, SUB)][:HALO].astype(jnp.float32)
            out_ref[near + k, mid] = permittivity(regions_ref[p])
            out_ref[2 * near + k, mid] = dopant_ref[p]
            for field in range(2):
                at = (1 + field) * near + k
                out_ref[at, up] = jnp.where(odd_e, rows1_ref[field, p], rows2_ref[field, p])
                out_ref[at, down] = jnp.where(odd_e, rows2_ref[field, p], rows1_ref[field, p])


def edge_planes(mesh, old, regions, dopant, rows):
    _, own, lanes = regions.shape
    vmem = pl.BlockSpec(memory_space=pltpu.VMEM)
    shape = (3 * (HALO - 1) + HALO, own + 2 * HALO, lanes)
    return pl.pallas_call(
        edge_planes_kernel,
        in_specs=[vmem] * 6,
        out_specs=[vmem] * 2,
        out_shape=[jax.ShapeDtypeStruct(shape, jnp.float32)] * 2,
        compiler_params=pltpu.CompilerParams(vmem_limit_bytes=8 * MIB),
        cost_estimate=pl.CostEstimate(flops=0, bytes_accessed=EDGE_COST, transcendentals=0),
        name="edge_planes",
    )(mesh, old, regions, dopant, *rows)


def lay_kernel(
    mesh_ref, old_ref, regions_ref, dopant_ref, rows1_ref, rows2_ref, planes1_ref, planes2_ref,
    mesh_x, before_x, permit_x, dopant_x, first_x,
):
    e, s, ne, ns = position()
    odd_e, odd_s = (e & 1) == 1, (s & 1) == 1
    planes, own, _ = regions_ref.shape
    span = own + 2 * HALO
    row0 = pl.multiple_of(e * own, SUB)
    full_rows = mesh_ref.shape[1]
    up_in, down_in = e > 0, e < ne - 1
    up, mid, down = slice(0, HALO), slice(HALO, HALO + own), slice(HALO + own, span)
    up_b, mid_b, down_b = (slice(PAD + x.start, PAD + x.stop) for x in (up, mid, down))
    up_from = pl.multiple_of(jnp.maximum(row0 - SUB, 0), SUB)
    down_from = pl.multiple_of(jnp.minimum(row0 + own, full_rows - SUB), SUB)

    def lay(first, count, _):
        for k in range(count):
            p = first + k
            q = p + HALO
            mesh_x[q, mid] = mesh_ref[p, pl.ds(row0, own)]
            mesh_x[q, up] = mesh_ref[p, pl.ds(up_from, SUB)][SUB - HALO :]
            mesh_x[q, down] = mesh_ref[p, pl.ds(down_from, SUB)][:HALO]
            before_x[q, mid_b] = old_ref[p, pl.ds(row0, own)]
            before_x[q, up_b] = jnp.where(up_in, old_ref[p, pl.ds(up_from, SUB)][SUB - HALO :], 0.0)
            before_x[q, down_b] = jnp.where(down_in, old_ref[p, pl.ds(down_from, SUB)][:HALO], 0.0)
            permit_x[q, mid] = permittivity(regions_ref[p])
            dopant_x[q, mid] = dopant_ref[p]
            permit_x[q, up] = jnp.where(odd_e, rows1_ref[0, p], rows2_ref[0, p])
            permit_x[q, down] = jnp.where(odd_e, rows2_ref[0, p], rows1_ref[0, p])
            dopant_x[q, up] = jnp.where(odd_e, rows1_ref[1, p], rows2_ref[1, p])
            dopant_x[q, down] = jnp.where(odd_e, rows2_ref[1, p], rows1_ref[1, p])
        return _

    grouped(planes, LAY, lay, None)
    whole_b = slice(PAD, PAD + span)
    near = HALO - 1
    for low in (True, False):
        a, b = (planes1_ref, planes2_ref) if low else (planes2_ref, planes1_ref)
        for k in range(near):
            q = 1 + k if low else HALO + planes + k
            mesh_x[q] = jnp.where(odd_s, a[k], b[k]).astype(jnp.int32)
            permit_x[q] = jnp.where(odd_s, a[near + k], b[near + k])
            dopant_x[q] = jnp.where(odd_s, a[2 * near + k], b[2 * near + k])
        for k in range(HALO):
            q = k if low else HALO + planes + k
            before_x[q, whole_b] = jnp.where(odd_s, a[3 * near + k], b[3 * near + k])

    def terms(first, count, _):
        for r in range(0, span, SUB):
            held = [before_x[1 + first + k, PAD + r : PAD + r + SUB] for k in range(-1, count + 1)]
            for k in range(count):
                q = 1 + first + k
                neighbours = around(
                    held[k + 1], held[k], held[k + 2],
                    before_x[q, PAD + r - 1 : PAD + r - 1 + SUB], before_x[q, PAD + r + 1 : PAD + r + 1 + SUB],
                )
                rows = slice(r, r + SUB)
                first_x[q, rows] = permit_x[q, rows] * (6.0 * held[k + 1] - neighbours) - dopant_x[q, rows]
        return _

    grouped(planes + 2 * near, BLOCK, terms, None)


def laid(mesh, old, regions, dopant, rows, edge_planes):
    planes, own, lanes = regions.shape
    cells = (planes + 2 * HALO, own + 2 * HALO, lanes)
    padded = (cells[0], cells[1] + 2 * PAD, lanes)
    vmem = pl.BlockSpec(memory_space=pltpu.VMEM)
    f32 = jnp.float32
    return pl.pallas_call(
        lay_kernel,
        in_specs=[vmem] * 8,
        out_specs=[vmem] * 5,
        out_shape=[
            jax.ShapeDtypeStruct(shape, kind)
            for shape, kind in ((cells, jnp.int32), (padded, f32), (cells, f32), (cells, f32), (cells, f32))
        ],
        compiler_params=pltpu.CompilerParams(vmem_limit_bytes=16 * MIB),
        cost_estimate=pl.CostEstimate(flops=0, bytes_accessed=LAY_COST, transcendentals=0),
        name="lay",
    )(mesh, old, regions, dopant, *rows, *edge_planes)


def sweep_kernel(
    tables_ref, beside1_ref, beside2_ref, mesh_x, before_x, permit_x, dopant_x, first_x,
    change_ref, most_ref, electron_s, hole_s, now_s, next_s,
):
    e, s, ne, ns = position()
    odd_s = (s & 1) == 1
    planes, own, _ = change_ref.shape
    slabs = tables_ref.shape[0]
    span = own + 2 * HALO
    up_in, down_in = e > 0, e < ne - 1
    tops = range(0, span, SUB)
    row = lax.broadcasted_iota(jnp.int32, (SUB, LANES), 0)

    def table_of(slab_value):
        return [
            [jnp.broadcast_to(slab_value[c, g : g + 1], (SUB, LANES)) for g in range(SUB)]
            for c in range(2)
        ]

    def densities(q, tables):
        for r in tops:
            rows = slice(r, r + SUB)
            found = lookup(tables, mesh_x[q, rows])
            if r == tops[0]:
                found = [jnp.where((row >= HALO) | up_in, v, 1.0) for v in found]
            if r == tops[-1]:
                found = [jnp.where((row < HALO) | down_in, v, 1.0) for v in found]
            electrons, holes = found
            electron_s[q, rows] = electrons
            hole_s[q, rows] = holes
            mismatch = first_x[q, rows] + electrons - holes
            jacobian = 6.0 * permit_x[q, rows] + electrons + holes
            now_s[q, PAD + r : PAD + r + SUB] = before_x[q, PAD + r : PAD + r + SUB] - mismatch / jacobian

    for slab in range(slabs):
        table = table_of(tables_ref[slab])

        def some(first, count, _, table=table, slab=slab):
            for k in range(count):
                densities(HALO + slab * PL + first + k, table)
            return _

        grouped(PL, LOOK, some, None)
    low_table = table_of(jnp.where(s > 0, jnp.where(odd_s, beside1_ref[...], beside2_ref[...]), 1.0))
    for q in range(1, HALO):
        densities(q, low_table)
    high_table = table_of(jnp.where(s < ns - 1, jnp.where(odd_s, beside2_ref[...], beside1_ref[...]), 1.0))
    for q in range(HALO + planes, HALO + planes + HALO - 1):
        densities(q, high_table)

    source = now_s
    for sweep in range(1, SWEEPS):
        final = sweep == SWEEPS - 1
        target = next_s if source is now_s else now_s
        starts = range(HALO, HALO + own, SUB) if final else tops

        def step(first, count, most, sweep=sweep, source=source, target=target, starts=starts, final=final):
            for r in starts:
                rows = slice(r, r + SUB)
                at = PAD + r
                rows_b = slice(at, at + SUB)
                held = [source[1 + sweep + first + k, rows_b] for k in range(-1, count + 1)]
                for k in range(count):
                    q = 1 + sweep + first + k
                    center = held[k + 1]
                    neighbours = around(
                        center, held[k], held[k + 2],
                        source[q, at - 1 : at - 1 + SUB], source[q, at + 1 : at + 1 + SUB],
                    )
                    permit = permit_x[q, rows]
                    before = before_x[q, rows_b]
                    moved = center - before
                    electrons = electron_s[q, rows] * jnp.exp(moved)
                    holes = hole_s[q, rows] * jnp.exp(-moved)
                    mismatch = permit * (6.0 * center - neighbours) - (dopant_x[q, rows] + holes - electrons)
                    jacobian = 6.0 * permit + electrons + holes
                    fresh = center - mismatch / jacobian
                    if final:
                        change = fresh - before
                        change_ref[q - HALO, r - HALO : r - HALO + SUB] = change
                        most = jnp.maximum(most, jnp.abs(change))
                    else:
                        target[q, rows_b] = fresh
            return most

        most = grouped(planes + 2 * (SWEEPS - 1 - sweep), BLOCK, step, jnp.zeros((SUB, LANES), jnp.float32))
        if final:
            most_ref[...] = jnp.broadcast_to(jnp.max(most, axis=0, keepdims=True)[None], most_ref.shape)
        source = target


def swept(tables, beside, fields, own):
    cells, padded = fields[0].shape, fields[1].shape
    planes, lanes = cells[0] - 2 * HALO, cells[2]
    vmem = pl.BlockSpec(memory_space=pltpu.VMEM)
    f32 = jnp.float32
    return pl.pallas_call(
        sweep_kernel,
        in_specs=[vmem] * 8,
        out_specs=[vmem, vmem],
        out_shape=[
            jax.ShapeDtypeStruct((planes, own, lanes), f32),
            jax.ShapeDtypeStruct((lax.axis_size(("energy", "space")), 1, lanes), f32),
        ],
        scratch_shapes=[pltpu.VMEM(cells, f32)] * 2 + [pltpu.VMEM(padded, f32)] * 2,
        compiler_params=pltpu.CompilerParams(vmem_limit_bytes=24 * MIB),
        name="sweeps",
    )(tables, *beside, *fields)


def settle_kernel(most_ref, old_ref, *rest):
    parts, out_ref, result, sems = rest[:-3], rest[-3], rest[-2], rest[-1]
    e = lax.axis_index("energy")
    planes, own, _ = parts[0].shape
    scale = 1.0 / (1.0 + jnp.max(most_ref[...]))
    size = planes // SETTLE
    copies = []
    for b in range(SETTLE):
        at = slice(b * size, (b + 1) * size)
        for k, part in enumerate(parts):
            rows = pl.ds(pl.multiple_of((e ^ k) * own, SUB), own)
            result[at, rows] = old_ref[at, rows] + part[at] * scale
        copies.append(pltpu.make_async_copy(result.at[at], out_ref.at[at], sems.at[b]))
        copies[-1].start()
    for copy in copies:
        copy.wait()


def settled(most, old, parts):
    vmem = pl.BlockSpec(memory_space=pltpu.VMEM)
    return pl.pallas_call(
        settle_kernel,
        in_specs=[vmem] * (2 + len(parts)),
        out_specs=pl.BlockSpec(memory_space=pl.ANY),
        out_shape=jax.ShapeDtypeStruct(old.shape, jnp.float32),
        scratch_shapes=[pltpu.VMEM(old.shape, jnp.float32), pltpu.SemaphoreType.DMA((SETTLE,))],
        compiler_params=pltpu.CompilerParams(vmem_limit_bytes=16 * MIB),
        name="settle",
    )(most, old, *parts)


def pairs(axis, odd_first):
    count = lax.axis_size(axis)
    out = []
    for low in range(1 if odd_first else 0, count - 1, 2):
        out += [(low, low + 1), (low + 1, low)]
    return out


def toggled(x, axis, mask):
    return lax.ppermute(x, axis, [(i, i ^ mask) for i in range(lax.axis_size(axis))])


def on_device(green_blocks, injection, mesh_state_choice, regions, dopant_charge_field, earlier_voltage):
    ne, ns = lax.axis_size("energy"), lax.axis_size("space")
    odd_s = lax.axis_index("space") & 1
    _, own, lanes = regions.shape

    rows = [
        lax.ppermute(x, "energy", pairs("energy", odd_first))
        for x, odd_first in zip(edge_rows(regions, dopant_charge_field, green_blocks[0], injection[0], mesh_state_choice, earlier_voltage), (False, True))
    ]
    sent = edge_planes(mesh_state_choice, earlier_voltage, regions, dopant_charge_field, rows)
    beyond = [lax.ppermute(x, "space", pairs("space", odd)) for x, odd in zip(sent, (False, True))]

    inject, _ = lax.optimization_barrier((injection[0], sent))
    tables = orbital_table(green_blocks[0], inject)
    terms = [tables] + [toggled(tables, "energy", k) for k in range(1, ne)]
    cells = laid(mesh_state_choice, earlier_voltage, regions, dopant_charge_field, rows, beyond)
    while len(terms) > 1:
        terms = [terms[2 * k] + terms[2 * k + 1] for k in range(len(terms) // 2)]
    tables = terms[0]
    beside = []
    for odd_first in (False, True):
        at_low = odd_s if not odd_first else 1 - odd_s
        edge = jnp.where(at_low == 1, tables[0], tables[-1])
        beside.append(lax.ppermute(edge, "space", pairs("space", odd_first)))

    change, most = swept(tables, beside, cells, own)
    parts = {0: change}
    for k in range(2, ne, 2):
        parts[k] = toggled(change, "energy", k)
    parts[1] = toggled(change, "energy", 1)
    most = lax.all_to_all(most, ("energy", "space"), 0, 0)
    far = [parts[k] for k in range(2, ne, 2)]
    most, far = lax.optimization_barrier((most, far))
    for k, part in zip(range(2, ne, 2), far):
        parts[k ^ 1] = toggled(part, "energy", 1)
    return settled(most, earlier_voltage, [parts[k] for k in range(ne)])


def solution(mesh):
    placed = (
        P("energy", "space", None, None, None),
        P("energy", "space", None, None),
        P("space", None, None),
        P("space", "energy", None),
        P("space", "energy", None),
        P("space", None, None),
    )
    return jax.shard_map(
        on_device, mesh=mesh, in_specs=placed, out_specs=P("space", None, None), check_vma=False
    )
```

time: 1120 us -> 48.8 us (0.04)
  local copies, waits for them, and re-layouts: 942 us -> 5.01 us
  blocking collectives: 47.4 us -> 0 us
  waiting for transfers between devices: 47.9 us -> 9.26 us
  starting transfers between devices: 44.7 us -> 23.8 us
  between operations: 14.4 us -> 0.14 us
  other arithmetic: 12.1 us -> 0.02 us
  matrix products: 11.5 us -> 0 us
    gather x2 -> x0, local copies, waits for them, and re-layouts: 938 us -> none  [deposit_occupation(): deposited = jnp.take(species_occupations, linear_offset, axis=1)]
    pmax x1 -> x0, blocking collectives: 47.4 us -> none  [on_device(): largest = lax.pmax(jnp.max(jnp.abs(change)), ('energy', 'space'))]
    ppermute x16 -> x12, starting transfers between devices: 44.7 us -> 18 us  [the longest x6 7.74 us: toggled(): lax.ppermute(x, axis, [(i, i ^ mask) for i in range(lax.axis_size(axis))])]
    reduce_scatter x1 -> x0, waiting for transfers between devices: 20.9 us -> none  [on_device(): lax.psum_scatter(whole_mesh, 'energy', scatter_dimension=2, tiled=True)]
    all_gather x1 -> x0, waiting for transfers between devices: 18.2 us -> none  [on_device(): return lax.all_gather(settled, 'energy', axis=1, tiled=True)]
    dot_general x1 -> x0, matrix products: 11.5 us -> none  [on_device(): jnp.einsum('esij,espj->spi', squared, injection, precision=lax.Precision....]
  transfers between devices with their start and end apart: 18 -> 13, of which waited for: 10 -> 5; matrix products, arithmetic and copies ran while one was open for 0% -> 0% of each run, Pallas kernels for 0% -> 2%
where the time goes in v2:
time: 48.8 us; the launch traced here: 48.7 us
  starting transfers between devices  23.8 us (49%)
  Pallas kernels  10.4 us (21%)
  waiting for transfers between devices  9.26 us (19%)
  local copies, waits for them, and re-layouts  5.01 us (10%)
    ppermute x6, starting transfers between devices, toggled(): lax.ppermute(x, axis, [(i, i ^ mask) for i in range(lax.axis_size(axis))])  7.74 us
    all_to_all x1, waiting for transfers between devices, on_device(): most = lax.all_to_all(most, ('energy', 'space'), 0, 0)  6.72 us
    ppermute x2, starting transfers between devices, on_device(): beside.append(lax.ppermute(edge, 'space', pairs('space', odd_first)))  6.26 us
    all_to_all x1, starting transfers between devices, on_device(): most = lax.all_to_all(most, ('energy', 'space'), 0, 0)  5.78 us
    pallas_call x1, Pallas kernels, swept(): pl.pallas_call(sweep_kernel, in_specs=[vmem] * 8, out_specs=[vmem, vmem],...  5.2 us
    unnamed x16, local copies, waits for them, and re-layouts  5.01 us
    pallas_call x1, Pallas kernels, orbital_table(): pl.pallas_call(table_kernel, in_specs=[vmem, vmem], out_specs=vmem, out_s...  3.02 us
    ppermute x2, starting transfers between devices, on_device(): lax.ppermute(x, 'space', pairs('space', odd))  2.73 us
  transfers between devices with their start and end apart: 13, of which 5 were waited for; matrix products, arithmetic and copies ran while one was open for 0% of the time, Pallas kernels for 2%

profile of v2, /device:TPU:0, one launch (start us, length us, event | category | flops | bytes accessed | tf_op | source)
XLA Modules:
  0.0 48.7 jit_solution(7318506307853222570)
XLA Ops:
  0.0 0.0 copy-start.1
  0.0 0.0 copy-start.2
  0.0 0.0 copy-start
  0.0 0.0 copy-start.3
  0.0 1.1 %copy-done.3 = s32[32,16,128]{2,1,0:T(8,128)S(1)} copy-done((s32[32,16,128]{2,1,0:T(8,128)S(1)}, s32[32,16,128]{2,1,0:T(8,128)}, u32[]{:S(2)}) %copy-start.3) | copy-done | bytes 262168
  1.1 0.0 copy-start.5
  1.1 1.5 %copy-done.5 = f32[32,16,128]{2,1,0:T(8,128)S(1)} copy-done((f32[32,16,128]{2,1,0:T(8,128)S(1)}, f32[32,16,128]{2,1,0:T(8,128)}, u32[]{:S(2)}) %copy-start.5) | copy-done | bytes 262168
  2.6 0.0 copy-start.4
  2.6 0.0 copy-start.6
  2.6 0.0 copy-start.7
  2.6 0.1 edge_rows.1
  2.7 0.5 %collective-permute-start = (f32[2,32,4,128]{3,2,1,0:T(4,128)S(1)}, f32[2,32,4,128]{3,2,1,0:T(4,128)S(1)}, u32[]{:S(2)}, u32[]{:S(2)}) collective-permute-start(f32[2,32,4,128]{3,2,1,0:T(4,128)S(1)} %get-tuple-element.19), channel_id=1, source_target_pairs={{0,8},{8,0},{16,24},{24,16},{1,9},{9,1},{17,25},{25,17},{2,10},{10... | collective-permute-start | bytes 393224 | tf_op jit(solution)/shard_map/ppermute | solution.py:460
  3.3 0.8 %collective-permute-start.1 = (f32[2,32,4,128]{3,2,1,0:T(4,128)S(1)}, f32[2,32,4,128]{3,2,1,0:T(4,128)S(1)}, u32[]{:S(2)}, u32[]{:S(2)}) collective-permute-start(f32[2,32,4,128]{3,2,1,0:T(4,128)S(1)} %get-tuple-element.20), channel_id=1, source_target_pairs={{8,16},{16,8},{9,17},{17,9},{10,18},{18,10},{11,19},{19,11},{12,20... | collective-permute-start | bytes 393224 | tf_op jit(solution)/shard_map/ppermute | solution.py:460
  4.1 0.2 collective-permute-done.rows1_ref
  4.3 0.0 collective-permute-done.1.rows2_ref
  4.3 0.0 copy-done.1
  4.3 0.0 copy-done.2
  4.3 0.0 copy-done.4
  4.3 0.0 copy-done.6
  4.3 0.1 edge_planes.1
  4.4 2.4 %copy-done = f32[1,2,2,1024,1024]{4,3,2,1,0:T(8,128)S(1)} copy-done((f32[1,2,2,1024,1024]{4,3,2,1,0:T(8,128)S(1)}, f32[1,2,2,1024,1024]{4,3,2,1,0:T(8,128)}, u32[]{:S(2)}) %copy-start) | copy-done | bytes 16777240
  6.7 0.0 copy-done.7
  6.7 3.0 %table.1 = f32[2,2,8,128]{3,2,1,0:T(8,128)S(1)} custom-call(f32[2,2,1024,1024]{3,2,1,0:T(8,128)S(1)} %bitcast.7, f32[2,2,1024]{2,1,0:T(2,128)S(1)} %bitcast.9), custom_call_target="tpu_custom_call" | custom-call | bytes 10485760 | tf_op jit(solution)/shard_map/table/pallas_call | solution.py:94
  9.8 2.4 %collective-permute-start.4 = (f32[2,2,8,128]{3,2,1,0:T(8,128)S(1)}, f32[2,2,8,128]{3,2,1,0:T(8,128)S(1)}, u32[]{:S(2)}, u32[]{:S(2)}) collective-permute-start(f32[2,2,8,128]{3,2,1,0:T(8,128)S(1)} %table.1), channel_id=1, source_target_pairs={{0,24},{8,16},{16,8},{24,0},{1,25},{9,17},{17,9},{25,1},{2,26},{10... | collective-permute-start | bytes 49160 | tf_op jit(solution)/shard_map/ppermute | solution.py:451
  12.2 3.5 %collective-permute-start.3 = (f32[2,2,8,128]{3,2,1,0:T(8,128)S(1)}, f32[2,2,8,128]{3,2,1,0:T(8,128)S(1)}, u32[]{:S(2)}, u32[]{:S(2)}) collective-permute-start(f32[2,2,8,128]{3,2,1,0:T(8,128)S(1)} %table.1), channel_id=1, source_target_pairs={{0,16},{8,24},{16,0},{24,8},{1,17},{9,25},{17,1},{25,9},{2,18},{10... | collective-permute-start | bytes 49160 | tf_op jit(solution)/shard_map/ppermute | solution.py:451
  15.6 0.0 collective-permute-start.2
  15.6 2.1 %collective-permute-start.7 = (f32[13,24,128]{2,1,0:T(8,128)S(1)}, f32[13,24,128]{2,1,0:T(8,128)S(1)}, u32[]{:S(2)}, u32[]{:S(2)}) collective-permute-start(f32[13,24,128]{2,1,0:T(8,128)S(1)} %get-tuple-element.21), channel_id=1, source_target_pairs={{0,1},{1,0},{2,3},{3,2},{4,5},{5,4},{6,7},{7,6},{8,9},{9,8},{10,11... | collective-permute-start | bytes 479240 | tf_op jit(solution)/shard_map/ppermute | solution.py:464
  17.7 0.7 %collective-permute-start.8 = (f32[13,24,128]{2,1,0:T(8,128)S(1)}, f32[13,24,128]{2,1,0:T(8,128)S(1)}, u32[]{:S(2)}, u32[]{:S(2)}) collective-permute-start(f32[13,24,128]{2,1,0:T(8,128)S(1)} %get-tuple-element.22), channel_id=1, source_target_pairs={{1,2},{2,1},{3,4},{4,3},{5,6},{6,5},{9,10},{10,9},{11,12},{12,11},... | collective-permute-start | bytes 479240 | tf_op jit(solution)/shard_map/ppermute | solution.py:464
  18.4 0.0 collective-permute-done.4
  18.4 0.0 collective-permute-done.3
  18.4 0.0 collective-permute-done.2
  18.5 0.7 %collective-permute-start.6 = (f32[2,8,128]{2,1,0:T(8,128)S(1)}, f32[2,8,128]{2,1,0:T(8,128)S(1)}, u32[]{:S(2)}, u32[]{:S(2)}) collective-permute-start(f32[2,8,128]{2,1,0:T(8,128)S(1)} %get-tuple-element.33), channel_id=1, source_target_pairs={{1,2},{2,1},{3,4},{4,3},{5,6},{6,5},{9,10},{10,9},{11,12},{12,11},... | collective-permute-start | bytes 24584 | tf_op jit(solution)/shard_map/ppermute | solution.py:477
  19.1 5.6 %collective-permute-start.5 = (f32[2,8,128]{2,1,0:T(8,128)S(1)}, f32[2,8,128]{2,1,0:T(8,128)S(1)}, u32[]{:S(2)}, u32[]{:S(2)}) collective-permute-start(f32[2,8,128]{2,1,0:T(8,128)S(1)} %get-tuple-element.34), channel_id=1, source_target_pairs={{0,1},{1,0},{2,3},{3,2},{4,5},{5,4},{6,7},{7,6},{8,9},{9,8},{10,11... | collective-permute-start | bytes 24584 | tf_op jit(solution)/shard_map/ppermute | solution.py:477
  24.7 0.6 %collective-permute-done.7.planes1_ref = f32[13,24,128]{2,1,0:T(8,128)S(1)} collective-permute-done((f32[13,24,128]{2,1,0:T(8,128)S(1)}, f32[13,24,128]{2,1,0:T(8,128)S(1)}, u32[]{:S(2)}, u32[]{:S(2)}) %collective-permute-start.7) | collective-permute-done | bytes 159776 | tf_op jit(solution)/shard_map/ppermute | solution.py:464
  25.3 0.0 collective-permute-done.8.planes2_ref
  25.3 0.8 %lay.1 = (s32[40,24,128]{2,1,0:T(8,128)S(1)}, f32[40,40,128]{2,1,0:T(8,128)S(1)}, f32[40,24,128]{2,1,0:T(8,128)S(1)}, f32[40,24,128]{2,1,0:T(8,128)S(1)}, f32[40,24,128]{2,1,0:T(8,128)S(1)}) custom-call(s32[32,64,128]{2,1,0:T(8,128)S(1)} %copy-done.2, f32[32,64,128]{2,1,0:T(8,128)S(1)} %copy-done.1, s32[32,16,128]{2,1,0:T(8,128)S(1)} %copy-done.4, ...), custom_call_target="tpu_custom_call" | custom-call | bytes 3145728 | tf_op jit(solution)/shard_map/lay/pallas_call | solution.py:287
  26.1 0.0 collective-permute-done.6.beside2_ref
  26.1 0.2 collective-permute-done.5.beside1_ref
  26.4 5.2 %sweeps.1 = (f32[32,16,128]{2,1,0:T(8,128)S(1)}, f32[32,1,128]{2,1,0:T(1,128)}) custom-call(f32[2,2,8,128]{3,2,1,0:T(8,128)S(1)} %add_add_fusion.tables_ref, f32[2,8,128]{2,1,0:T(8,128)S(1)} %collective-permute-done.5.beside1_ref, f32[2,8,128]{2,1,0:T(8,128)S(1)} %collective-permute-done.6.beside2_ref, s32[40,24,128]{2,1,0:T(8,128)S(1)} %get-tuple-element.24.mesh_x, ...), custom_call_target="tpu_custom_call" | custom-call | tf_op jit(solution)/shard_map/sweeps/pallas_call | solution.py:397
  31.6 1.5 %collective-permute-start.9 = (f32[32,16,128]{2,1,0:T(8,128)S(1)}, f32[32,16,128]{2,1,0:T(8,128)S(1)}, u32[]{:S(2)}, u32[]{:S(2)}) collective-permute-start(f32[32,16,128]{2,1,0:T(8,128)S(1)} %get-tuple-element.30.rest_0_), channel_id=1, source_target_pairs={{0,16},{8,24},{16,0},{24,8},{1,17},{9,25},{17,1},{25,9},{2,18},{10... | collective-permute-start | bytes 786440 | tf_op jit(solution)/shard_map/ppermute | solution.py:451
  33.1 5.8 %all-to-all-start = ((f32[32,1,128]{2,1,0:T(1,128)}), f32[32,1,128]{2,1,0:T(1,128)S(1)}, u32[]{:S(2)}, u32[]{:S(2)}) async-start(f32[32,1,128]{2,1,0:T(1,128)} %get-tuple-element.29), calls=%async_computation | async-start | bytes 32768 | tf_op jit(solution)/shard_map/all_to_all | solution.py:484
  38.9 0.3 collective-permute-start.10
  39.2 6.7 %all-to-all-done.most_ref = f32[32,1,128]{2,1,0:T(1,128)S(1)} async-done(((f32[32,1,128]{2,1,0:T(1,128)}), f32[32,1,128]{2,1,0:T(1,128)S(1)}, u32[]{:S(2)}, u32[]{:S(2)}) %all-to-all-start) | async-done | bytes 16416 | tf_op jit(solution)/shard_map/all_to_all | solution.py:484
  45.9 0.0 collective-permute-done.9.rest_2_
  45.9 0.0 collective-permute-start.11
  45.9 0.0 collective-permute-done.10.rest_1_
  45.9 1.5 %collective-permute-done.11.rest_3_ = f32[32,16,128]{2,1,0:T(8,128)S(1)} collective-permute-done((f32[32,16,128]{2,1,0:T(8,128)S(1)}, f32[32,16,128]{2,1,0:T(8,128)S(1)}, u32[]{:S(2)}, u32[]{:S(2)}) %collective-permute-start.11) | collective-permute-done | bytes 262176 | tf_op jit(solution)/shard_map/ppermute | solution.py:451
  47.5 1.2 %settle.1 = f32[32,64,128]{2,1,0:T(8,128)} custom-call(f32[32,1,128]{2,1,0:T(1,128)S(1)} %all-to-all-done.most_ref, f32[32,64,128]{2,1,0:T(8,128)S(1)} %copy-done.1, f32[32,16,128]{2,1,0:T(8,128)S(1)} %get-tuple-element.30.rest_0_, f32[32,16,128]{2,1,0:T(8,128)S(1)} %collective-permute-done.10.rest_1_, f32[32,16,128]{2,1,0:T(8,128)S(1)} %collective-permute-done.9.rest_2_, ...), custom_call_target="tpu_custom_call" | custom-call | tf_op jit(solution)/shard_map/settle/pallas_call | solution.py:431
  (2 shorter events, 0.0 us)
Async XLA Ops:
  0.0 4.3 %copy-start.1 = (f32[32,64,128]{2,1,0:T(8,128)S(1)}, f32[32,64,128]{2,1,0:T(8,128)}, u32[]{:S(2)}) copy-start(f32[32,64,128]{2,1,0:T(8,128)} %old_ref.7) | copy-start | bytes 3145732
  0.0 4.3 %copy-start.2 = (s32[32,64,128]{2,1,0:T(8,128)S(1)}, s32[32,64,128]{2,1,0:T(8,128)}, u32[]{:S(2)}) copy-start(s32[32,64,128]{2,1,0:T(8,128)} %mesh_ref.5) | copy-start | bytes 3145732
  0.0 6.7 %copy-start = (f32[1,2,2,1024,1024]{4,3,2,1,0:T(8,128)S(1)}, f32[1,2,2,1024,1024]{4,3,2,1,0:T(8,128)}, u32[]{:S(2)}) copy-start(f32[1,2,2,1024,1024]{4,3,2,1,0:T(8,128)} %param.6) | copy-start | bytes 50331652
  0.0 1.1 %copy-start.3 = (s32[32,16,128]{2,1,0:T(8,128)S(1)}, s32[32,16,128]{2,1,0:T(8,128)}, u32[]{:S(2)}) copy-start(s32[32,16,128]{2,1,0:T(8,128)} %regions_ref.5) | copy-start | bytes 786436
  1.1 1.5 %copy-start.5 = (f32[32,16,128]{2,1,0:T(8,128)S(1)}, f32[32,16,128]{2,1,0:T(8,128)}, u32[]{:S(2)}) copy-start(f32[32,16,128]{2,1,0:T(8,128)} %dopant_ref.5) | copy-start | bytes 786436
  2.6 1.6 %copy-start.4 = (s32[32,16,128]{2,1,0:T(8,128)S(1)}, s32[32,16,128]{2,1,0:T(8,128)}, u32[]{:S(2)}) copy-start(s32[32,16,128]{2,1,0:T(8,128)} %regions_ref.5) | copy-start | bytes 786436
  2.6 1.6 %copy-start.6 = (f32[32,16,128]{2,1,0:T(8,128)S(1)}, f32[32,16,128]{2,1,0:T(8,128)}, u32[]{:S(2)}) copy-start(f32[32,16,128]{2,1,0:T(8,128)} %dopant_ref.5) | copy-start | bytes 786436
  2.6 4.1 %copy-start.7 = (f32[1,2,2,1024]{3,2,1,0:T(2,128)S(1)}, f32[1,2,2,1024]{3,2,1,0:T(2,128)}, u32[]{:S(2)}) copy-start(f32[1,2,2,1024]{3,2,1,0:T(2,128)} %param.7) | copy-start | bytes 49156
  2.7 1.5 %collective-permute-start = (f32[2,32,4,128]{3,2,1,0:T(4,128)S(1)}, f32[2,32,4,128]{3,2,1,0:T(4,128)S(1)}, u32[]{:S(2)}, u32[]{:S(2)}) collective-permute-start(f32[2,32,4,128]{3,2,1,0:T(4,128)S(1)} %get-tuple-element.19), channel_id=1, source_target_pairs={{0,8},{8,0},{16,24},{24,16},{1,9},{9,1},{17,25},{25,17},{2,10},{10... | collective-permute-start | bytes 393224 | tf_op jit(solution)/shard_map/ppermute | solution.py:460
  3.3 1.0 %collective-permute-start.1 = (f32[2,32,4,128]{3,2,1,0:T(4,128)S(1)}, f32[2,32,4,128]{3,2,1,0:T(4,128)S(1)}, u32[]{:S(2)}, u32[]{:S(2)}) collective-permute-start(f32[2,32,4,128]{3,2,1,0:T(4,128)S(1)} %get-tuple-element.20), channel_id=1, source_target_pairs={{8,16},{16,8},{9,17},{17,9},{10,18},{18,10},{11,19},{19,11},{12,20... | collective-permute-start | bytes 393224 | tf_op jit(solution)/shard_map/ppermute | solution.py:460
  9.8 8.6 %collective-permute-start.4 = (f32[2,2,8,128]{3,2,1,0:T(8,128)S(1)}, f32[2,2,8,128]{3,2,1,0:T(8,128)S(1)}, u32[]{:S(2)}, u32[]{:S(2)}) collective-permute-start(f32[2,2,8,128]{3,2,1,0:T(8,128)S(1)} %table.1), channel_id=1, source_target_pairs={{0,24},{8,16},{16,8},{24,0},{1,25},{9,17},{17,9},{25,1},{2,26},{10... | collective-permute-start | bytes 49160 | tf_op jit(solution)/shard_map/ppermute | solution.py:451
  12.2 6.2 %collective-permute-start.3 = (f32[2,2,8,128]{3,2,1,0:T(8,128)S(1)}, f32[2,2,8,128]{3,2,1,0:T(8,128)S(1)}, u32[]{:S(2)}, u32[]{:S(2)}) collective-permute-start(f32[2,2,8,128]{3,2,1,0:T(8,128)S(1)} %table.1), channel_id=1, source_target_pairs={{0,16},{8,24},{16,0},{24,8},{1,17},{9,25},{17,1},{25,9},{2,18},{10... | collective-permute-start | bytes 49160 | tf_op jit(solution)/shard_map/ppermute | solution.py:451
  15.6 2.8 %collective-permute-start.2 = (f32[2,2,8,128]{3,2,1,0:T(8,128)S(1)}, f32[2,2,8,128]{3,2,1,0:T(8,128)S(1)}, u32[]{:S(2)}, u32[]{:S(2)}) collective-permute-start(f32[2,2,8,128]{3,2,1,0:T(8,128)S(1)} %table.1), channel_id=1, source_target_pairs={{0,8},{8,0},{16,24},{24,16},{1,9},{9,1},{17,25},{25,17},{2,10},{10... | collective-permute-start | bytes 49160 | tf_op jit(solution)/shard_map/ppermute | solution.py:451
  15.6 9.7 %collective-permute-start.7 = (f32[13,24,128]{2,1,0:T(8,128)S(1)}, f32[13,24,128]{2,1,0:T(8,128)S(1)}, u32[]{:S(2)}, u32[]{:S(2)}) collective-permute-start(f32[13,24,128]{2,1,0:T(8,128)S(1)} %get-tuple-element.21), channel_id=1, source_target_pairs={{0,1},{1,0},{2,3},{3,2},{4,5},{5,4},{6,7},{7,6},{8,9},{9,8},{10,11... | collective-permute-start | bytes 479240 | tf_op jit(solution)/shard_map/ppermute | solution.py:464
  17.7 7.6 %collective-permute-start.8 = (f32[13,24,128]{2,1,0:T(8,128)S(1)}, f32[13,24,128]{2,1,0:T(8,128)S(1)}, u32[]{:S(2)}, u32[]{:S(2)}) collective-permute-start(f32[13,24,128]{2,1,0:T(8,128)S(1)} %get-tuple-element.22), channel_id=1, source_target_pairs={{1,2},{2,1},{3,4},{4,3},{5,6},{6,5},{9,10},{10,9},{11,12},{12,11},... | collective-permute-start | bytes 479240 | tf_op jit(solution)/shard_map/ppermute | solution.py:464
  18.5 7.7 %collective-permute-start.6 = (f32[2,8,128]{2,1,0:T(8,128)S(1)}, f32[2,8,128]{2,1,0:T(8,128)S(1)}, u32[]{:S(2)}, u32[]{:S(2)}) collective-permute-start(f32[2,8,128]{2,1,0:T(8,128)S(1)} %get-tuple-element.33), channel_id=1, source_target_pairs={{1,2},{2,1},{3,4},{4,3},{5,6},{6,5},{9,10},{10,9},{11,12},{12,11},... | collective-permute-start | bytes 24584 | tf_op jit(solution)/shard_map/ppermute | solution.py:477
  19.1 7.2 %collective-permute-start.5 = (f32[2,8,128]{2,1,0:T(8,128)S(1)}, f32[2,8,128]{2,1,0:T(8,128)S(1)}, u32[]{:S(2)}, u32[]{:S(2)}) collective-permute-start(f32[2,8,128]{2,1,0:T(8,128)S(1)} %get-tuple-element.34), channel_id=1, source_target_pairs={{0,1},{1,0},{2,3},{3,2},{4,5},{5,4},{6,7},{7,6},{8,9},{9,8},{10,11... | collective-permute-start | bytes 24584 | tf_op jit(solution)/shard_map/ppermute | solution.py:477
  31.6 14.4 %collective-permute-start.9 = (f32[32,16,128]{2,1,0:T(8,128)S(1)}, f32[32,16,128]{2,1,0:T(8,128)S(1)}, u32[]{:S(2)}, u32[]{:S(2)}) collective-permute-start(f32[32,16,128]{2,1,0:T(8,128)S(1)} %get-tuple-element.30.rest_0_), channel_id=1, source_target_pairs={{0,16},{8,24},{16,0},{24,8},{1,17},{9,25},{17,1},{25,9},{2,18},{10... | collective-permute-start | bytes 786440 | tf_op jit(solution)/shard_map/ppermute | solution.py:451
  33.1 12.8 %all-to-all-start = ((f32[32,1,128]{2,1,0:T(1,128)}), f32[32,1,128]{2,1,0:T(1,128)S(1)}, u32[]{:S(2)}, u32[]{:S(2)}) async-start(f32[32,1,128]{2,1,0:T(1,128)} %get-tuple-element.29), calls=%async_computation | async-start | bytes 32768 | tf_op jit(solution)/shard_map/all_to_all | solution.py:484
  38.9 7.0 %collective-permute-start.10 = (f32[32,16,128]{2,1,0:T(8,128)S(1)}, f32[32,16,128]{2,1,0:T(8,128)S(1)}, u32[]{:S(2)}, u32[]{:S(2)}) collective-permute-start(f32[32,16,128]{2,1,0:T(8,128)S(1)} %get-tuple-element.30.rest_0_), channel_id=1, source_target_pairs={{0,8},{8,0},{16,24},{24,16},{1,9},{9,1},{17,25},{25,17},{2,10},{10... | collective-permute-start | bytes 786440 | tf_op jit(solution)/shard_map/ppermute | solution.py:451
  45.9 1.5 %collective-permute-start.11 = (f32[32,16,128]{2,1,0:T(8,128)S(1)}, f32[32,16,128]{2,1,0:T(8,128)S(1)}, u32[]{:S(2)}, u32[]{:S(2)}) collective-permute-start(f32[32,16,128]{2,1,0:T(8,128)S(1)} %collective-permute-done.9.rest_2_), channel_id=1, source_target_pairs={{0,8},{8,0},{16,24},{24,16},{1,9},{9,1},{17,25},{25,17},{2,10},{10... | collective-permute-start | bytes 786440 | tf_op jit(solution)/shard_map/ppermute | solution.py:451

commit v3 on v2

v3 whole, which is shorter than its diff:
```python
import functools

import jax
import jax.numpy as jnp
from jax import lax
from jax.experimental import pallas as pl
from jax.experimental.pallas import tpu as pltpu
from jax.sharding import PartitionSpec as P

PL = 16
SWEEPS = 4
HALO = 4
PAD = 8
LANES = 128
SUB = 8
MIB = 1 << 20
BLOCK = 16
LOOK = 16
LAY = 16
SETTLE = 4
EDGE_COST = 10 * MIB
TABLE_COST = 10 * MIB
LAY_COST = 3 * MIB
LATER = pl.ANY
PAIRS = 16


def merge(parts, width):
    lane = lax.broadcasted_iota(jnp.int32, (SUB, LANES), 1)
    while len(parts) > 1:
        low = (lane & width) == 0
        merged = []
        for a, b in zip(parts[::2], parts[1::2]):
            merged.append(jnp.where(low, a, b) + pltpu.roll(jnp.where(low, b, a), width, 1))
        parts = merged
        width *= 2
    return parts[0]


def table_kernel(green_ref, inject_ref, rows1_ref, rows2_ref, out_ref, packed1_ref, packed2_ref, part_ref):
    slabs, _, states, columns = green_ref.shape
    chunks = columns // LANES
    groups = states // SUB
    for packed_ref, rows_ref in ((packed1_ref, rows1_ref), (packed2_ref, rows2_ref)):
        packed_ref[2 * slabs * SUB :] = rows_ref[...]
    for slab in range(slabs):
        weights = [
            [
                jnp.broadcast_to(inject_ref[slab, c : c + 1, k * LANES : (k + 1) * LANES], (SUB, LANES))
                for k in range(chunks)
            ]
            for c in range(2)
        ]

        def some_groups(i, _, slab=slab, weights=weights):
            for pair in range(PAIRS):
                sums = [[], []]
                for g in range(2):
                    rows = pl.ds(pl.multiple_of((i * (2 * PAIRS) + 2 * pair + g) * SUB, SUB), SUB)
                    total = [None, None]
                    for k in range(chunks):
                        cols = slice(k * LANES, (k + 1) * LANES)
                        re = green_ref[slab, 0, rows, cols]
                        im = green_ref[slab, 1, rows, cols]
                        squared = re * re + im * im
                        for c in range(2):
                            term = squared * weights[c][k]
                            total[c] = term if total[c] is None else total[c] + term
                    for c in range(2):
                        sums[c].append(total[c])
                for c in range(2):
                    part_ref[slab, c, i * PAIRS + pair] = merge(sums[c], 1)
            return _

        lax.fori_loop(0, groups // (2 * PAIRS), some_groups, None)
    lane = lax.broadcasted_iota(jnp.int32, (SUB, LANES), 1)
    count, width = groups // 2, 2
    while count > 1:
        low = (lane & width) == 0
        count //= 2
        for slab in range(slabs):
            for c in range(2):
                for k in range(count):
                    a, b = part_ref[slab, c, 2 * k], part_ref[slab, c, 2 * k + 1]
                    both = jnp.where(low, a, b) + pltpu.roll(jnp.where(low, b, a), width, 1)
                    if count > 1:
                        part_ref[slab, c, k] = both
                    else:
                        out_ref[slab, c] = both
                        at = (2 * slab + c) * SUB
                        packed1_ref[at : at + SUB] = both
                        packed2_ref[at : at + SUB] = both
        width *= 2


def orbital_table(green, inject, rows):
    slabs, _, states, _ = green.shape
    vmem = pl.BlockSpec(memory_space=pltpu.VMEM)
    packed = jax.ShapeDtypeStruct((2 * slabs * SUB + rows[0].shape[0], LANES), jnp.float32)
    return pl.pallas_call(
        table_kernel,
        in_specs=[vmem] * 4,
        out_specs=[vmem] * 3,
        out_shape=[jax.ShapeDtypeStruct((slabs, 2, SUB, LANES), jnp.float32), packed, packed],
        scratch_shapes=[pltpu.VMEM((slabs, 2, states // SUB // 2, SUB, LANES), jnp.float32)],
        compiler_params=pltpu.CompilerParams(vmem_limit_bytes=20 * MIB),
        cost_estimate=pl.CostEstimate(flops=0, bytes_accessed=TABLE_COST, transcendentals=0),
        name="table",
    )(green, inject, *rows)


def lookup(tables, choice):
    lane = choice >> 3
    group = choice & (SUB - 1)
    bits = [(group & (1 << b)) != 0 for b in range(3)]
    out = []
    for table in tables:
        found = [jnp.take_along_axis(t, lane, axis=1, mode="promise_in_bounds") for t in table]
        for bit in bits:
            found = [jnp.where(bit, found[2 * k + 1], found[2 * k]) for k in range(len(found) // 2)]
        out.append(found[0])
    return out


def permittivity(regions):
    return jnp.where(regions == 0, 1.0, jnp.where(regions == 1, 0.33, 1.7)).astype(jnp.float32)


def grouped(count, size, step, carry):
    odd = count % size
    if odd:
        carry = step(0, odd, carry)
    return lax.fori_loop(0, count // size, lambda i, c: step(odd + i * size, size, c), carry)


def around(center, below, above, left, right):
    lane = lax.broadcasted_iota(jnp.int32, (SUB, LANES), 1)
    after = jnp.where(lane < LANES - 1, pltpu.roll(center, LANES - 1, 1), 0.0)
    ahead = jnp.where(lane > 0, pltpu.roll(center, 1, 1), 0.0)
    return above + below + right + left + after + ahead


def position():
    return lax.axis_index("energy"), lax.axis_index("space"), lax.axis_size("energy"), lax.axis_size("space")


NEAR = HALO - 1


def edge_kernel(
    regions_ref, dopant_ref, mesh_ref, old_ref, green_ref, inject_ref,
    rows1_ref, rows2_ref, planes1_ref, planes2_ref,
    regions_s, dopant_s, mesh_s, old_s, sems,
):
    e, s, ne, _ = position()
    odd_e, odd_s = (e & 1) == 1, (s & 1) == 1
    planes, own, _ = regions_s.shape
    pieces = [(regions_ref, regions_s), (dopant_ref, dopant_s)]
    for source, held in ((mesh_ref, mesh_s), (old_ref, old_s)):
        pieces.append((source.at[0:HALO], held.at[0]))
        pieces.append((source.at[planes - HALO : planes], held.at[1]))
    copies = [pltpu.make_async_copy(a, b, sems.at[k]) for k, (a, b) in enumerate(pieces)]
    for copy in copies:
        copy.start()
    for copy in copies[:2]:
        copy.wait()
    top, bottom = slice(0, NEAR), slice(own - NEAR, own)
    for p in range(planes):
        for field, values in ((0, permittivity(regions_s[p])), (1, dopant_s[p])):
            at = (field * planes + p) * NEAR
            rows1_ref[at : at + NEAR] = jnp.where(odd_e, values[top], values[bottom])
            rows2_ref[at : at + NEAR] = jnp.where(odd_e, values[bottom], values[top])
    for copy in copies[2:]:
        copy.wait()
    row0 = pl.multiple_of(e * own, SUB)
    up_from = pl.multiple_of(jnp.maximum(row0 - SUB, 0), SUB)
    down_from = pl.multiple_of(jnp.minimum(row0 + own, mesh_s.shape[2] - SUB), SUB)
    span = own + 2 * HALO
    for out_ref, side in ((planes1_ref, jnp.where(odd_s, 0, 1)), (planes2_ref, jnp.where(odd_s, 1, 0))):
        for k in range(NEAR):
            p, at = k + side, k * span
            out_ref[at : at + HALO] = mesh_s[side, p, pl.ds(up_from, SUB)][SUB - HALO :].astype(jnp.float32)
            out_ref[at + HALO : at + HALO + own] = mesh_s[side, p, pl.ds(row0, own)].astype(jnp.float32)
            out_ref[at + HALO + own : at + span] = mesh_s[side, p, pl.ds(down_from, SUB)][:HALO].astype(jnp.float32)
            low = planes - NEAR + k
            for field, at in ((0, (NEAR + HALO) * span + k * own), (1, (NEAR + HALO) * span + (NEAR + k) * own)):
                held = regions_s if field == 0 else dopant_s
                values = jnp.where(side == 0, held[k], held[low])
                out_ref[at : at + own] = permittivity(values) if field == 0 else values
        for k in range(HALO):
            at = (NEAR + k) * span
            out_ref[at : at + HALO] = jnp.where(e > 0, old_s[side, k, pl.ds(up_from, SUB)][SUB - HALO :], 0.0)
            out_ref[at + HALO : at + HALO + own] = old_s[side, k, pl.ds(row0, own)]
            out_ref[at + HALO + own : at + span] = jnp.where(
                e < ne - 1, old_s[side, k, pl.ds(down_from, SUB)][:HALO], 0.0
            )


def edges(regions, dopant, mesh, old, green, inject):
    planes, own, lanes = regions.shape
    rows = jax.ShapeDtypeStruct((2 * NEAR * planes, lanes), jnp.float32)
    cells = jax.ShapeDtypeStruct(((NEAR + HALO) * (own + 2 * HALO) + 2 * NEAR * own, lanes), jnp.float32)
    held = (2, HALO) + mesh.shape[1:]
    outs = pl.pallas_call(
        edge_kernel,
        in_specs=[pl.BlockSpec(memory_space=pl.ANY)] * 6,
        out_specs=[pl.BlockSpec(memory_space=pltpu.VMEM)] * 4,
        out_shape=[rows, rows, cells, cells],
        scratch_shapes=[
            pltpu.VMEM(regions.shape, jnp.int32),
            pltpu.VMEM(regions.shape, jnp.float32),
            pltpu.VMEM(held, jnp.int32),
            pltpu.VMEM(held, jnp.float32),
            pltpu.SemaphoreType.DMA((6,)),
        ],
        compiler_params=pltpu.CompilerParams(vmem_limit_bytes=8 * MIB),
        cost_estimate=pl.CostEstimate(flops=0, bytes_accessed=EDGE_COST, transcendentals=0),
        name="edges",
    )(*(pltpu.with_memory_space_constraint(x, pltpu.HBM) for x in (regions, dopant, mesh, old, green, inject)))
    return outs[:2], outs[2:]


def beside_rows(rows1_ref, rows2_ref, at):
    e, _, ne, _ = position()
    odd = (e & 1) == 1
    one = rows1_ref[at : at + NEAR]
    two = jnp.where((e > 0) & (e < ne - 1), rows2_ref[at : at + NEAR], 0.0)
    return jnp.where(odd, one, two), jnp.where(odd, two, one)


def join_kernel(*refs):
    rows1_ref, rows2_ref = refs[-5:-3]
    tables_ref, first_ref, second_ref = refs[-3:]
    odd_s = (lax.axis_index("space") & 1) == 1
    slabs = tables_ref.shape[0]
    ahead = 2 * slabs * SUB
    planes = (rows1_ref.shape[0] - ahead) // (2 * NEAR)
    tables = []
    for slab in range(slabs):
        for c in range(2):
            at = (2 * slab + c) * SUB
            terms = [ref[slab, c] if len(ref.shape) == 4 else ref[at : at + SUB] for ref in refs[:-5]]
            while len(terms) > 1:
                terms = [a + b for a, b in zip(terms[::2], terms[1::2])]
            tables_ref[slab, c] = terms[0]
            tables.append(terms[0])
    for k in range(NEAR):
        for field in range(2):
            low = beside_rows(rows1_ref, rows2_ref, ahead + (field * planes + k) * NEAR)
            high = beside_rows(rows1_ref, rows2_ref, ahead + (field * planes + planes - NEAR + k) * NEAR)
            top = (field * NEAR + k) * SUB
            for at, a, b in zip((top + 1, top + HALO), low, high):
                first_ref[at : at + NEAR] = jnp.where(odd_s, a, b)
                second_ref[at : at + NEAR] = jnp.where(odd_s, b, a)
    for c in range(2):
        top = (2 * NEAR + c) * SUB
        low, high = tables[c], tables[2 * (slabs - 1) + c]
        first_ref[top : top + SUB] = jnp.where(odd_s, low, high)
        second_ref[top : top + SUB] = jnp.where(odd_s, high, low)


def joined(terms, rows):
    vmem = pl.BlockSpec(memory_space=pltpu.VMEM)
    packed = jax.ShapeDtypeStruct((2 * (NEAR + 1) * SUB, LANES), jnp.float32)
    outs = pl.pallas_call(
        join_kernel,
        in_specs=[vmem] * (len(terms) + 2),
        out_specs=[vmem] * 3,
        out_shape=[jax.ShapeDtypeStruct(terms[0].shape, jnp.float32), packed, packed],
        compiler_params=pltpu.CompilerParams(vmem_limit_bytes=8 * MIB),
        name="join",
    )(*terms, *rows)
    return outs[0], outs[1:]


def broadcast_table(slab_value):
    return [[jnp.broadcast_to(slab_value[c, g : g + 1], (SUB, LANES)) for g in range(SUB)] for c in range(2)]


def first_sweep(choice, tables, center, bend, permit, dopant, outside):
    electrons, holes = lookup(tables, choice)
    if outside is not None:
        electrons, holes = jnp.where(outside, 1.0, electrons), jnp.where(outside, 1.0, holes)
    mismatch = permit * bend - (dopant + holes - electrons)
    jacobian = 6.0 * permit + electrons + holes
    return electrons, holes, center - mismatch / jacobian


def outside_rows(r, span):
    e, _, ne, _ = position()
    row = lax.broadcasted_iota(jnp.int32, (SUB, LANES), 0)
    outside = None
    if r == 0:
        outside = (row < HALO) & (e == 0)
    if r == span - SUB:
        below = (row >= SUB - HALO) & (e == ne - 1)
        outside = below if outside is None else outside | below
    return outside


def lay_kernel(mesh_ref, old_ref, planes1_ref, planes2_ref, mesh_x, before_x, bend_x):
    e, s, ne, _ = position()
    odd_s = (s & 1) == 1
    planes, span, _ = mesh_x.shape
    own = span - 2 * HALO
    row0 = pl.multiple_of(e * own, SUB)
    up, mid, down = slice(0, HALO), slice(HALO, HALO + own), slice(HALO + own, span)
    up_b, mid_b, down_b = (slice(PAD + x.start, PAD + x.stop) for x in (up, mid, down))
    up_from = pl.multiple_of(jnp.maximum(row0 - SUB, 0), SUB)
    down_from = pl.multiple_of(jnp.minimum(row0 + own, mesh_ref.shape[1] - SUB), SUB)

    def lay(first, count, _):
        for k in range(count):
            p = first + k
            q = p + HALO
            mesh_x[p, mid] = mesh_ref[p, pl.ds(row0, own)]
            mesh_x[p, up] = mesh_ref[p, pl.ds(up_from, SUB)][SUB - HALO :]
            mesh_x[p, down] = mesh_ref[p, pl.ds(down_from, SUB)][:HALO]
            before_x[q, mid_b] = old_ref[p, pl.ds(row0, own)]
            before_x[q, up_b] = jnp.where(e > 0, old_ref[p, pl.ds(up_from, SUB)][SUB - HALO :], 0.0)
            before_x[q, down_b] = jnp.where(e < ne - 1, old_ref[p, pl.ds(down_from, SUB)][:HALO], 0.0)
        return _

    grouped(planes, LAY, lay, None)
    for k in range(HALO):
        at = (NEAR + k) * span
        a, b = planes1_ref[at : at + span], planes2_ref[at : at + span]
        before_x[k, PAD : PAD + span] = jnp.where(odd_s, a, b)
        before_x[HALO + planes + k, PAD : PAD + span] = jnp.where(odd_s, b, a)

    def bends(first, count, _):
        for r in range(0, span, SUB):
            at = PAD + r
            held = [before_x[HALO + first + k, at : at + SUB] for k in range(-1, count + 1)]
            for k in range(count):
                q = HALO + first + k
                neighbours = around(
                    held[k + 1], held[k], held[k + 2],
                    before_x[q, at - 1 : at - 1 + SUB], before_x[q, at + 1 : at + 1 + SUB],
                )
                bend_x[first + k, r : r + SUB] = 6.0 * held[k + 1] - neighbours
        return _

    grouped(planes, BLOCK, bends, None)


def laid(mesh, old, beyond, own):
    planes, _, lanes = mesh.shape
    cells = (planes, own + 2 * HALO, lanes)
    padded = (planes + 2 * HALO, own + 2 * HALO + 2 * PAD, lanes)
    vmem = pl.BlockSpec(memory_space=pltpu.VMEM)
    f32 = jnp.float32
    return pl.pallas_call(
        lay_kernel,
        in_specs=[vmem] * 4,
        out_specs=[vmem] * 3,
        out_shape=[jax.ShapeDtypeStruct(*x) for x in ((cells, jnp.int32), (padded, f32), (cells, f32))],
        compiler_params=pltpu.CompilerParams(vmem_limit_bytes=16 * MIB),
        cost_estimate=pl.CostEstimate(flops=0, bytes_accessed=LAY_COST, transcendentals=0),
        name="lay",
    )(mesh, old, *beyond)


def own_kernel(
    tables_ref, mesh_x, before_x, bend_x, regions_ref, dopant_ref, rows1_ref, rows2_ref,
    permit_x, dopant_x, electron_x, hole_x, now_x,
):
    planes, own, _ = regions_ref.shape
    slabs = tables_ref.shape[0]
    span = own + 2 * HALO
    up, mid, down = slice(HALO - NEAR, HALO), slice(HALO, HALO + own), slice(HALO + own, HALO + own + NEAR)
    for p in range(planes):
        permit_x[p, mid] = permittivity(regions_ref[p])
        dopant_x[p, mid] = dopant_ref[p]
        for field, field_x in ((0, permit_x), (1, dopant_x)):
            at = 2 * slabs * SUB + (field * planes + p) * NEAR
            field_x[p, up], field_x[p, down] = beside_rows(rows1_ref, rows2_ref, at)
    for slab in range(slabs):
        tables = broadcast_table(tables_ref[slab])

        def some(first, count, _, tables=tables, slab=slab):
            for r in range(0, span, SUB):
                at, rows = PAD + r, slice(r, r + SUB)
                for k in range(count):
                    p = slab * PL + first + k
                    electron_x[p, rows], hole_x[p, rows], now_x[p, rows] = first_sweep(
                        mesh_x[p, rows], tables, before_x[HALO + p, at : at + SUB], bend_x[p, rows],
                        permit_x[p, rows], dopant_x[p, rows], outside_rows(r, span),
                    )
            return _

        grouped(PL, LOOK, some, None)


def own_planes(tables, laid_out, regions, dopant, rows):
    vmem = pl.BlockSpec(memory_space=pltpu.VMEM)
    cells = laid_out[0].shape
    return pl.pallas_call(
        own_kernel,
        in_specs=[vmem] * 8,
        out_specs=[vmem] * 5,
        out_shape=[jax.ShapeDtypeStruct(cells, jnp.float32)] * 5,
        compiler_params=pltpu.CompilerParams(vmem_limit_bytes=16 * MIB),
        cost_estimate=pl.CostEstimate(flops=0, bytes_accessed=LAY_COST, transcendentals=0),
        name="own",
    )(tables, *laid_out, regions, dopant, *rows)


def sweep_kernel(
    packed1_ref, packed2_ref, planes1_ref, planes2_ref, before_x, permit_o, dopant_o, electron_o, hole_o, now_o,
    change_ref, most_ref, permit_x, dopant_x, electron_x, hole_x, now_s, next_s,
):
    _, s, _, ns = position()
    odd_s = (s & 1) == 1
    planes, own, _ = change_ref.shape
    span = own + 2 * HALO
    tops = range(0, span, SUB)

    def bring(first, count, _):
        for k in range(count):
            p = first + k
            q = HALO + p
            for r in tops:
                rows = slice(r, r + SUB)
                permit_x[q, rows] = permit_o[p, rows]
                dopant_x[q, rows] = dopant_o[p, rows]
                electron_x[q, rows] = electron_o[p, rows]
                hole_x[q, rows] = hole_o[p, rows]
                now_s[q, PAD + r : PAD + r + SUB] = now_o[p, rows]
        return _

    grouped(planes, LAY, bring, None)
    for low in (True, False):
        a, b = (packed1_ref, packed2_ref) if low else (packed2_ref, packed1_ref)
        c, d = (planes1_ref, planes2_ref) if low else (planes2_ref, planes1_ref)
        inside = s > 0 if low else s < ns - 1
        top = 2 * NEAR * SUB
        tables = [
            [
                jnp.where(
                    inside,
                    jnp.where(
                        odd_s,
                        jnp.broadcast_to(a[t + g : t + g + 1], (SUB, LANES)),
                        jnp.broadcast_to(b[t + g : t + g + 1], (SUB, LANES)),
                    ),
                    1.0,
                )
                for g in range(SUB)
            ]
            for t in (top, top + SUB)
        ]
        for k in range(NEAR):
            q = 1 + k if low else HALO + planes + k
            for field, field_x in ((0, permit_x), (1, dopant_x)):
                t = (field * NEAR + k) * SUB
                m = (NEAR + HALO) * span + (field * NEAR + k) * own
                field_x[q, :HALO] = jnp.where(odd_s, a[t : t + HALO], b[t : t + HALO])
                field_x[q, HALO : HALO + own] = jnp.where(odd_s, c[m : m + own], d[m : m + own])
                field_x[q, HALO + own :] = jnp.where(odd_s, a[t + HALO : t + SUB], b[t + HALO : t + SUB])
            for r in tops:
                at, rows = PAD + r, slice(r, r + SUB)
                here = slice(k * span + r, k * span + r + SUB)
                permit, dopant = permit_x[q, rows], dopant_x[q, rows]
                choice = jnp.where(odd_s, c[here], d[here]).astype(jnp.int32)
                center = before_x[q, at : at + SUB]
                neighbours = around(
                    center, before_x[q - 1, at : at + SUB], before_x[q + 1, at : at + SUB],
                    before_x[q, at - 1 : at - 1 + SUB], before_x[q, at + 1 : at + 1 + SUB],
                )
                electrons, holes, fresh = first_sweep(
                    choice, tables, center, 6.0 * center - neighbours, permit, dopant, outside_rows(r, span)
                )
                electron_x[q, rows] = electrons
                hole_x[q, rows] = holes
                now_s[q, at : at + SUB] = fresh

    source = now_s
    for sweep in range(1, SWEEPS):
        final = sweep == SWEEPS - 1
        target = next_s if source is now_s else now_s
        starts = range(HALO, HALO + own, SUB) if final else tops

        def step(first, count, most, sweep=sweep, source=source, target=target, starts=starts, final=final):
            for r in starts:
                rows = slice(r, r + SUB)
                at = PAD + r
                rows_b = slice(at, at + SUB)
                held = [source[1 + sweep + first + k, rows_b] for k in range(-1, count + 1)]
                for k in range(count):
                    q = 1 + sweep + first + k
                    center = held[k + 1]
                    neighbours = around(
                        center, held[k], held[k + 2],
                        source[q, at - 1 : at - 1 + SUB], source[q, at + 1 : at + 1 + SUB],
                    )
                    permit = permit_x[q, rows]
                    before = before_x[q, rows_b]
                    moved = center - before
                    electrons = electron_x[q, rows] * jnp.exp(moved)
                    holes = hole_x[q, rows] * jnp.exp(-moved)
                    mismatch = permit * (6.0 * center - neighbours) - (dopant_x[q, rows] + holes - electrons)
                    jacobian = 6.0 * permit + electrons + holes
                    fresh = center - mismatch / jacobian
                    if final:
                        change = fresh - before
                        change_ref[q - HALO, r - HALO : r - HALO + SUB] = change
                        most = jnp.maximum(most, jnp.abs(change))
                    else:
                        target[q, rows_b] = fresh
            return most

        most = grouped(planes + 2 * (SWEEPS - 1 - sweep), BLOCK, step, jnp.zeros((SUB, LANES), jnp.float32))
        if final:
            most_ref[...] = jnp.broadcast_to(jnp.max(most, axis=0, keepdims=True)[None], most_ref.shape)
        source = target


def swept(packed, beyond, fields, own):
    planes, span, lanes = fields[1].shape
    padded = fields[0].shape
    cells = (padded[0], span, lanes)
    vmem = pl.BlockSpec(memory_space=pltpu.VMEM)
    f32 = jnp.float32
    return pl.pallas_call(
        sweep_kernel,
        in_specs=[vmem] * 10,
        out_specs=[vmem, vmem],
        out_shape=[
            jax.ShapeDtypeStruct((planes, own, lanes), f32),
            jax.ShapeDtypeStruct((lax.axis_size(("energy", "space")), 1, lanes), f32),
        ],
        scratch_shapes=[pltpu.VMEM(cells, f32)] * 4 + [pltpu.VMEM(padded, f32)] * 2,
        compiler_params=pltpu.CompilerParams(vmem_limit_bytes=24 * MIB),
        name="sweeps",
    )(*packed, *beyond, *fields)


def settle_kernel(most_ref, old_ref, *rest):
    parts, out_ref, result, sems = rest[:-3], rest[-3], rest[-2], rest[-1]
    e = lax.axis_index("energy")
    planes, own, _ = parts[0].shape
    scale = 1.0 / (1.0 + jnp.max(most_ref[...]))
    size = planes // SETTLE
    copies = []
    for b in range(SETTLE):
        at = slice(b * size, (b + 1) * size)
        for k, part in enumerate(parts):
            rows = pl.ds(pl.multiple_of((e ^ k) * own, SUB), own)
            result[at, rows] = old_ref[at, rows] + part[at] * scale
        copies.append(pltpu.make_async_copy(result.at[at], out_ref.at[at], sems.at[b]))
        copies[-1].start()
    for copy in copies:
        copy.wait()


def settled(most, old, parts):
    vmem = pl.BlockSpec(memory_space=pltpu.VMEM)
    return pl.pallas_call(
        settle_kernel,
        in_specs=[vmem] * (2 + len(parts)),
        out_specs=pl.BlockSpec(memory_space=pl.ANY),
        out_shape=jax.ShapeDtypeStruct(old.shape, jnp.float32),
        scratch_shapes=[pltpu.VMEM(old.shape, jnp.float32), pltpu.SemaphoreType.DMA((SETTLE,))],
        compiler_params=pltpu.CompilerParams(vmem_limit_bytes=16 * MIB),
        name="settle",
    )(most, old, *parts)


def pairs(axis, odd_first):
    count = lax.axis_size(axis)
    out = []
    for low in range(1 if odd_first else 0, count - 1, 2):
        out += [(low, low + 1), (low + 1, low)]
    return out


def toggled(x, axis, mask):
    return lax.ppermute(x, axis, [(i, i ^ mask) for i in range(lax.axis_size(axis))])


def on_device(green_blocks, injection, mesh_state_choice, regions, dopant_charge_field, earlier_voltage):
    ne = lax.axis_size("energy")
    own = regions.shape[1]
    green, inject = green_blocks[0], injection[0]

    def exchanged(sent, axis):
        return [lax.ppermute(x, axis, pairs(axis, odd_first)) for x, odd_first in zip(sent, (False, True))]

    rows, beyond = edges(regions, dopant_charge_field, mesh_state_choice, earlier_voltage, green, inject)
    beyond = exchanged(beyond, "space")
    tables, packed1, packed2 = orbital_table(green, inject, rows)
    (tables, packed1, packed2), beyond = lax.optimization_barrier(((tables, packed1, packed2), beyond))
    second = [k for k in range(3, ne) if k & (k + 1) == 0]
    terms = [tables]
    for k in range(1, ne):
        sent = packed1 if k == 1 else packed2 if k in second else tables
        terms.append(toggled(sent, "energy", k))
    e = lax.axis_index("energy")
    partner = jnp.where(e & 1 == 1, e + 1, e - 1)
    rows = [terms[1], terms[3]]
    for k in second[1:]:
        rows[1] = jnp.where(e ^ partner == k, terms[k], rows[1])
    laid_out = laid(mesh_state_choice, earlier_voltage, beyond, own)
    terms, laid_out = lax.optimization_barrier((terms, laid_out))
    tables, packed = joined(terms, rows)
    packed = exchanged(packed, "space")
    fields = own_planes(tables, laid_out, regions, dopant_charge_field, rows)
    change, most = swept(packed, beyond, (laid_out[1], *fields), own)
    parts = {0: change}
    for k in range(2, ne, 2):
        parts[k] = toggled(change, "energy", k)
    parts[1] = toggled(change, "energy", 1)
    most = lax.all_to_all(most, ("energy", "space"), 0, 0)
    far = [parts[k] for k in range(2, ne, 2)]
    most, far = lax.optimization_barrier((most, far))
    for k, part in zip(range(2, ne, 2), far):
        parts[k ^ 1] = toggled(part, "energy", 1)
    return settled(most, earlier_voltage, [parts[k] for k in range(ne)])


def solution(mesh):
    placed = (
        P("energy", "space", None, None, None),
        P("energy", "space", None, None),
        P("space", None, None),
        P("space", "energy", None),
        P("space", "energy", None),
        P("space", None, None),
    )
    return jax.shard_map(
        on_device, mesh=mesh, in_specs=placed, out_specs=P("space", None, None), check_vma=False
    )
```

time: 48.8 us -> 43.7 us (0.90)
  local copies, waits for them, and re-layouts: 5.01 us -> 0.85 us
  starting transfers between devices: 23.8 us -> 20.1 us
  waiting for transfers between devices: 9.26 us -> 11.8 us
    unnamed x16 -> x12, local copies, waits for them, and re-layouts: 5.01 us -> 0.85 us
    ppermute x6, waiting for transfers between devices: 1.54 us -> 5.06 us  [toggled(): lax.ppermute(x, axis, [(i, i ^ mask) for i in range(lax.axis_size(axis))])]
    ppermute x6 -> x4, starting transfers between devices: 10.3 us -> 7.1 us  [exchanged(): lax.ppermute(x, axis, pairs(axis, odd_first))]
    ppermute x6, starting transfers between devices: 7.74 us -> 5.15 us  [toggled(): lax.ppermute(x, axis, [(i, i ^ mask) for i in range(lax.axis_size(axis))])]
    all_to_all x1, starting transfers between devices: 5.78 us -> 7.85 us  [on_device(): most = lax.all_to_all(most, ('energy', 'space'), 0, 0)]
    ppermute x6 -> x4, waiting for transfers between devices: 1 us -> 0.01 us  [exchanged(): lax.ppermute(x, axis, pairs(axis, odd_first))]
    pallas_call x5 -> x6, Pallas kernels: 9.21 us -> 9.51 us  [the longest x1 3.04 us: orbital_table(): pl.pallas_call(table_kernel, in_specs=[vmem] * 4, out_specs=[vmem] * 3, o...]
  transfers between devices with their start and end apart: 13 -> 11, of which waited for: 5 -> 3; matrix products, arithmetic and copies ran while one was open for 0% -> 0% of each run, Pallas kernels for 2% -> 13%
where the time goes in v3:
time: 43.7 us; the launch traced here: 43.6 us
  starting transfers between devices  20.1 us (46%)
  waiting for transfers between devices  11.8 us (27%)
  Pallas kernels  10.7 us (24%)
  local copies, waits for them, and re-layouts  0.85 us (2%)
    all_to_all x1, starting transfers between devices, on_device(): most = lax.all_to_all(most, ('energy', 'space'), 0, 0)  7.85 us
    ppermute x4, starting transfers between devices, exchanged(): lax.ppermute(x, axis, pairs(axis, odd_first))  7.1 us
    all_to_all x1, waiting for transfers between devices, on_device(): most = lax.all_to_all(most, ('energy', 'space'), 0, 0)  6.72 us
    ppermute x6, starting transfers between devices, toggled(): lax.ppermute(x, axis, [(i, i ^ mask) for i in range(lax.axis_size(axis))])  5.15 us
    ppermute x6, waiting for transfers between devices, toggled(): lax.ppermute(x, axis, [(i, i ^ mask) for i in range(lax.axis_size(axis))])  5.06 us
    pallas_call x1, Pallas kernels, orbital_table(): pl.pallas_call(table_kernel, in_specs=[vmem] * 4, out_specs=[vmem] * 3, o...  3.04 us
    pallas_call x1, Pallas kernels, swept(): pl.pallas_call(sweep_kernel, in_specs=[vmem] * 10, out_specs=[vmem, vmem]...  2.57 us
    pallas_call x1, Pallas kernels, own_planes(): pl.pallas_call(own_kernel, in_specs=[vmem] * 8, out_specs=[vmem] * 5, out...  2.01 us
  transfers between devices with their start and end apart: 11, of which 3 were waited for; matrix products, arithmetic and copies ran while one was open for 0% of the time, Pallas kernels for 13%

profile of v3, /device:TPU:0, one launch (start us, length us, event | category | flops | bytes accessed | tf_op | source)
XLA Modules:
  0.0 43.6 jit_solution(15313417600432198075)
XLA Ops:
  0.0 0.0 copy-start.5
  0.0 0.0 copy-start
  0.0 0.0 copy-start.1
  0.0 0.0 copy-start.2
  0.0 0.0 copy-start.3
  0.0 0.0 copy-start.4
  0.0 1.4 %edges.1 = (f32[192,128]{1,0:T(8,128)S(1)}, f32[192,128]{1,0:T(8,128)S(1)}, f32[264,128]{1,0:T(8,128)S(1)}, f32[264,128]{1,0:T(8,128)S(1)}) custom-call(s32[32,16,128]{2,1,0:T(8,128)} %regions_ref.3, f32[32,16,128]{2,1,0:T(8,128)} %dopant_ref.3, s32[32,64,128]{2,1,0:T(8,128)} %mesh_ref.3, f32[32,64,128]{2,1,0:T(8,128)} %old_ref.5, ...), custom_call_target="tpu_custom_call" | custom-call | bytes 10485760 | tf_op jit(solution)/shard_map/edges/pallas_call | solution.py:204
  1.4 3.0 %collective-permute-start = (f32[264,128]{1,0:T(8,128)S(1)}, f32[264,128]{1,0:T(8,128)S(1)}, u32[]{:S(2)}, u32[]{:S(2)}) collective-permute-start(f32[264,128]{1,0:T(8,128)S(1)} %get-tuple-element.44), channel_id=1, source_target_pairs={{0,1},{1,0},{2,3},{3,2},{4,5},{5,4},{6,7},{7,6},{8,9},{9,8},{10,11... | collective-permute-start | bytes 405512 | tf_op jit(solution)/shard_map/ppermute | solution.py:588
  4.5 0.8 %collective-permute-start.1 = (f32[264,128]{1,0:T(8,128)S(1)}, f32[264,128]{1,0:T(8,128)S(1)}, u32[]{:S(2)}, u32[]{:S(2)}) collective-permute-start(f32[264,128]{1,0:T(8,128)S(1)} %get-tuple-element.45), channel_id=1, source_target_pairs={{1,2},{2,1},{3,4},{4,3},{5,6},{6,5},{9,10},{10,9},{11,12},{12,11},... | collective-permute-start | bytes 405512 | tf_op jit(solution)/shard_map/ppermute | solution.py:588
  5.3 0.0 copy-done.5
  5.3 0.8 %copy-done = f32[1,2,2,1024,1024]{4,3,2,1,0:T(8,128)S(1)} copy-done((f32[1,2,2,1024,1024]{4,3,2,1,0:T(8,128)S(1)}, f32[1,2,2,1024,1024]{4,3,2,1,0:T(8,128)}, u32[]{:S(2)}) %copy-start) | copy-done | bytes 16777240
  6.1 3.0 %table.1 = (f32[2,2,8,128]{3,2,1,0:T(8,128)S(1)}, f32[224,128]{1,0:T(8,128)S(1)}, f32[224,128]{1,0:T(8,128)S(1)}) custom-call(f32[2,2,1024,1024]{3,2,1,0:T(8,128)S(1)} %bitcast.3, f32[2,2,1024]{2,1,0:T(2,128)S(1)} %bitcast.5, f32[192,128]{1,0:T(8,128)S(1)} %get-tuple-element.39.rows1_ref, f32[192,128]{1,0:T(8,128)S(1)} %get-tuple-element.40.rows2_ref), custom_call_target="tpu_custom_call" | custom-call | bytes 10485760 | tf_op jit(solution)/shard_map/table/pallas_call | solution.py:100
  9.1 0.0 collective-permute-done.planes1_ref
  9.1 0.0 collective-permute-done.1.planes2_ref
  9.1 0.5 %collective-permute-start.2 = (f32[224,128]{1,0:T(8,128)S(1)}, f32[224,128]{1,0:T(8,128)S(1)}, u32[]{:S(2)}, u32[]{:S(2)}) collective-permute-start(f32[224,128]{1,0:T(8,128)S(1)} %get-tuple-element.47), channel_id=1, source_target_pairs={{0,8},{8,0},{16,24},{24,16},{1,9},{9,1},{17,25},{25,17},{2,10},{10... | collective-permute-start | bytes 344072 | tf_op jit(solution)/shard_map/ppermute | solution.py:579
  9.7 2.6 %collective-permute-start.4 = (f32[224,128]{1,0:T(8,128)S(1)}, f32[224,128]{1,0:T(8,128)S(1)}, u32[]{:S(2)}, u32[]{:S(2)}) collective-permute-start(f32[224,128]{1,0:T(8,128)S(1)} %get-tuple-element.48), channel_id=1, source_target_pairs={{0,24},{8,16},{16,8},{24,0},{1,25},{9,17},{17,9},{25,1},{2,26},{10... | collective-permute-start | bytes 344072 | tf_op jit(solution)/shard_map/ppermute | solution.py:579
  12.3 0.0 collective-permute-start.3
  12.3 0.0 copy-done.1
  12.3 0.0 copy-done.2
  12.3 0.5 %lay.1 = (s32[32,24,128]{2,1,0:T(8,128)S(1)}, f32[40,40,128]{2,1,0:T(8,128)S(1)}, f32[32,24,128]{2,1,0:T(8,128)S(1)}) custom-call(s32[32,64,128]{2,1,0:T(8,128)S(1)} %copy-done.2, f32[32,64,128]{2,1,0:T(8,128)S(1)} %copy-done.1, f32[264,128]{1,0:T(8,128)S(1)} %collective-permute-done.planes1_ref, f32[264,128]{1,0:T(8,128)S(1)} %collective-permute-done.1.planes2_ref), custom_call_target="tpu_custom_call" | custom-call | bytes 3145728 | tf_op jit(solution)/shard_map/lay/pallas_call | solution.py:353
  12.8 3.5 %collective-permute-done.3.refs_2_ = f32[2,2,8,128]{3,2,1,0:T(8,128)S(1)} collective-permute-done((f32[2,2,8,128]{3,2,1,0:T(8,128)S(1)}, f32[2,2,8,128]{3,2,1,0:T(8,128)S(1)}, u32[]{:S(2)}, u32[]{:S(2)}) %collective-permute-start.3) | collective-permute-done | bytes 16416 | tf_op jit(solution)/shard_map/ppermute | solution.py:579
  16.3 0.0 collective-permute-done.2.refs_1_.refs_4_.rows1_ref
  16.3 0.0 collective-permute-done.4.refs_3_.refs_5_.rows2_ref
  16.4 2.6 %collective-permute-start.5 = (f32[64,128]{1,0:T(8,128)S(1)}, f32[64,128]{1,0:T(8,128)S(1)}, u32[]{:S(2)}, u32[]{:S(2)}) collective-permute-start(f32[64,128]{1,0:T(8,128)S(1)} %get-tuple-element.58), channel_id=1, source_target_pairs={{0,1},{1,0},{2,3},{3,2},{4,5},{5,4},{6,7},{7,6},{8,9},{9,8},{10,11... | collective-permute-start | bytes 98312 | tf_op jit(solution)/shard_map/ppermute | solution.py:588
  19.0 0.7 %collective-permute-start.6 = (f32[64,128]{1,0:T(8,128)S(1)}, f32[64,128]{1,0:T(8,128)S(1)}, u32[]{:S(2)}, u32[]{:S(2)}) collective-permute-start(f32[64,128]{1,0:T(8,128)S(1)} %get-tuple-element.59), channel_id=1, source_target_pairs={{1,2},{2,1},{3,4},{4,3},{5,6},{6,5},{9,10},{10,9},{11,12},{12,11},... | collective-permute-start | bytes 98312 | tf_op jit(solution)/shard_map/ppermute | solution.py:588
  19.7 0.0 copy-done.3
  19.7 0.0 copy-done.4
  19.7 2.0 %own.1 = (f32[32,24,128]{2,1,0:T(8,128)S(1)}, f32[32,24,128]{2,1,0:T(8,128)S(1)}, f32[32,24,128]{2,1,0:T(8,128)S(1)}, f32[32,24,128]{2,1,0:T(8,128)S(1)}, f32[32,24,128]{2,1,0:T(8,128)S(1)}) custom-call(f32[2,2,8,128]{3,2,1,0:T(8,128)S(1)} %get-tuple-element.61.tables_ref, s32[32,24,128]{2,1,0:T(8,128)S(1)} %get-tuple-element.62.mesh_x, ...), custom_call_target="tpu_custom_call" | custom-call | bytes 3145728 | tf_op jit(solution)/shard_map/own/pallas_call | solution.py:398
  21.7 0.0 collective-permute-done.5.packed1_ref
  21.7 0.0 collective-permute-done.6.packed2_ref
  21.7 2.6 %sweeps.1 = (f32[32,16,128]{2,1,0:T(8,128)S(1)}, f32[32,1,128]{2,1,0:T(1,128)}) custom-call(f32[64,128]{1,0:T(8,128)S(1)} %collective-permute-done.5.packed1_ref, f32[64,128]{1,0:T(8,128)S(1)} %collective-permute-done.6.packed2_ref, f32[264,128]{1,0:T(8,128)S(1)} %collective-permute-done.planes1_ref, f32[264,128]{1,0:T(8,128)S(1)} %collective-permute-done.1.planes2_ref, ...), custom_call_target="tpu_custom_call" | custom-call | tf_op jit(solution)/shard_map/sweeps/pallas_call | solution.py:525
  24.3 1.6 %collective-permute-start.7 = (f32[32,16,128]{2,1,0:T(8,128)S(1)}, f32[32,16,128]{2,1,0:T(8,128)S(1)}, u32[]{:S(2)}, u32[]{:S(2)}) collective-permute-start(f32[32,16,128]{2,1,0:T(8,128)S(1)} %get-tuple-element.70.rest_0_), channel_id=1, source_target_pairs={{0,16},{8,24},{16,0},{24,8},{1,17},{9,25},{17,1},{25,9},{2,18},{10... | collective-permute-start | bytes 786440 | tf_op jit(solution)/shard_map/ppermute | solution.py:579
  25.9 7.8 %all-to-all-start = ((f32[32,1,128]{2,1,0:T(1,128)}), f32[32,1,128]{2,1,0:T(1,128)S(1)}, u32[]{:S(2)}, u32[]{:S(2)}) async-start(f32[32,1,128]{2,1,0:T(1,128)} %get-tuple-element.69), calls=%async_computation | async-start | bytes 32768 | tf_op jit(solution)/shard_map/all_to_all | solution.py:614
  33.8 0.3 collective-permute-start.8
  34.1 6.7 %all-to-all-done.most_ref = f32[32,1,128]{2,1,0:T(1,128)S(1)} async-done(((f32[32,1,128]{2,1,0:T(1,128)}), f32[32,1,128]{2,1,0:T(1,128)S(1)}, u32[]{:S(2)}, u32[]{:S(2)}) %all-to-all-start) | async-done | bytes 16416 | tf_op jit(solution)/shard_map/all_to_all | solution.py:614
  40.8 0.0 collective-permute-done.7.rest_2_
  40.8 0.0 collective-permute-start.9
  40.8 0.0 collective-permute-done.8.rest_1_
  40.8 1.5 %collective-permute-done.9.rest_3_ = f32[32,16,128]{2,1,0:T(8,128)S(1)} collective-permute-done((f32[32,16,128]{2,1,0:T(8,128)S(1)}, f32[32,16,128]{2,1,0:T(8,128)S(1)}, u32[]{:S(2)}, u32[]{:S(2)}) %collective-permute-start.9) | collective-permute-done | bytes 262176 | tf_op jit(solution)/shard_map/ppermute | solution.py:579
  42.4 1.2 %settle.1 = f32[32,64,128]{2,1,0:T(8,128)} custom-call(f32[32,1,128]{2,1,0:T(1,128)S(1)} %all-to-all-done.most_ref, f32[32,64,128]{2,1,0:T(8,128)S(1)} %copy-done.1, f32[32,16,128]{2,1,0:T(8,128)S(1)} %get-tuple-element.70.rest_0_, f32[32,16,128]{2,1,0:T(8,128)S(1)} %collective-permute-done.8.rest_1_, f32[32,16,128]{2,1,0:T(8,128)S(1)} %collective-permute-done.7.rest_2_, ...), custom_call_target="tpu_custom_call" | custom-call | tf_op jit(solution)/shard_map/settle/pallas_call | solution.py:559
  (1 shorter events, 0.0 us)
Async XLA Ops:
  0.0 5.3 %copy-start.5 = (f32[1,2,2,1024]{3,2,1,0:T(2,128)S(1)}, f32[1,2,2,1024]{3,2,1,0:T(2,128)}, u32[]{:S(2)}) copy-start(f32[1,2,2,1024]{3,2,1,0:T(2,128)} %param.7) | copy-start | bytes 49156
  0.0 6.1 %copy-start = (f32[1,2,2,1024,1024]{4,3,2,1,0:T(8,128)S(1)}, f32[1,2,2,1024,1024]{4,3,2,1,0:T(8,128)}, u32[]{:S(2)}) copy-start(f32[1,2,2,1024,1024]{4,3,2,1,0:T(8,128)} %param.6) | copy-start | bytes 50331652
  0.0 12.3 %copy-start.1 = (f32[32,64,128]{2,1,0:T(8,128)S(1)}, f32[32,64,128]{2,1,0:T(8,128)}, u32[]{:S(2)}) copy-start(f32[32,64,128]{2,1,0:T(8,128)} %old_ref.5) | copy-start | bytes 3145732
  0.0 12.3 %copy-start.2 = (s32[32,64,128]{2,1,0:T(8,128)S(1)}, s32[32,64,128]{2,1,0:T(8,128)}, u32[]{:S(2)}) copy-start(s32[32,64,128]{2,1,0:T(8,128)} %mesh_ref.3) | copy-start | bytes 3145732
  0.0 19.7 %copy-start.3 = (s32[32,16,128]{2,1,0:T(8,128)S(1)}, s32[32,16,128]{2,1,0:T(8,128)}, u32[]{:S(2)}) copy-start(s32[32,16,128]{2,1,0:T(8,128)} %regions_ref.3) | copy-start | bytes 786436
  0.0 19.7 %copy-start.4 = (f32[32,16,128]{2,1,0:T(8,128)S(1)}, f32[32,16,128]{2,1,0:T(8,128)}, u32[]{:S(2)}) copy-start(f32[32,16,128]{2,1,0:T(8,128)} %dopant_ref.3) | copy-start | bytes 786436
  1.4 7.7 %collective-permute-start = (f32[264,128]{1,0:T(8,128)S(1)}, f32[264,128]{1,0:T(8,128)S(1)}, u32[]{:S(2)}, u32[]{:S(2)}) collective-permute-start(f32[264,128]{1,0:T(8,128)S(1)} %get-tuple-element.44), channel_id=1, source_target_pairs={{0,1},{1,0},{2,3},{3,2},{4,5},{5,4},{6,7},{7,6},{8,9},{9,8},{10,11... | collective-permute-start | bytes 405512 | tf_op jit(solution)/shard_map/ppermute | solution.py:588
  4.5 4.7 %collective-permute-start.1 = (f32[264,128]{1,0:T(8,128)S(1)}, f32[264,128]{1,0:T(8,128)S(1)}, u32[]{:S(2)}, u32[]{:S(2)}) collective-permute-start(f32[264,128]{1,0:T(8,128)S(1)} %get-tuple-element.45), channel_id=1, source_target_pairs={{1,2},{2,1},{3,4},{4,3},{5,6},{6,5},{9,10},{10,9},{11,12},{12,11},... | collective-permute-start | bytes 405512 | tf_op jit(solution)/shard_map/ppermute | solution.py:588
  9.1 7.2 %collective-permute-start.2 = (f32[224,128]{1,0:T(8,128)S(1)}, f32[224,128]{1,0:T(8,128)S(1)}, u32[]{:S(2)}, u32[]{:S(2)}) collective-permute-start(f32[224,128]{1,0:T(8,128)S(1)} %get-tuple-element.47), channel_id=1, source_target_pairs={{0,8},{8,0},{16,24},{24,16},{1,9},{9,1},{17,25},{25,17},{2,10},{10... | collective-permute-start | bytes 344072 | tf_op jit(solution)/shard_map/ppermute | solution.py:579
  9.7 6.7 %collective-permute-start.4 = (f32[224,128]{1,0:T(8,128)S(1)}, f32[224,128]{1,0:T(8,128)S(1)}, u32[]{:S(2)}, u32[]{:S(2)}) collective-permute-start(f32[224,128]{1,0:T(8,128)S(1)} %get-tuple-element.48), channel_id=1, source_target_pairs={{0,24},{8,16},{16,8},{24,0},{1,25},{9,17},{17,9},{25,1},{2,26},{10... | collective-permute-start | bytes 344072 | tf_op jit(solution)/shard_map/ppermute | solution.py:579
  12.3 4.0 %collective-permute-start.3 = (f32[2,2,8,128]{3,2,1,0:T(8,128)S(1)}, f32[2,2,8,128]{3,2,1,0:T(8,128)S(1)}, u32[]{:S(2)}, u32[]{:S(2)}) collective-permute-start(f32[2,2,8,128]{3,2,1,0:T(8,128)S(1)} %get-tuple-element.54.refs_0_), channel_id=1, source_target_pairs={{0,16},{8,24},{16,0},{24,8},{1,17},{9,25},{17,1},{25,9},{2,18},{10... | collective-permute-start | bytes 49160 | tf_op jit(solution)/shard_map/ppermute | solution.py:579
  16.4 5.3 %collective-permute-start.5 = (f32[64,128]{1,0:T(8,128)S(1)}, f32[64,128]{1,0:T(8,128)S(1)}, u32[]{:S(2)}, u32[]{:S(2)}) collective-permute-start(f32[64,128]{1,0:T(8,128)S(1)} %get-tuple-element.58), channel_id=1, source_target_pairs={{0,1},{1,0},{2,3},{3,2},{4,5},{5,4},{6,7},{7,6},{8,9},{9,8},{10,11... | collective-permute-start | bytes 98312 | tf_op jit(solution)/shard_map/ppermute | solution.py:588
  19.0 2.7 %collective-permute-start.6 = (f32[64,128]{1,0:T(8,128)S(1)}, f32[64,128]{1,0:T(8,128)S(1)}, u32[]{:S(2)}, u32[]{:S(2)}) collective-permute-start(f32[64,128]{1,0:T(8,128)S(1)} %get-tuple-element.59), channel_id=1, source_target_pairs={{1,2},{2,1},{3,4},{4,3},{5,6},{6,5},{9,10},{10,9},{11,12},{12,11},... | collective-permute-start | bytes 98312 | tf_op jit(solution)/shard_map/ppermute | solution.py:588
  24.3 16.5 %collective-permute-start.7 = (f32[32,16,128]{2,1,0:T(8,128)S(1)}, f32[32,16,128]{2,1,0:T(8,128)S(1)}, u32[]{:S(2)}, u32[]{:S(2)}) collective-permute-start(f32[32,16,128]{2,1,0:T(8,128)S(1)} %get-tuple-element.70.rest_0_), channel_id=1, source_target_pairs={{0,16},{8,24},{16,0},{24,8},{1,17},{9,25},{17,1},{25,9},{2,18},{10... | collective-permute-start | bytes 786440 | tf_op jit(solution)/shard_map/ppermute | solution.py:579
  25.9 14.9 %all-to-all-start = ((f32[32,1,128]{2,1,0:T(1,128)}), f32[32,1,128]{2,1,0:T(1,128)S(1)}, u32[]{:S(2)}, u32[]{:S(2)}) async-start(f32[32,1,128]{2,1,0:T(1,128)} %get-tuple-element.69), calls=%async_computation | async-start | bytes 32768 | tf_op jit(solution)/shard_map/all_to_all | solution.py:614
  33.8 7.0 %collective-permute-start.8 = (f32[32,16,128]{2,1,0:T(8,128)S(1)}, f32[32,16,128]{2,1,0:T(8,128)S(1)}, u32[]{:S(2)}, u32[]{:S(2)}) collective-permute-start(f32[32,16,128]{2,1,0:T(8,128)S(1)} %get-tuple-element.70.rest_0_), channel_id=1, source_target_pairs={{0,8},{8,0},{16,24},{24,16},{1,9},{9,1},{17,25},{25,17},{2,10},{10... | collective-permute-start | bytes 786440 | tf_op jit(solution)/shard_map/ppermute | solution.py:579
  40.8 1.5 %collective-permute-start.9 = (f32[32,16,128]{2,1,0:T(8,128)S(1)}, f32[32,16,128]{2,1,0:T(8,128)S(1)}, u32[]{:S(2)}, u32[]{:S(2)}) collective-permute-start(f32[32,16,128]{2,1,0:T(8,128)S(1)} %collective-permute-done.7.rest_2_), channel_id=1, source_target_pairs={{0,8},{8,0},{16,24},{24,16},{1,9},{9,1},{17,25},{25,17},{2,10},{10... | collective-permute-start | bytes 786440 | tf_op jit(solution)/shard_map/ppermute | solution.py:579

commit v4 on v3

--- a/solution.py
+++ b/solution.py
@@ -14,15 +14,15 @@
 LANES = 128
 SUB = 8
 MIB = 1 << 20
-BLOCK = 16
+BLOCK = 32
 LOOK = 16
 LAY = 16
-SETTLE = 4
+SETTLE = 2
 EDGE_COST = 10 * MIB
 TABLE_COST = 10 * MIB
 LAY_COST = 3 * MIB
 LATER = pl.ANY
-PAIRS = 16
+PAIRS = 64
 
 
 def merge(parts, width):
@@ -536,35 +536,64 @@
     )(*packed, *beyond, *fields)
 
 
-def settle_kernel(most_ref, old_ref, *rest):
-    parts, out_ref, result, sems = rest[:-3], rest[-3], rest[-2], rest[-1]
+def write_rows(out_ref, result, sems, old_ref, parts, masks, scale):
     e = lax.axis_index("energy")
     planes, own, _ = parts[0].shape
-    scale = 1.0 / (1.0 + jnp.max(most_ref[...]))
     size = planes // SETTLE
     copies = []
     for b in range(SETTLE):
         at = slice(b * size, (b + 1) * size)
-        for k, part in enumerate(parts):
-            rows = pl.ds(pl.multiple_of((e ^ k) * own, SUB), own)
-            result[at, rows] = old_ref[at, rows] + part[at] * scale
-        copies.append(pltpu.make_async_copy(result.at[at], out_ref.at[at], sems.at[b]))
-        copies[-1].start()
+        for k, (mask, part) in enumerate(zip(masks, parts)):
+            rows = pl.ds(pl.multiple_of((e ^ mask) * own, SUB), own)
+            result[k, at] = old_ref[at, rows] + part[at] * scale
+            copies.append(pltpu.make_async_copy(result.at[k, at], out_ref.at[at, rows], sems.at[b, k]))
+            copies[-1].start()
     for copy in copies:
         copy.wait()
 
 
-def settled(most, old, parts):
-    vmem = pl.BlockSpec(memory_space=pltpu.VMEM)
+def settle_kernel(most_ref, old_ref, *rest, masks):
+    parts, (out_ref, scale_ref, result, sems) = rest[:-4], rest[-4:]
+    scale = 1.0 / (1.0 + jnp.max(most_ref[...]))
+    scale_ref[...] = jnp.full(scale_ref.shape, scale)
+    write_rows(out_ref, result, sems, old_ref, parts, masks, scale)
+
+
+def settle_more_kernel(scale_ref, old_ref, *rest, masks):
+    parts, (_, out_ref, result, sems) = rest[:-4], rest[-4:]
+    write_rows(out_ref, result, sems, old_ref, parts, masks, scale_ref[0:1][None])
+
+
+def settled(most, old, parts, late):
+    vmem, anywhere = pl.BlockSpec(memory_space=pltpu.VMEM), pl.BlockSpec(memory_space=pl.ANY)
+    whole = jax.ShapeDtypeStruct(old.shape, jnp.float32)
+
+    def scratch(count):
+        return [
+            pltpu.VMEM((count,) + parts[0].shape, jnp.float32),
+            pltpu.SemaphoreType.DMA((SETTLE, count)),
+        ]
+
+    out, scale = pl.pallas_call(
+        functools.partial(settle_kernel, masks=tuple(parts)),
+        in_specs=[vmem] * (2 + len(parts)),
+        out_specs=[anywhere, vmem],
+        out_shape=[whole, jax.ShapeDtypeStruct((SUB, LANES), jnp.float32)],
+        scratch_shapes=scratch(len(parts)),
+        compiler_params=pltpu.CompilerParams(vmem_limit_bytes=16 * MIB),
+        cost_estimate=pl.CostEstimate(flops=0, bytes_accessed=LAY_COST, transcendentals=0),
+        name="settle",
+    )(most, old, *parts.values())
     return pl.pallas_call(
-        settle_kernel,
-        in_specs=[vmem] * (2 + len(parts)),
-        out_specs=pl.BlockSpec(memory_space=pl.ANY),
-        out_shape=jax.ShapeDtypeStruct(old.shape, jnp.float32),
-        scratch_shapes=[pltpu.VMEM(old.shape, jnp.float32), pltpu.SemaphoreType.DMA((SETTLE,))],
+        functools.partial(settle_more_kernel, masks=tuple(late)),
+        in_specs=[vmem] * (2 + len(late)) + [anywhere],
+        out_specs=anywhere,
+        out_shape=whole,
+        input_output_aliases={2 + len(late): 0},
+        scratch_shapes=scratch(len(late)),
         compiler_params=pltpu.CompilerParams(vmem_limit_bytes=16 * MIB),
-        name="settle",
-    )(most, old, *parts)
+        name="settle_more",
+    )(scale, old, *late.values(), out)
 
 
 def pairs(axis, odd_first):
@@ -590,11 +619,11 @@
     rows, beyond = edges(regions, dopant_charge_field, mesh_state_choice, earlier_voltage, green, inject)
     beyond = exchanged(beyond, "space")
     tables, packed1, packed2 = orbital_table(green, inject, rows)
-    (tables, packed1, packed2), beyond = lax.optimization_barrier(((tables, packed1, packed2), beyond))
+    alone, beyond = lax.optimization_barrier((tables, beyond))
     second = [k for k in range(3, ne) if k & (k + 1) == 0]
     terms = [tables]
     for k in range(1, ne):
-        sent = packed1 if k == 1 else packed2 if k in second else tables
+        sent = packed1 if k == 1 else packed2 if k in second else alone
         terms.append(toggled(sent, "energy", k))
     e = lax.axis_index("energy")
     partner = jnp.where(e & 1 == 1, e + 1, e - 1)
@@ -607,7 +636,7 @@
     packed = exchanged(packed, "space")
     fields = own_planes(tables, laid_out, regions, dopant_charge_field, rows)
     change, most = swept(packed, beyond, (laid_out[1], *fields), own)
-    parts = {0: change}
+    parts, late = {0: change}, {}
     for k in range(2, ne, 2):
         parts[k] = toggled(change, "energy", k)
     parts[1] = toggled(change, "energy", 1)
@@ -615,8 +644,8 @@
     far = [parts[k] for k in range(2, ne, 2)]
     most, far = lax.optimization_barrier((most, far))
     for k, part in zip(range(2, ne, 2), far):
-        parts[k ^ 1] = toggled(part, "energy", 1)
-    return settled(most, earlier_voltage, [parts[k] for k in range(ne)])
+        late[k ^ 1] = toggled(part, "energy", 1)
+    return settled(most, earlier_voltage, parts, late)
 
 
 def solution(mesh):

time: 43.7 us -> 41.5 us (0.950)
  waiting for transfers between devices: 11.8 us -> 10.7 us
  starting transfers between devices: 20.1 us -> 19.1 us
    ppermute x6, waiting for transfers between devices: 5.06 us -> 4.01 us  [toggled(): lax.ppermute(x, axis, [(i, i ^ mask) for i in range(lax.axis_size(axis))])]
    pallas_call x1 -> x2, Pallas kernels: 1.19 us -> 1.85 us  [the longest x1 1.11 us: settled(): pl.pallas_call(functools.partial(settle_kernel, masks=tuple(parts)), in_s...]
    pallas_call x1, Pallas kernels: 3.04 us -> 2.44 us  [orbital_table(): pl.pallas_call(table_kernel, in_specs=[vmem] * 4, out_specs=[vmem] * 3, o...]
    all_to_all x1, starting transfers between devices: 7.85 us -> 7.28 us  [on_device(): most = lax.all_to_all(most, ('energy', 'space'), 0, 0)]
  transfers between devices with their start and end apart: 11 -> 11, of which waited for: 3 -> 4; matrix products, arithmetic and copies ran while one was open for 0% -> 0% of each run, Pallas kernels for 13% -> 14%
where the time goes in v4:
time: 41.5 us; the launch traced here: 41.3 us
  starting transfers between devices  19.1 us (46%)
  waiting for transfers between devices  10.7 us (26%)
  Pallas kernels  10.5 us (25%)
  local copies, waits for them, and re-layouts  0.85 us (2%)
    all_to_all x1, starting transfers between devices, on_device(): most = lax.all_to_all(most, ('energy', 'space'), 0, 0)  7.28 us
    ppermute x4, starting transfers between devices, exchanged(): lax.ppermute(x, axis, pairs(axis, odd_first))  6.86 us
    all_to_all x1, waiting for transfers between devices, on_device(): most = lax.all_to_all(most, ('energy', 'space'), 0, 0)  6.72 us
    ppermute x6, starting transfers between devices, toggled(): lax.ppermute(x, axis, [(i, i ^ mask) for i in range(lax.axis_size(axis))])  4.99 us
    ppermute x6, waiting for transfers between devices, toggled(): lax.ppermute(x, axis, [(i, i ^ mask) for i in range(lax.axis_size(axis))])  4.01 us
    pallas_call x1, Pallas kernels, orbital_table(): pl.pallas_call(table_kernel, in_specs=[vmem] * 4, out_specs=[vmem] * 3, o...  2.44 us
    pallas_call x1, Pallas kernels, swept(): pl.pallas_call(sweep_kernel, in_specs=[vmem] * 10, out_specs=[vmem, vmem]...  2.35 us
    pallas_call x1, Pallas kernels, own_planes(): pl.pallas_call(own_kernel, in_specs=[vmem] * 8, out_specs=[vmem] * 5, out...  2.01 us
  transfers between devices with their start and end apart: 11, of which 4 were waited for; matrix products, arithmetic and copies ran while one was open for 0% of the time, Pallas kernels for 14%

profile of v4, /device:TPU:0, one launch (start us, length us, event | category | flops | bytes accessed | tf_op | source)
XLA Modules:
  0.0 41.3 jit_solution(9187443205017108410)
XLA Ops:
  0.0 0.0 copy-start.5
  0.0 0.0 copy-start
  0.0 0.0 copy-start.1
  0.0 0.0 copy-start.2
  0.0 0.0 copy-start.3
  0.0 0.0 copy-start.4
  0.0 1.4 %edges.1 = (f32[192,128]{1,0:T(8,128)S(1)}, f32[192,128]{1,0:T(8,128)S(1)}, f32[264,128]{1,0:T(8,128)S(1)}, f32[264,128]{1,0:T(8,128)S(1)}) custom-call(s32[32,16,128]{2,1,0:T(8,128)} %regions_ref.3, f32[32,16,128]{2,1,0:T(8,128)} %dopant_ref.3, s32[32,64,128]{2,1,0:T(8,128)} %mesh_ref.3, f32[32,64,128]{2,1,0:T(8,128)} %old_ref.7, ...), custom_call_target="tpu_custom_call" | custom-call | bytes 10485760 | tf_op jit(solution)/shard_map/edges/pallas_call | solution.py:204
  1.4 3.0 %collective-permute-start.1 = (f32[264,128]{1,0:T(8,128)S(1)}, f32[264,128]{1,0:T(8,128)S(1)}, u32[]{:S(2)}, u32[]{:S(2)}) collective-permute-start(f32[264,128]{1,0:T(8,128)S(1)} %get-tuple-element.43), channel_id=1, source_target_pairs={{0,1},{1,0},{2,3},{3,2},{4,5},{5,4},{6,7},{7,6},{8,9},{9,8},{10,11... | collective-permute-start | bytes 405512 | tf_op jit(solution)/shard_map/ppermute | solution.py:617
  4.5 0.8 %collective-permute-start.2 = (f32[264,128]{1,0:T(8,128)S(1)}, f32[264,128]{1,0:T(8,128)S(1)}, u32[]{:S(2)}, u32[]{:S(2)}) collective-permute-start(f32[264,128]{1,0:T(8,128)S(1)} %get-tuple-element.44), channel_id=1, source_target_pairs={{1,2},{2,1},{3,4},{4,3},{5,6},{6,5},{9,10},{10,9},{11,12},{12,11},... | collective-permute-start | bytes 405512 | tf_op jit(solution)/shard_map/ppermute | solution.py:617
  5.3 0.0 copy-done.5
  5.3 0.8 %copy-done = f32[1,2,2,1024,1024]{4,3,2,1,0:T(8,128)S(1)} copy-done((f32[1,2,2,1024,1024]{4,3,2,1,0:T(8,128)S(1)}, f32[1,2,2,1024,1024]{4,3,2,1,0:T(8,128)}, u32[]{:S(2)}) %copy-start) | copy-done | bytes 16777240
  6.1 2.4 %table.1 = (f32[2,2,8,128]{3,2,1,0:T(8,128)S(1)}, f32[224,128]{1,0:T(8,128)S(1)}, f32[224,128]{1,0:T(8,128)S(1)}) custom-call(f32[2,2,1024,1024]{3,2,1,0:T(8,128)S(1)} %bitcast.3, f32[2,2,1024]{2,1,0:T(2,128)S(1)} %bitcast.5, f32[192,128]{1,0:T(8,128)S(1)} %get-tuple-element.39.rows1_ref, f32[192,128]{1,0:T(8,128)S(1)} %get-tuple-element.40.rows2_ref), custom_call_target="tpu_custom_call" | custom-call | bytes 10485760 | tf_op jit(solution)/shard_map/table/pallas_call | solution.py:100
  8.5 0.5 %collective-permute-start = (f32[224,128]{1,0:T(8,128)S(1)}, f32[224,128]{1,0:T(8,128)S(1)}, u32[]{:S(2)}, u32[]{:S(2)}) collective-permute-start(f32[224,128]{1,0:T(8,128)S(1)} %get-tuple-element.42), channel_id=1, source_target_pairs={{0,8},{8,0},{16,24},{24,16},{1,9},{9,1},{17,25},{25,17},{2,10},{10... | collective-permute-start | bytes 344072 | tf_op jit(solution)/shard_map/ppermute | solution.py:608
  9.0 2.6 %collective-permute-start.4 = (f32[224,128]{1,0:T(8,128)S(1)}, f32[224,128]{1,0:T(8,128)S(1)}, u32[]{:S(2)}, u32[]{:S(2)}) collective-permute-start(f32[224,128]{1,0:T(8,128)S(1)} %get-tuple-element.46), channel_id=1, source_target_pairs={{0,24},{8,16},{16,8},{24,0},{1,25},{9,17},{17,9},{25,1},{2,26},{10... | collective-permute-start | bytes 344072 | tf_op jit(solution)/shard_map/ppermute | solution.py:608
  11.6 0.0 collective-permute-done.1.planes1_ref
  11.6 0.0 collective-permute-done.2.planes2_ref
  11.7 0.0 collective-permute-start.3
  11.7 0.0 copy-done.1
  11.7 0.0 copy-done.2
  11.7 0.4 lay.1
  12.1 0.0 collective-permute-done.refs_1_.refs_4_.rows1_ref
  12.1 3.0 %collective-permute-done.4.refs_3_.refs_5_.rows2_ref = f32[224,128]{1,0:T(8,128)S(1)} collective-permute-done((f32[224,128]{1,0:T(8,128)S(1)}, f32[224,128]{1,0:T(8,128)S(1)}, u32[]{:S(2)}, u32[]{:S(2)}) %collective-permute-start.4) | collective-permute-done | bytes 114720 | tf_op jit(solution)/shard_map/ppermute | solution.py:608
  15.1 0.6 %collective-permute-done.3.refs_2_ = f32[2,2,8,128]{3,2,1,0:T(8,128)S(1)} collective-permute-done((f32[2,2,8,128]{3,2,1,0:T(8,128)S(1)}, f32[2,2,8,128]{3,2,1,0:T(8,128)S(1)}, u32[]{:S(2)}, u32[]{:S(2)}) %collective-permute-start.3) | collective-permute-done | bytes 16416 | tf_op jit(solution)/shard_map/ppermute | solution.py:608
  15.7 2.4 %collective-permute-start.5 = (f32[64,128]{1,0:T(8,128)S(1)}, f32[64,128]{1,0:T(8,128)S(1)}, u32[]{:S(2)}, u32[]{:S(2)}) collective-permute-start(f32[64,128]{1,0:T(8,128)S(1)} %get-tuple-element.56), channel_id=1, source_target_pairs={{0,1},{1,0},{2,3},{3,2},{4,5},{5,4},{6,7},{7,6},{8,9},{9,8},{10,11... | collective-permute-start | bytes 98312 | tf_op jit(solution)/shard_map/ppermute | solution.py:617
  18.1 0.7 %collective-permute-start.6 = (f32[64,128]{1,0:T(8,128)S(1)}, f32[64,128]{1,0:T(8,128)S(1)}, u32[]{:S(2)}, u32[]{:S(2)}) collective-permute-start(f32[64,128]{1,0:T(8,128)S(1)} %get-tuple-element.57), channel_id=1, source_target_pairs={{1,2},{2,1},{3,4},{4,3},{5,6},{6,5},{9,10},{10,9},{11,12},{12,11},... | collective-permute-start | bytes 98312 | tf_op jit(solution)/shard_map/ppermute | solution.py:617
  18.8 0.0 copy-done.3
  18.8 0.0 copy-done.4
  18.8 2.0 %own.1 = (f32[32,24,128]{2,1,0:T(8,128)S(1)}, f32[32,24,128]{2,1,0:T(8,128)S(1)}, f32[32,24,128]{2,1,0:T(8,128)S(1)}, f32[32,24,128]{2,1,0:T(8,128)S(1)}, f32[32,24,128]{2,1,0:T(8,128)S(1)}) custom-call(f32[2,2,8,128]{3,2,1,0:T(8,128)S(1)} %get-tuple-element.59.tables_ref, s32[32,24,128]{2,1,0:T(8,128)S(1)} %get-tuple-element.60.mesh_x, ...), custom_call_target="tpu_custom_call" | custom-call | bytes 3145728 | tf_op jit(solution)/shard_map/own/pallas_call | solution.py:398
  20.8 0.0 collective-permute-done.5.packed1_ref
  20.8 0.0 collective-permute-done.6.packed2_ref
  20.8 2.4 %sweeps.1 = (f32[32,16,128]{2,1,0:T(8,128)S(1)}, f32[32,1,128]{2,1,0:T(1,128)}) custom-call(f32[64,128]{1,0:T(8,128)S(1)} %collective-permute-done.5.packed1_ref, f32[64,128]{1,0:T(8,128)S(1)} %collective-permute-done.6.packed2_ref, f32[264,128]{1,0:T(8,128)S(1)} %collective-permute-done.1.planes1_ref, f32[264,128]{1,0:T(8,128)S(1)} %collective-permute-done.2.planes2_ref, ...), custom_call_target="tpu_custom_call" | custom-call | tf_op jit(solution)/shard_map/sweeps/pallas_call | solution.py:525
  23.2 1.5 %collective-permute-start.7 = (f32[32,16,128]{2,1,0:T(8,128)S(1)}, f32[32,16,128]{2,1,0:T(8,128)S(1)}, u32[]{:S(2)}, u32[]{:S(2)}) collective-permute-start(f32[32,16,128]{2,1,0:T(8,128)S(1)} %get-tuple-element.68.rest_0_), channel_id=1, source_target_pairs={{0,16},{8,24},{16,0},{24,8},{1,17},{9,25},{17,1},{25,9},{2,18},{10... | collective-permute-start | bytes 786440 | tf_op jit(solution)/shard_map/ppermute | solution.py:608
  24.7 7.3 %all-to-all-start = ((f32[32,1,128]{2,1,0:T(1,128)}), f32[32,1,128]{2,1,0:T(1,128)S(1)}, u32[]{:S(2)}, u32[]{:S(2)}) async-start(f32[32,1,128]{2,1,0:T(1,128)} %get-tuple-element.67), calls=%async_computation | async-start | bytes 32768 | tf_op jit(solution)/shard_map/all_to_all | solution.py:643
  32.0 0.3 collective-permute-start.8
  32.3 6.7 %all-to-all-done.most_ref = f32[32,1,128]{2,1,0:T(1,128)S(1)} async-done(((f32[32,1,128]{2,1,0:T(1,128)}), f32[32,1,128]{2,1,0:T(1,128)S(1)}, u32[]{:S(2)}, u32[]{:S(2)}) %all-to-all-start) | async-done | bytes 16416 | tf_op jit(solution)/shard_map/all_to_all | solution.py:643
  39.0 0.0 collective-permute-done.7.rest_1_
  39.0 0.0 collective-permute-start.9
  39.0 0.0 collective-permute-done.8.rest_2_
  39.0 1.1 %settle.1 = (f32[32,64,128]{2,1,0:T(8,128)}, f32[8,128]{1,0:T(8,128)S(1)}) custom-call(f32[32,1,128]{2,1,0:T(1,128)S(1)} %all-to-all-done.most_ref, f32[32,64,128]{2,1,0:T(8,128)S(1)} %copy-done.1, f32[32,16,128]{2,1,0:T(8,128)S(1)} %get-tuple-element.68.rest_0_, f32[32,16,128]{2,1,0:T(8,128)S(1)} %collective-permute-done.7.rest_1_, ...), custom_call_target="tpu_custom_call" | custom-call | bytes 3145728 | tf_op jit(solution)/shard_map/settle/pallas_call | solution.py:577
  40.2 0.4 %collective-permute-done.9.rest_0_ = f32[32,16,128]{2,1,0:T(8,128)S(1)} collective-permute-done((f32[32,16,128]{2,1,0:T(8,128)S(1)}, f32[32,16,128]{2,1,0:T(8,128)S(1)}, u32[]{:S(2)}, u32[]{:S(2)}) %collective-permute-start.9) | collective-permute-done | bytes 262176 | tf_op jit(solution)/shard_map/ppermute | solution.py:608
  40.6 0.7 %settle_more.1 = f32[32,64,128]{2,1,0:T(8,128)} custom-call(f32[8,128]{1,0:T(8,128)S(1)} %get-tuple-element.70.scale_ref, f32[32,64,128]{2,1,0:T(8,128)S(1)} %copy-done.1, f32[32,16,128]{2,1,0:T(8,128)S(1)} %collective-permute-done.9.rest_0_, f32[32,64,128]{2,1,0:T(8,128)} %get-tuple-element.72.rest_1_), custom_call_target="tpu_custom_call", output_to_operand_aliasing={{}: (3, {})} | custom-call | tf_op jit(solution)/shard_map/settle_more/pallas_call | solution.py:587
  (1 shorter events, 0.0 us)
Async XLA Ops:
  0.0 5.3 %copy-start.5 = (f32[1,2,2,1024]{3,2,1,0:T(2,128)S(1)}, f32[1,2,2,1024]{3,2,1,0:T(2,128)}, u32[]{:S(2)}) copy-start(f32[1,2,2,1024]{3,2,1,0:T(2,128)} %param.7) | copy-start | bytes 49156
  0.0 6.1 %copy-start = (f32[1,2,2,1024,1024]{4,3,2,1,0:T(8,128)S(1)}, f32[1,2,2,1024,1024]{4,3,2,1,0:T(8,128)}, u32[]{:S(2)}) copy-start(f32[1,2,2,1024,1024]{4,3,2,1,0:T(8,128)} %param.6) | copy-start | bytes 50331652
  0.0 11.7 %copy-start.1 = (f32[32,64,128]{2,1,0:T(8,128)S(1)}, f32[32,64,128]{2,1,0:T(8,128)}, u32[]{:S(2)}) copy-start(f32[32,64,128]{2,1,0:T(8,128)} %old_ref.7) | copy-start | bytes 3145732
  0.0 11.7 %copy-start.2 = (s32[32,64,128]{2,1,0:T(8,128)S(1)}, s32[32,64,128]{2,1,0:T(8,128)}, u32[]{:S(2)}) copy-start(s32[32,64,128]{2,1,0:T(8,128)} %mesh_ref.3) | copy-start | bytes 3145732
  0.0 18.8 %copy-start.3 = (s32[32,16,128]{2,1,0:T(8,128)S(1)}, s32[32,16,128]{2,1,0:T(8,128)}, u32[]{:S(2)}) copy-start(s32[32,16,128]{2,1,0:T(8,128)} %regions_ref.3) | copy-start | bytes 786436
  0.0 18.8 %copy-start.4 = (f32[32,16,128]{2,1,0:T(8,128)S(1)}, f32[32,16,128]{2,1,0:T(8,128)}, u32[]{:S(2)}) copy-start(f32[32,16,128]{2,1,0:T(8,128)} %dopant_ref.3) | copy-start | bytes 786436
  1.4 10.2 %collective-permute-start.1 = (f32[264,128]{1,0:T(8,128)S(1)}, f32[264,128]{1,0:T(8,128)S(1)}, u32[]{:S(2)}, u32[]{:S(2)}) collective-permute-start(f32[264,128]{1,0:T(8,128)S(1)} %get-tuple-element.43), channel_id=1, source_target_pairs={{0,1},{1,0},{2,3},{3,2},{4,5},{5,4},{6,7},{7,6},{8,9},{9,8},{10,11... | collective-permute-start | bytes 405512 | tf_op jit(solution)/shard_map/ppermute | solution.py:617
  4.5 7.2 %collective-permute-start.2 = (f32[264,128]{1,0:T(8,128)S(1)}, f32[264,128]{1,0:T(8,128)S(1)}, u32[]{:S(2)}, u32[]{:S(2)}) collective-permute-start(f32[264,128]{1,0:T(8,128)S(1)} %get-tuple-element.44), channel_id=1, source_target_pairs={{1,2},{2,1},{3,4},{4,3},{5,6},{6,5},{9,10},{10,9},{11,12},{12,11},... | collective-permute-start | bytes 405512 | tf_op jit(solution)/shard_map/ppermute | solution.py:617
  8.5 3.6 %collective-permute-start = (f32[224,128]{1,0:T(8,128)S(1)}, f32[224,128]{1,0:T(8,128)S(1)}, u32[]{:S(2)}, u32[]{:S(2)}) collective-permute-start(f32[224,128]{1,0:T(8,128)S(1)} %get-tuple-element.42), channel_id=1, source_target_pairs={{0,8},{8,0},{16,24},{24,16},{1,9},{9,1},{17,25},{25,17},{2,10},{10... | collective-permute-start | bytes 344072 | tf_op jit(solution)/shard_map/ppermute | solution.py:608
  9.0 6.1 %collective-permute-start.4 = (f32[224,128]{1,0:T(8,128)S(1)}, f32[224,128]{1,0:T(8,128)S(1)}, u32[]{:S(2)}, u32[]{:S(2)}) collective-permute-start(f32[224,128]{1,0:T(8,128)S(1)} %get-tuple-element.46), channel_id=1, source_target_pairs={{0,24},{8,16},{16,8},{24,0},{1,25},{9,17},{17,9},{25,1},{2,26},{10... | collective-permute-start | bytes 344072 | tf_op jit(solution)/shard_map/ppermute | solution.py:608
  11.7 4.0 %collective-permute-start.3 = (f32[2,2,8,128]{3,2,1,0:T(8,128)S(1)}, f32[2,2,8,128]{3,2,1,0:T(8,128)S(1)}, u32[]{:S(2)}, u32[]{:S(2)}) collective-permute-start(f32[2,2,8,128]{3,2,1,0:T(8,128)S(1)} %get-tuple-element.52.refs_0_), channel_id=1, source_target_pairs={{0,16},{8,24},{16,0},{24,8},{1,17},{9,25},{17,1},{25,9},{2,18},{10... | collective-permute-start | bytes 49160 | tf_op jit(solution)/shard_map/ppermute | solution.py:608
  15.7 5.1 %collective-permute-start.5 = (f32[64,128]{1,0:T(8,128)S(1)}, f32[64,128]{1,0:T(8,128)S(1)}, u32[]{:S(2)}, u32[]{:S(2)}) collective-permute-start(f32[64,128]{1,0:T(8,128)S(1)} %get-tuple-element.56), channel_id=1, source_target_pairs={{0,1},{1,0},{2,3},{3,2},{4,5},{5,4},{6,7},{7,6},{8,9},{9,8},{10,11... | collective-permute-start | bytes 98312 | tf_op jit(solution)/shard_map/ppermute | solution.py:617
  18.1 2.7 %collective-permute-start.6 = (f32[64,128]{1,0:T(8,128)S(1)}, f32[64,128]{1,0:T(8,128)S(1)}, u32[]{:S(2)}, u32[]{:S(2)}) collective-permute-start(f32[64,128]{1,0:T(8,128)S(1)} %get-tuple-element.57), channel_id=1, source_target_pairs={{1,2},{2,1},{3,4},{4,3},{5,6},{6,5},{9,10},{10,9},{11,12},{12,11},... | collective-permute-start | bytes 98312 | tf_op jit(solution)/shard_map/ppermute | solution.py:617
  23.2 15.8 %collective-permute-start.7 = (f32[32,16,128]{2,1,0:T(8,128)S(1)}, f32[32,16,128]{2,1,0:T(8,128)S(1)}, u32[]{:S(2)}, u32[]{:S(2)}) collective-permute-start(f32[32,16,128]{2,1,0:T(8,128)S(1)} %get-tuple-element.68.rest_0_), channel_id=1, source_target_pairs={{0,16},{8,24},{16,0},{24,8},{1,17},{9,25},{17,1},{25,9},{2,18},{10... | collective-permute-start | bytes 786440 | tf_op jit(solution)/shard_map/ppermute | solution.py:608
  24.7 14.3 %all-to-all-start = ((f32[32,1,128]{2,1,0:T(1,128)}), f32[32,1,128]{2,1,0:T(1,128)S(1)}, u32[]{:S(2)}, u32[]{:S(2)}) async-start(f32[32,1,128]{2,1,0:T(1,128)} %get-tuple-element.67), calls=%async_computation | async-start | bytes 32768 | tf_op jit(solution)/shard_map/all_to_all | solution.py:643
  32.0 7.0 %collective-permute-start.8 = (f32[32,16,128]{2,1,0:T(8,128)S(1)}, f32[32,16,128]{2,1,0:T(8,128)S(1)}, u32[]{:S(2)}, u32[]{:S(2)}) collective-permute-start(f32[32,16,128]{2,1,0:T(8,128)S(1)} %get-tuple-element.68.rest_0_), channel_id=1, source_target_pairs={{0,8},{8,0},{16,24},{24,16},{1,9},{9,1},{17,25},{25,17},{2,10},{10... | collective-permute-start | bytes 786440 | tf_op jit(solution)/shard_map/ppermute | solution.py:608
  39.0 1.5 %collective-permute-start.9 = (f32[32,16,128]{2,1,0:T(8,128)S(1)}, f32[32,16,128]{2,1,0:T(8,128)S(1)}, u32[]{:S(2)}, u32[]{:S(2)}) collective-permute-start(f32[32,16,128]{2,1,0:T(8,128)S(1)} %collective-permute-done.7.rest_1_), channel_id=1, source_target_pairs={{0,8},{8,0},{16,24},{24,16},{1,9},{9,1},{17,25},{25,17},{2,10},{10... | collective-permute-start | bytes 786440 | tf_op jit(solution)/shard_map/ppermute | solution.py:608

commit v5 on v4

--- a/solution.py
+++ b/solution.py
@@ -130,6 +130,8 @@
     odd = count % size
     if odd:
         carry = step(0, odd, carry)
+    if count // size < 2:
+        return step(odd, size, carry) if count >= size else carry
     return lax.fori_loop(0, count // size, lambda i, c: step(odd + i * size, size, c), carry)
 
 
@@ -361,9 +363,19 @@
     )(mesh, old, *beyond)
 
 
+def later_sweep(center, below, above, left, right, before, permit, dopant, electrons, holes):
+    moved = center - before
+    electrons = electrons * jnp.exp(moved)
+    holes = holes * jnp.exp(-moved)
+    bend = 6.0 * center - around(center, below, above, left, right)
+    mismatch = permit * bend - (dopant + holes - electrons)
+    jacobian = 6.0 * permit + electrons + holes
+    return center - mismatch / jacobian
+
+
 def own_kernel(
     tables_ref, mesh_x, before_x, bend_x, regions_ref, dopant_ref, rows1_ref, rows2_ref,
-    permit_x, dopant_x, electron_x, hole_x, now_x,
+    permit_x, dopant_x, electron_x, hole_x, change_x, most_x, *level_x,
 ):
     planes, own, _ = regions_ref.shape
     slabs = tables_ref.shape[0]
@@ -383,7 +395,7 @@
                 at, rows = PAD + r, slice(r, r + SUB)
                 for k in range(count):
                     p = slab * PL + first + k
-                    electron_x[p, rows], hole_x[p, rows], now_x[p, rows] = first_sweep(
+                    electron_x[p, rows], hole_x[p, rows], level_x[0][p, at : at + SUB] = first_sweep(
                         mesh_x[p, rows], tables, before_x[HALO + p, at : at + SUB], bend_x[p, rows],
                         permit_x[p, rows], dopant_x[p, rows], outside_rows(r, span),
                     )
@@ -392,48 +404,70 @@
         grouped(PL, LOOK, some, None)
 
 
+    for sweep in range(1, SWEEPS):
+        final = sweep == SWEEPS - 1
+        starts = range(HALO, HALO + own, SUB) if final else range(0, span, SUB)
+
+        def step(first, count, most, sweep=sweep, starts=starts, final=final):
+            source = level_x[sweep - 1]
+            for r in starts:
+                rows = slice(r, r + SUB)
+                at = PAD + r
+                held = [source[sweep + first + k, at : at + SUB] for k in range(-1, count + 1)]
+                for k in range(count):
+                    p = sweep + first + k
+                    before = before_x[HALO + p, at : at + SUB]
+                    fresh = later_sweep(
+                        held[k + 1], held[k], held[k + 2],
+                        source[p, at - 1 : at - 1 + SUB], source[p, at + 1 : at + 1 + SUB],
+                        before, permit_x[p, rows], dopant_x[p, rows], electron_x[p, rows], hole_x[p, rows],
+                    )
+                    if final:
+                        change_x[p, r - HALO : r - HALO + SUB] = fresh - before
+                        most = jnp.maximum(most, jnp.abs(fresh - before))
+                    else:
+                        level_x[sweep][p, at : at + SUB] = fresh
+            return most
+
+        most = grouped(planes - 2 * sweep, BLOCK, step, jnp.zeros((SUB, LANES), jnp.float32))
+        if final:
+            most_x[...] = most
+
+
 def own_planes(tables, laid_out, regions, dopant, rows):
     vmem = pl.BlockSpec(memory_space=pltpu.VMEM)
     cells = laid_out[0].shape
+    padded = (cells[0],) + laid_out[1].shape[1:]
+    shapes = [cells] * 4 + [regions.shape, (SUB, LANES)] + [padded] * (SWEEPS - 1)
     return pl.pallas_call(
         own_kernel,
         in_specs=[vmem] * 8,
-        out_specs=[vmem] * 5,
-        out_shape=[jax.ShapeDtypeStruct(cells, jnp.float32)] * 5,
-        compiler_params=pltpu.CompilerParams(vmem_limit_bytes=16 * MIB),
+        out_specs=[vmem] * len(shapes),
+        out_shape=[jax.ShapeDtypeStruct(shape, jnp.float32) for shape in shapes],
+        compiler_params=pltpu.CompilerParams(vmem_limit_bytes=24 * MIB),
         cost_estimate=pl.CostEstimate(flops=0, bytes_accessed=LAY_COST, transcendentals=0),
         name="own",
     )(tables, *laid_out, regions, dopant, *rows)
 
 
 def sweep_kernel(
-    packed1_ref, packed2_ref, planes1_ref, planes2_ref, before_x, permit_o, dopant_o, electron_o, hole_o, now_o,
-    change_ref, most_ref, permit_x, dopant_x, electron_x, hole_x, now_s, next_s,
+    packed1_ref, packed2_ref, planes1_ref, planes2_ref, before_x, permit_o, dopant_o, electron_o, hole_o, change_o,
+    most_o, level1_o, level2_o, level3_o, change_ref, most_ref, permit_s, dopant_s, electron_s, hole_s, level_s,
 ):
     _, s, _, ns = position()
     odd_s = (s & 1) == 1
     planes, own, _ = change_ref.shape
     span = own + 2 * HALO
     tops = range(0, span, SUB)
-
-    def bring(first, count, _):
-        for k in range(count):
-            p = first + k
-            q = HALO + p
-            for r in tops:
-                rows = slice(r, r + SUB)
-                permit_x[q, rows] = permit_o[p, rows]
-                dopant_x[q, rows] = dopant_o[p, rows]
-                electron_x[q, rows] = electron_o[p, rows]
-                hole_x[q, rows] = hole_o[p, rows]
-                now_s[q, PAD + r : PAD + r + SUB] = now_o[p, rows]
-        return _
-
-    grouped(planes, LAY, bring, None)
-    for low in (True, False):
-        a, b = (packed1_ref, packed2_ref) if low else (packed2_ref, packed1_ref)
-        c, d = (planes1_ref, planes2_ref) if low else (planes2_ref, planes1_ref)
-        inside = s > 0 if low else s < ns - 1
+    levels_o = (level1_o, level2_o, level3_o)
+
+    def plane_of(end, j):
+        return j if end == 0 else planes + 2 * HALO - 1 - j
+
+    for end in range(2):
+        a, b = (packed1_ref, packed2_ref) if end == 0 else (packed2_ref, packed1_ref)
+        c, d = (planes1_ref, planes2_ref) if end == 0 else (planes2_ref, planes1_ref)
+        inside = s > 0 if end == 0 else s < ns - 1
         top = 2 * NEAR * SUB
         tables = [
             [
@@ -450,87 +484,77 @@
             ]
             for t in (top, top + SUB)
         ]
-        for k in range(NEAR):
-            q = 1 + k if low else HALO + planes + k
-            for field, field_x in ((0, permit_x), (1, dopant_x)):
+        for j in range(1, HALO):
+            q = plane_of(end, j)
+            k = j - 1 if end == 0 else NEAR - j
+            for field, field_s in ((0, permit_s), (1, dopant_s)):
                 t = (field * NEAR + k) * SUB
                 m = (NEAR + HALO) * span + (field * NEAR + k) * own
-                field_x[q, :HALO] = jnp.where(odd_s, a[t : t + HALO], b[t : t + HALO])
-                field_x[q, HALO : HALO + own] = jnp.where(odd_s, c[m : m + own], d[m : m + own])
-                field_x[q, HALO + own :] = jnp.where(odd_s, a[t + HALO : t + SUB], b[t + HALO : t + SUB])
+                field_s[end, j, :HALO] = jnp.where(odd_s, a[t : t + HALO], b[t : t + HALO])
+                field_s[end, j, HALO : HALO + own] = jnp.where(odd_s, c[m : m + own], d[m : m + own])
+                field_s[end, j, HALO + own :] = jnp.where(odd_s, a[t + HALO : t + SUB], b[t + HALO : t + SUB])
             for r in tops:
                 at, rows = PAD + r, slice(r, r + SUB)
                 here = slice(k * span + r, k * span + r + SUB)
-                permit, dopant = permit_x[q, rows], dopant_x[q, rows]
                 choice = jnp.where(odd_s, c[here], d[here]).astype(jnp.int32)
                 center = before_x[q, at : at + SUB]
                 neighbours = around(
                     center, before_x[q - 1, at : at + SUB], before_x[q + 1, at : at + SUB],
                     before_x[q, at - 1 : at - 1 + SUB], before_x[q, at + 1 : at + 1 + SUB],
                 )
-                electrons, holes, fresh = first_sweep(
-                    choice, tables, center, 6.0 * center - neighbours, permit, dopant, outside_rows(r, span)
+                electron_s[end, j, rows], hole_s[end, j, rows], level_s[end, 0, j, at : at + SUB] = first_sweep(
+                    choice, tables, center, 6.0 * center - neighbours,
+                    permit_s[end, j, rows], dopant_s[end, j, rows], outside_rows(r, span),
                 )
-                electron_x[q, rows] = electrons
-                hole_x[q, rows] = holes
-                now_s[q, at : at + SUB] = fresh
-
-    source = now_s
+        for sweep in range(1, SWEEPS):
+            for j in (HALO + sweep - 1, HALO + sweep):
+                p = plane_of(end, j) - HALO
+                level_s[end, sweep - 1, j] = levels_o[sweep - 1][p]
+    for p in range(SWEEPS - 1, planes - SWEEPS + 1):
+        change_ref[p] = change_o[p]
+
+    most = most_o[...]
     for sweep in range(1, SWEEPS):
         final = sweep == SWEEPS - 1
-        target = next_s if source is now_s else now_s
-        starts = range(HALO, HALO + own, SUB) if final else tops
-
-        def step(first, count, most, sweep=sweep, source=source, target=target, starts=starts, final=final):
-            for r in starts:
-                rows = slice(r, r + SUB)
-                at = PAD + r
-                rows_b = slice(at, at + SUB)
-                held = [source[1 + sweep + first + k, rows_b] for k in range(-1, count + 1)]
-                for k in range(count):
-                    q = 1 + sweep + first + k
-                    center = held[k + 1]
-                    neighbours = around(
-                        center, held[k], held[k + 2],
-                        source[q, at - 1 : at - 1 + SUB], source[q, at + 1 : at + 1 + SUB],
+        for end in range(2):
+            source = level_s.at[end, sweep - 1]
+            for r in range(HALO, HALO + own, SUB) if final else tops:
+                at, rows = PAD + r, slice(r, r + SUB)
+                for j in range(1 + sweep, HALO + sweep):
+                    q = plane_of(end, j)
+                    p = q - HALO
+                    if j < HALO:
+                        fields = [ref[end, j, rows] for ref in (permit_s, dopant_s, electron_s, hole_s)]
+                    else:
+                        fields = [ref[p, rows] for ref in (permit_o, dopant_o, electron_o, hole_o)]
+                    before = before_x[q, at : at + SUB]
+                    fresh = later_sweep(
+                        source[j, at : at + SUB], source[j - 1, at : at + SUB], source[j + 1, at : at + SUB],
+                        source[j, at - 1 : at - 1 + SUB], source[j, at + 1 : at + 1 + SUB], before, *fields,
                     )
-                    permit = permit_x[q, rows]
-                    before = before_x[q, rows_b]
-                    moved = center - before
-                    electrons = electron_x[q, rows] * jnp.exp(moved)
-                    holes = hole_x[q, rows] * jnp.exp(-moved)
-                    mismatch = permit * (6.0 * center - neighbours) - (dopant_x[q, rows] + holes - electrons)
-                    jacobian = 6.0 * permit + electrons + holes
-                    fresh = center - mismatch / jacobian
                     if final:
-                        change = fresh - before
-                        change_ref[q - HALO, r - HALO : r - HALO + SUB] = change
-                        most = jnp.maximum(most, jnp.abs(change))
+                        change_ref[p, r - HALO : r - HALO + SUB] = fresh - before
+                        most = jnp.maximum(most, jnp.abs(fresh - before))
                     else:
-                        target[q, rows_b] = fresh
-            return most
-
-        most = grouped(planes + 2 * (SWEEPS - 1 - sweep), BLOCK, step, jnp.zeros((SUB, LANES), jnp.float32))
-        if final:
-            most_ref[...] = jnp.broadcast_to(jnp.max(most, axis=0, keepdims=True)[None], most_ref.shape)
-        source = target
+                        level_s[end, sweep, j, at : at + SUB] = fresh
+    most_ref[...] = jnp.broadcast_to(jnp.max(most, axis=0, keepdims=True)[None], most_ref.shape)
 
 
 def swept(packed, beyond, fields, own):
     planes, span, lanes = fields[1].shape
-    padded = fields[0].shape
-    cells = (padded[0], span, lanes)
+    height = fields[0].shape[1]
     vmem = pl.BlockSpec(memory_space=pltpu.VMEM)
     f32 = jnp.float32
     return pl.pallas_call(
         sweep_kernel,
-        in_specs=[vmem] * 10,
+        in_specs=[vmem] * (4 + len(fields)),
         out_specs=[vmem, vmem],
         out_shape=[
             jax.ShapeDtypeStruct((planes, own, lanes), f32),
             jax.ShapeDtypeStruct((lax.axis_size(("energy", "space")), 1, lanes), f32),
         ],
-        scratch_shapes=[pltpu.VMEM(cells, f32)] * 4 + [pltpu.VMEM(padded, f32)] * 2,
+        scratch_shapes=[pltpu.VMEM((2, HALO, span, lanes), f32)] * 4
+        + [pltpu.VMEM((2, SWEEPS - 1, 2 * HALO, height, lanes), f32)],
         compiler_params=pltpu.CompilerParams(vmem_limit_bytes=24 * MIB),
         name="sweeps",
     )(*packed, *beyond, *fields)

time: 41.5 us -> 40.5 us (0.976)
  starting transfers between devices: 19.1 us -> 18.2 us
    all_to_all x1, starting transfers between devices: 7.28 us -> 6.31 us  [on_device(): most = lax.all_to_all(most, ('energy', 'space'), 0, 0)]
  transfers between devices with their start and end apart: 11 -> 11, of which waited for: 4 -> 4; matrix products, arithmetic and copies ran while one was open for 0% -> 0% of each run, Pallas kernels for 14% -> 17%
where the time goes in v5:
time: 40.5 us; the launch traced here: 40.3 us
  starting transfers between devices  18.2 us (45%)
  waiting for transfers between devices  10.7 us (26%)
  Pallas kernels  10.4 us (26%)
  local copies, waits for them, and re-layouts  0.85 us (2%)
    ppermute x4, starting transfers between devices, exchanged(): lax.ppermute(x, axis, pairs(axis, odd_first))  6.86 us
    all_to_all x1, waiting for transfers between devices, on_device(): most = lax.all_to_all(most, ('energy', 'space'), 0, 0)  6.72 us
    all_to_all x1, starting transfers between devices, on_device(): most = lax.all_to_all(most, ('energy', 'space'), 0, 0)  6.31 us
    ppermute x6, starting transfers between devices, toggled(): lax.ppermute(x, axis, [(i, i ^ mask) for i in range(lax.axis_size(axis))])  4.99 us
    ppermute x6, waiting for transfers between devices, toggled(): lax.ppermute(x, axis, [(i, i ^ mask) for i in range(lax.axis_size(axis))])  4.01 us
    pallas_call x1, Pallas kernels, own_planes(): pl.pallas_call(own_kernel, in_specs=[vmem] * 8, out_specs=[vmem] * len(sh...  2.99 us
    pallas_call x1, Pallas kernels, orbital_table(): pl.pallas_call(table_kernel, in_specs=[vmem] * 4, out_specs=[vmem] * 3, o...  2.44 us
    pallas_call x1, Pallas kernels, edges(): pl.pallas_call(edge_kernel, in_specs=[pl.BlockSpec(memory_space=pl.ANY)]...  1.41 us
  transfers between devices with their start and end apart: 11, of which 4 were waited for; matrix products, arithmetic and copies ran while one was open for 0% of the time, Pallas kernels for 17%

profile of v5, /device:TPU:0, one launch (start us, length us, event | category | flops | bytes accessed | tf_op | source)
XLA Modules:
  0.0 40.3 jit_solution(4939546224754325746)
XLA Ops:
  0.0 0.0 copy-start.5
  0.0 0.0 copy-start
  0.0 0.0 copy-start.1
  0.0 0.0 copy-start.2
  0.0 0.0 copy-start.3
  0.0 0.0 copy-start.4
  0.0 1.4 %edges.1 = (f32[192,128]{1,0:T(8,128)S(1)}, f32[192,128]{1,0:T(8,128)S(1)}, f32[264,128]{1,0:T(8,128)S(1)}, f32[264,128]{1,0:T(8,128)S(1)}) custom-call(s32[32,16,128]{2,1,0:T(8,128)} %regions_ref.3, f32[32,16,128]{2,1,0:T(8,128)} %dopant_ref.3, s32[32,64,128]{2,1,0:T(8,128)} %mesh_ref.3, f32[32,64,128]{2,1,0:T(8,128)} %old_ref.7, ...), custom_call_target="tpu_custom_call" | custom-call | bytes 10485760 | tf_op jit(solution)/shard_map/edges/pallas_call | solution.py:206
  1.4 3.0 %collective-permute-start.1 = (f32[264,128]{1,0:T(8,128)S(1)}, f32[264,128]{1,0:T(8,128)S(1)}, u32[]{:S(2)}, u32[]{:S(2)}) collective-permute-start(f32[264,128]{1,0:T(8,128)S(1)} %get-tuple-element.47), channel_id=1, source_target_pairs={{0,1},{1,0},{2,3},{3,2},{4,5},{5,4},{6,7},{7,6},{8,9},{9,8},{10,11... | collective-permute-start | bytes 405512 | tf_op jit(solution)/shard_map/ppermute | solution.py:641
  4.5 0.8 %collective-permute-start.2 = (f32[264,128]{1,0:T(8,128)S(1)}, f32[264,128]{1,0:T(8,128)S(1)}, u32[]{:S(2)}, u32[]{:S(2)}) collective-permute-start(f32[264,128]{1,0:T(8,128)S(1)} %get-tuple-element.48), channel_id=1, source_target_pairs={{1,2},{2,1},{3,4},{4,3},{5,6},{6,5},{9,10},{10,9},{11,12},{12,11},... | collective-permute-start | bytes 405512 | tf_op jit(solution)/shard_map/ppermute | solution.py:641
  5.3 0.0 copy-done.5
  5.3 0.8 %copy-done = f32[1,2,2,1024,1024]{4,3,2,1,0:T(8,128)S(1)} copy-done((f32[1,2,2,1024,1024]{4,3,2,1,0:T(8,128)S(1)}, f32[1,2,2,1024,1024]{4,3,2,1,0:T(8,128)}, u32[]{:S(2)}) %copy-start) | copy-done | bytes 16777240
  6.1 2.4 %table.1 = (f32[2,2,8,128]{3,2,1,0:T(8,128)S(1)}, f32[224,128]{1,0:T(8,128)S(1)}, f32[224,128]{1,0:T(8,128)S(1)}) custom-call(f32[2,2,1024,1024]{3,2,1,0:T(8,128)S(1)} %bitcast.3, f32[2,2,1024]{2,1,0:T(2,128)S(1)} %bitcast.5, f32[192,128]{1,0:T(8,128)S(1)} %get-tuple-element.43.rows1_ref, f32[192,128]{1,0:T(8,128)S(1)} %get-tuple-element.44.rows2_ref), custom_call_target="tpu_custom_call" | custom-call | bytes 10485760 | tf_op jit(solution)/shard_map/table/pallas_call | solution.py:100
  8.5 0.5 %collective-permute-start = (f32[224,128]{1,0:T(8,128)S(1)}, f32[224,128]{1,0:T(8,128)S(1)}, u32[]{:S(2)}, u32[]{:S(2)}) collective-permute-start(f32[224,128]{1,0:T(8,128)S(1)} %get-tuple-element.46), channel_id=1, source_target_pairs={{0,8},{8,0},{16,24},{24,16},{1,9},{9,1},{17,25},{25,17},{2,10},{10... | collective-permute-start | bytes 344072 | tf_op jit(solution)/shard_map/ppermute | solution.py:632
  9.0 2.6 %collective-permute-start.4 = (f32[224,128]{1,0:T(8,128)S(1)}, f32[224,128]{1,0:T(8,128)S(1)}, u32[]{:S(2)}, u32[]{:S(2)}) collective-permute-start(f32[224,128]{1,0:T(8,128)S(1)} %get-tuple-element.50), channel_id=1, source_target_pairs={{0,24},{8,16},{16,8},{24,0},{1,25},{9,17},{17,9},{25,1},{2,26},{10... | collective-permute-start | bytes 344072 | tf_op jit(solution)/shard_map/ppermute | solution.py:632
  11.6 0.0 collective-permute-done.1.planes1_ref
  11.6 0.0 collective-permute-done.2.planes2_ref
  11.7 0.0 collective-permute-start.3
  11.7 0.0 copy-done.1
  11.7 0.0 copy-done.2
  11.7 0.4 lay.1
  12.1 0.0 collective-permute-done.refs_1_.refs_4_.rows1_ref
  12.1 3.0 %collective-permute-done.4.refs_3_.refs_5_.rows2_ref = f32[224,128]{1,0:T(8,128)S(1)} collective-permute-done((f32[224,128]{1,0:T(8,128)S(1)}, f32[224,128]{1,0:T(8,128)S(1)}, u32[]{:S(2)}, u32[]{:S(2)}) %collective-permute-start.4) | collective-permute-done | bytes 114720 | tf_op jit(solution)/shard_map/ppermute | solution.py:632
  15.1 0.6 %collective-permute-done.3.refs_2_ = f32[2,2,8,128]{3,2,1,0:T(8,128)S(1)} collective-permute-done((f32[2,2,8,128]{3,2,1,0:T(8,128)S(1)}, f32[2,2,8,128]{3,2,1,0:T(8,128)S(1)}, u32[]{:S(2)}, u32[]{:S(2)}) %collective-permute-start.3) | collective-permute-done | bytes 16416 | tf_op jit(solution)/shard_map/ppermute | solution.py:632
  15.7 2.4 %collective-permute-start.5 = (f32[64,128]{1,0:T(8,128)S(1)}, f32[64,128]{1,0:T(8,128)S(1)}, u32[]{:S(2)}, u32[]{:S(2)}) collective-permute-start(f32[64,128]{1,0:T(8,128)S(1)} %get-tuple-element.60), channel_id=1, source_target_pairs={{0,1},{1,0},{2,3},{3,2},{4,5},{5,4},{6,7},{7,6},{8,9},{9,8},{10,11... | collective-permute-start | bytes 98312 | tf_op jit(solution)/shard_map/ppermute | solution.py:641
  18.1 0.7 %collective-permute-start.6 = (f32[64,128]{1,0:T(8,128)S(1)}, f32[64,128]{1,0:T(8,128)S(1)}, u32[]{:S(2)}, u32[]{:S(2)}) collective-permute-start(f32[64,128]{1,0:T(8,128)S(1)} %get-tuple-element.61), channel_id=1, source_target_pairs={{1,2},{2,1},{3,4},{4,3},{5,6},{6,5},{9,10},{10,9},{11,12},{12,11},... | collective-permute-start | bytes 98312 | tf_op jit(solution)/shard_map/ppermute | solution.py:641
  18.8 0.0 copy-done.3
  18.8 0.0 copy-done.4
  18.8 3.0 %own.1 = (f32[32,24,128]{2,1,0:T(8,128)S(1)}, f32[32,24,128]{2,1,0:T(8,128)S(1)}, f32[32,24,128]{2,1,0:T(8,128)S(1)}, f32[32,24,128]{2,1,0:T(8,128)S(1)}, f32[32...) custom-call(f32[2,2,8,128]{3,2,1,0:T(8,128)S(1)} %get-tuple-element., ...), custom_call_target="tpu_custom_call" | custom-call | bytes 3145728 | tf_op jit(solution)/shard_map/own/pallas_call | solution.py:442
  21.8 0.0 collective-permute-done.5.packed1_ref
  21.8 0.0 collective-permute-done.6.packed2_ref
  21.8 1.4 %sweeps.1 = (f32[32,16,128]{2,1,0:T(8,128)S(1)}, f32[32,1,128]{2,1,0:T(1,128)}) custom-call(f32[64,128]{1,0:T(8,128)S(1)} %collective-permute-done.5.packed1_ref, f32[64,128]{1,0:T(8,128)S(1)} %collective-permute-done.6.packed2_ref, f32[264,128]{1,0:T(8,128)S(1)} %collective-permute-done.1.planes1_ref, f32[264,128]{1,0:T(8,128)S(1)} %collective-permute-done.2.planes2_ref, ...), custom_call_target="tpu_custom_call" | custom-call | tf_op jit(solution)/shard_map/sweeps/pallas_call | solution.py:548
  23.2 1.5 %collective-permute-start.7 = (f32[32,16,128]{2,1,0:T(8,128)S(1)}, f32[32,16,128]{2,1,0:T(8,128)S(1)}, u32[]{:S(2)}, u32[]{:S(2)}) collective-permute-start(f32[32,16,128]{2,1,0:T(8,128)S(1)} %get-tuple-element.76.rest_0_), channel_id=1, source_target_pairs={{0,16},{8,24},{16,0},{24,8},{1,17},{9,25},{17,1},{25,9},{2,18},{10... | collective-permute-start | bytes 786440 | tf_op jit(solution)/shard_map/ppermute | solution.py:632
  24.7 6.3 %all-to-all-start = ((f32[32,1,128]{2,1,0:T(1,128)}), f32[32,1,128]{2,1,0:T(1,128)S(1)}, u32[]{:S(2)}, u32[]{:S(2)}) async-start(f32[32,1,128]{2,1,0:T(1,128)} %get-tuple-element.75), calls=%async_computation | async-start | bytes 32768 | tf_op jit(solution)/shard_map/all_to_all | solution.py:667
  31.0 0.3 collective-permute-start.8
  31.3 6.7 %all-to-all-done.most_ref = f32[32,1,128]{2,1,0:T(1,128)S(1)} async-done(((f32[32,1,128]{2,1,0:T(1,128)}), f32[32,1,128]{2,1,0:T(1,128)S(1)}, u32[]{:S(2)}, u32[]{:S(2)}) %all-to-all-start) | async-done | bytes 16416 | tf_op jit(solution)/shard_map/all_to_all | solution.py:667
  38.0 0.0 collective-permute-done.7.rest_1_
  38.0 0.0 collective-permute-start.9
  38.0 0.0 collective-permute-done.8.rest_2_
  38.1 1.1 %settle.1 = (f32[32,64,128]{2,1,0:T(8,128)}, f32[8,128]{1,0:T(8,128)S(1)}) custom-call(f32[32,1,128]{2,1,0:T(1,128)S(1)} %all-to-all-done.most_ref, f32[32,64,128]{2,1,0:T(8,128)S(1)} %copy-done.1, f32[32,16,128]{2,1,0:T(8,128)S(1)} %get-tuple-element.76.rest_0_, f32[32,16,128]{2,1,0:T(8,128)S(1)} %collective-permute-done.7.rest_1_, ...), custom_call_target="tpu_custom_call" | custom-call | bytes 3145728 | tf_op jit(solution)/shard_map/settle/pallas_call | solution.py:601
  39.2 0.4 %collective-permute-done.9.rest_0_ = f32[32,16,128]{2,1,0:T(8,128)S(1)} collective-permute-done((f32[32,16,128]{2,1,0:T(8,128)S(1)}, f32[32,16,128]{2,1,0:T(8,128)S(1)}, u32[]{:S(2)}, u32[]{:S(2)}) %collective-permute-start.9) | collective-permute-done | bytes 262176 | tf_op jit(solution)/shard_map/ppermute | solution.py:632
  39.6 0.7 %settle_more.1 = f32[32,64,128]{2,1,0:T(8,128)} custom-call(f32[8,128]{1,0:T(8,128)S(1)} %get-tuple-element.78.scale_ref, f32[32,64,128]{2,1,0:T(8,128)S(1)} %copy-done.1, f32[32,16,128]{2,1,0:T(8,128)S(1)} %collective-permute-done.9.rest_0_, f32[32,64,128]{2,1,0:T(8,128)} %get-tuple-element.80.rest_1_), custom_call_target="tpu_custom_call", output_to_operand_aliasing={{}: (3, {})} | custom-call | tf_op jit(solution)/shard_map/settle_more/pallas_call | solution.py:611
  (1 shorter events, 0.0 us)
Async XLA Ops:
  0.0 5.3 %copy-start.5 = (f32[1,2,2,1024]{3,2,1,0:T(2,128)S(1)}, f32[1,2,2,1024]{3,2,1,0:T(2,128)}, u32[]{:S(2)}) copy-start(f32[1,2,2,1024]{3,2,1,0:T(2,128)} %param.7) | copy-start | bytes 49156
  0.0 6.1 %copy-start = (f32[1,2,2,1024,1024]{4,3,2,1,0:T(8,128)S(1)}, f32[1,2,2,1024,1024]{4,3,2,1,0:T(8,128)}, u32[]{:S(2)}) copy-start(f32[1,2,2,1024,1024]{4,3,2,1,0:T(8,128)} %param.6) | copy-start | bytes 50331652
  0.0 11.7 %copy-start.1 = (f32[32,64,128]{2,1,0:T(8,128)S(1)}, f32[32,64,128]{2,1,0:T(8,128)}, u32[]{:S(2)}) copy-start(f32[32,64,128]{2,1,0:T(8,128)} %old_ref.7) | copy-start | bytes 3145732
  0.0 11.7 %copy-start.2 = (s32[32,64,128]{2,1,0:T(8,128)S(1)}, s32[32,64,128]{2,1,0:T(8,128)}, u32[]{:S(2)}) copy-start(s32[32,64,128]{2,1,0:T(8,128)} %mesh_ref.3) | copy-start | bytes 3145732
  0.0 18.8 %copy-start.3 = (s32[32,16,128]{2,1,0:T(8,128)S(1)}, s32[32,16,128]{2,1,0:T(8,128)}, u32[]{:S(2)}) copy-start(s32[32,16,128]{2,1,0:T(8,128)} %regions_ref.3) | copy-start | bytes 786436
  0.0 18.8 %copy-start.4 = (f32[32,16,128]{2,1,0:T(8,128)S(1)}, f32[32,16,128]{2,1,0:T(8,128)}, u32[]{:S(2)}) copy-start(f32[32,16,128]{2,1,0:T(8,128)} %dopant_ref.3) | copy-start | bytes 786436
  1.4 10.2 %collective-permute-start.1 = (f32[264,128]{1,0:T(8,128)S(1)}, f32[264,128]{1,0:T(8,128)S(1)}, u32[]{:S(2)}, u32[]{:S(2)}) collective-permute-start(f32[264,128]{1,0:T(8,128)S(1)} %get-tuple-element.47), channel_id=1, source_target_pairs={{0,1},{1,0},{2,3},{3,2},{4,5},{5,4},{6,7},{7,6},{8,9},{9,8},{10,11... | collective-permute-start | bytes 405512 | tf_op jit(solution)/shard_map/ppermute | solution.py:641
  4.5 7.2 %collective-permute-start.2 = (f32[264,128]{1,0:T(8,128)S(1)}, f32[264,128]{1,0:T(8,128)S(1)}, u32[]{:S(2)}, u32[]{:S(2)}) collective-permute-start(f32[264,128]{1,0:T(8,128)S(1)} %get-tuple-element.48), channel_id=1, source_target_pairs={{1,2},{2,1},{3,4},{4,3},{5,6},{6,5},{9,10},{10,9},{11,12},{12,11},... | collective-permute-start | bytes 405512 | tf_op jit(solution)/shard_map/ppermute | solution.py:641
  8.5 3.5 %collective-permute-start = (f32[224,128]{1,0:T(8,128)S(1)}, f32[224,128]{1,0:T(8,128)S(1)}, u32[]{:S(2)}, u32[]{:S(2)}) collective-permute-start(f32[224,128]{1,0:T(8,128)S(1)} %get-tuple-element.46), channel_id=1, source_target_pairs={{0,8},{8,0},{16,24},{24,16},{1,9},{9,1},{17,25},{25,17},{2,10},{10... | collective-permute-start | bytes 344072 | tf_op jit(solution)/shard_map/ppermute | solution.py:632
  9.0 6.1 %collective-permute-start.4 = (f32[224,128]{1,0:T(8,128)S(1)}, f32[224,128]{1,0:T(8,128)S(1)}, u32[]{:S(2)}, u32[]{:S(2)}) collective-permute-start(f32[224,128]{1,0:T(8,128)S(1)} %get-tuple-element.50), channel_id=1, source_target_pairs={{0,24},{8,16},{16,8},{24,0},{1,25},{9,17},{17,9},{25,1},{2,26},{10... | collective-permute-start | bytes 344072 | tf_op jit(solution)/shard_map/ppermute | solution.py:632
  11.7 4.0 %collective-permute-start.3 = (f32[2,2,8,128]{3,2,1,0:T(8,128)S(1)}, f32[2,2,8,128]{3,2,1,0:T(8,128)S(1)}, u32[]{:S(2)}, u32[]{:S(2)}) collective-permute-start(f32[2,2,8,128]{3,2,1,0:T(8,128)S(1)} %get-tuple-element.56.refs_0_), channel_id=1, source_target_pairs={{0,16},{8,24},{16,0},{24,8},{1,17},{9,25},{17,1},{25,9},{2,18},{10... | collective-permute-start | bytes 49160 | tf_op jit(solution)/shard_map/ppermute | solution.py:632
  15.7 6.1 %collective-permute-start.5 = (f32[64,128]{1,0:T(8,128)S(1)}, f32[64,128]{1,0:T(8,128)S(1)}, u32[]{:S(2)}, u32[]{:S(2)}) collective-permute-start(f32[64,128]{1,0:T(8,128)S(1)} %get-tuple-element.60), channel_id=1, source_target_pairs={{0,1},{1,0},{2,3},{3,2},{4,5},{5,4},{6,7},{7,6},{8,9},{9,8},{10,11... | collective-permute-start | bytes 98312 | tf_op jit(solution)/shard_map/ppermute | solution.py:641
  18.1 3.7 %collective-permute-start.6 = (f32[64,128]{1,0:T(8,128)S(1)}, f32[64,128]{1,0:T(8,128)S(1)}, u32[]{:S(2)}, u32[]{:S(2)}) collective-permute-start(f32[64,128]{1,0:T(8,128)S(1)} %get-tuple-element.61), channel_id=1, source_target_pairs={{1,2},{2,1},{3,4},{4,3},{5,6},{6,5},{9,10},{10,9},{11,12},{12,11},... | collective-permute-start | bytes 98312 | tf_op jit(solution)/shard_map/ppermute | solution.py:641
  23.2 14.9 %collective-permute-start.7 = (f32[32,16,128]{2,1,0:T(8,128)S(1)}, f32[32,16,128]{2,1,0:T(8,128)S(1)}, u32[]{:S(2)}, u32[]{:S(2)}) collective-permute-start(f32[32,16,128]{2,1,0:T(8,128)S(1)} %get-tuple-element.76.rest_0_), channel_id=1, source_target_pairs={{0,16},{8,24},{16,0},{24,8},{1,17},{9,25},{17,1},{25,9},{2,18},{10... | collective-permute-start | bytes 786440 | tf_op jit(solution)/shard_map/ppermute | solution.py:632
  24.7 13.4 %all-to-all-start = ((f32[32,1,128]{2,1,0:T(1,128)}), f32[32,1,128]{2,1,0:T(1,128)S(1)}, u32[]{:S(2)}, u32[]{:S(2)}) async-start(f32[32,1,128]{2,1,0:T(1,128)} %get-tuple-element.75), calls=%async_computation | async-start | bytes 32768 | tf_op jit(solution)/shard_map/all_to_all | solution.py:667
  31.0 7.0 %collective-permute-start.8 = (f32[32,16,128]{2,1,0:T(8,128)S(1)}, f32[32,16,128]{2,1,0:T(8,128)S(1)}, u32[]{:S(2)}, u32[]{:S(2)}) collective-permute-start(f32[32,16,128]{2,1,0:T(8,128)S(1)} %get-tuple-element.76.rest_0_), channel_id=1, source_target_pairs={{0,8},{8,0},{16,24},{24,16},{1,9},{9,1},{17,25},{25,17},{2,10},{10... | collective-permute-start | bytes 786440 | tf_op jit(solution)/shard_map/ppermute | solution.py:632
  38.0 1.5 %collective-permute-start.9 = (f32[32,16,128]{2,1,0:T(8,128)S(1)}, f32[32,16,128]{2,1,0:T(8,128)S(1)}, u32[]{:S(2)}, u32[]{:S(2)}) collective-permute-start(f32[32,16,128]{2,1,0:T(8,128)S(1)} %collective-permute-done.7.rest_1_), channel_id=1, source_target_pairs={{0,8},{8,0},{16,24},{24,16},{1,9},{9,1},{17,25},{25,17},{2,10},{10... | collective-permute-start | bytes 786440 | tf_op jit(solution)/shard_map/ppermute | solution.py:632

commit v6 on v5

--- a/solution.py
+++ b/solution.py
@@ -643,11 +643,11 @@
     rows, beyond = edges(regions, dopant_charge_field, mesh_state_choice, earlier_voltage, green, inject)
     beyond = exchanged(beyond, "space")
     tables, packed1, packed2 = orbital_table(green, inject, rows)
-    alone, beyond = lax.optimization_barrier((tables, beyond))
+    packed1, beyond = lax.optimization_barrier((packed1, beyond))
     second = [k for k in range(3, ne) if k & (k + 1) == 0]
     terms = [tables]
     for k in range(1, ne):
-        sent = packed1 if k == 1 else packed2 if k in second else alone
+        sent = packed1 if k == 1 else packed2 if k in second else tables
         terms.append(toggled(sent, "energy", k))
     e = lax.axis_index("energy")
     partner = jnp.where(e & 1 == 1, e + 1, e - 1)

time: 40.5 us -> 40.4 us (level)
    ppermute x6, starting transfers between devices: 4.99 us -> 4.4 us  [toggled(): lax.ppermute(x, axis, [(i, i ^ mask) for i in range(lax.axis_size(axis))])]
    all_to_all x1, starting transfers between devices: 6.31 us -> 6.9 us  [on_device(): most = lax.all_to_all(most, ('energy', 'space'), 0, 0)]
  transfers between devices with their start and end apart: 11 -> 11, of which waited for: 4 -> 3; matrix products, arithmetic and copies ran while one was open for 0% -> 0% of each run, Pallas kernels for 17% -> 17%
where the time goes in v6:
time: 40.4 us; the launch traced here: 40.3 us
  starting transfers between devices  18.4 us (46%)
  waiting for transfers between devices  10.5 us (26%)
  Pallas kernels  10.4 us (26%)
  local copies, waits for them, and re-layouts  0.85 us (2%)
    ppermute x4, starting transfers between devices, exchanged(): lax.ppermute(x, axis, pairs(axis, odd_first))  7.09 us
    all_to_all x1, starting transfers between devices, on_device(): most = lax.all_to_all(most, ('energy', 'space'), 0, 0)  6.9 us
    all_to_all x1, waiting for transfers between devices, on_device(): most = lax.all_to_all(most, ('energy', 'space'), 0, 0)  6.72 us
    ppermute x6, starting transfers between devices, toggled(): lax.ppermute(x, axis, [(i, i ^ mask) for i in range(lax.axis_size(axis))])  4.4 us
    ppermute x6, waiting for transfers between devices, toggled(): lax.ppermute(x, axis, [(i, i ^ mask) for i in range(lax.axis_size(axis))])  3.72 us
    pallas_call x1, Pallas kernels, own_planes(): pl.pallas_call(own_kernel, in_specs=[vmem] * 8, out_specs=[vmem] * len(sh...  2.99 us
    pallas_call x1, Pallas kernels, orbital_table(): pl.pallas_call(table_kernel, in_specs=[vmem] * 4, out_specs=[vmem] * 3, o...  2.44 us
    pallas_call x1, Pallas kernels, edges(): pl.pallas_call(edge_kernel, in_specs=[pl.BlockSpec(memory_space=pl.ANY)]...  1.41 us
  transfers between devices with their start and end apart: 11, of which 3 were waited for; matrix products, arithmetic and copies ran while one was open for 0% of the time, Pallas kernels for 17%

profile of v6, /device:TPU:0, one launch (start us, length us, event | category | flops | bytes accessed | tf_op | source)
XLA Modules:
  0.0 40.3 jit_solution(5900611252000732704)
XLA Ops:
  0.0 0.0 copy-start.5
  0.0 0.0 copy-start
  0.0 0.0 copy-start.1
  0.0 0.0 copy-start.2
  0.0 0.0 copy-start.3
  0.0 0.0 copy-start.4
  0.0 1.4 %edges.1 = (f32[192,128]{1,0:T(8,128)S(1)}, f32[192,128]{1,0:T(8,128)S(1)}, f32[264,128]{1,0:T(8,128)S(1)}, f32[264,128]{1,0:T(8,128)S(1)}) custom-call(s32[32,16,128]{2,1,0:T(8,128)} %regions_ref.3, f32[32,16,128]{2,1,0:T(8,128)} %dopant_ref.3, s32[32,64,128]{2,1,0:T(8,128)} %mesh_ref.3, f32[32,64,128]{2,1,0:T(8,128)} %old_ref.7, ...), custom_call_target="tpu_custom_call" | custom-call | bytes 10485760 | tf_op jit(solution)/shard_map/edges/pallas_call | solution.py:206
  1.4 3.0 %collective-permute-start = (f32[264,128]{1,0:T(8,128)S(1)}, f32[264,128]{1,0:T(8,128)S(1)}, u32[]{:S(2)}, u32[]{:S(2)}) collective-permute-start(f32[264,128]{1,0:T(8,128)S(1)} %get-tuple-element.47), channel_id=1, source_target_pairs={{0,1},{1,0},{2,3},{3,2},{4,5},{5,4},{6,7},{7,6},{8,9},{9,8},{10,11... | collective-permute-start | bytes 405512 | tf_op jit(solution)/shard_map/ppermute | solution.py:641
  4.5 0.8 %collective-permute-start.1 = (f32[264,128]{1,0:T(8,128)S(1)}, f32[264,128]{1,0:T(8,128)S(1)}, u32[]{:S(2)}, u32[]{:S(2)}) collective-permute-start(f32[264,128]{1,0:T(8,128)S(1)} %get-tuple-element.48), channel_id=1, source_target_pairs={{1,2},{2,1},{3,4},{4,3},{5,6},{6,5},{9,10},{10,9},{11,12},{12,11},... | collective-permute-start | bytes 405512 | tf_op jit(solution)/shard_map/ppermute | solution.py:641
  5.3 0.0 copy-done.5
  5.3 0.8 %copy-done = f32[1,2,2,1024,1024]{4,3,2,1,0:T(8,128)S(1)} copy-done((f32[1,2,2,1024,1024]{4,3,2,1,0:T(8,128)S(1)}, f32[1,2,2,1024,1024]{4,3,2,1,0:T(8,128)}, u32[]{:S(2)}) %copy-start) | copy-done | bytes 16777240
  6.1 2.4 %table.1 = (f32[2,2,8,128]{3,2,1,0:T(8,128)S(1)}, f32[224,128]{1,0:T(8,128)S(1)}, f32[224,128]{1,0:T(8,128)S(1)}) custom-call(f32[2,2,1024,1024]{3,2,1,0:T(8,128)S(1)} %bitcast.3, f32[2,2,1024]{2,1,0:T(2,128)S(1)} %bitcast.5, f32[192,128]{1,0:T(8,128)S(1)} %get-tuple-element.43.rows1_ref, f32[192,128]{1,0:T(8,128)S(1)} %get-tuple-element.44.rows2_ref), custom_call_target="tpu_custom_call" | custom-call | bytes 10485760 | tf_op jit(solution)/shard_map/table/pallas_call | solution.py:100
  8.5 2.4 %collective-permute-start.4 = (f32[224,128]{1,0:T(8,128)S(1)}, f32[224,128]{1,0:T(8,128)S(1)}, u32[]{:S(2)}, u32[]{:S(2)}) collective-permute-start(f32[224,128]{1,0:T(8,128)S(1)} %get-tuple-element.50), channel_id=1, source_target_pairs={{0,24},{8,16},{16,8},{24,0},{1,25},{9,17},{17,9},{25,1},{2,26},{10... | collective-permute-start | bytes 344072 | tf_op jit(solution)/shard_map/ppermute | solution.py:632
  11.0 0.0 collective-permute-done.planes1_ref
  11.0 0.0 collective-permute-done.1.planes2_ref
  11.0 0.7 %collective-permute-start.2 = (f32[224,128]{1,0:T(8,128)S(1)}, f32[224,128]{1,0:T(8,128)S(1)}, u32[]{:S(2)}, u32[]{:S(2)}) collective-permute-start(f32[224,128]{1,0:T(8,128)S(1)} %get-tuple-element.49), channel_id=1, source_target_pairs={{0,8},{8,0},{16,24},{24,16},{1,9},{9,1},{17,25},{25,17},{2,10},{10... | collective-permute-start | bytes 344072 | tf_op jit(solution)/shard_map/ppermute | solution.py:632
  11.6 0.1 collective-permute-start.3
  11.7 0.0 copy-done.1
  11.7 0.0 copy-done.2
  11.7 0.4 lay.1
  12.1 3.3 %collective-permute-done.3.refs_2_ = f32[2,2,8,128]{3,2,1,0:T(8,128)S(1)} collective-permute-done((f32[2,2,8,128]{3,2,1,0:T(8,128)S(1)}, f32[2,2,8,128]{3,2,1,0:T(8,128)S(1)}, u32[]{:S(2)}, u32[]{:S(2)}) %collective-permute-start.3) | collective-permute-done | bytes 16416 | tf_op jit(solution)/shard_map/ppermute | solution.py:632
  15.4 0.0 collective-permute-done.4.refs_3_.refs_5_.rows2_ref
  15.4 0.0 collective-permute-done.2.refs_1_.refs_4_.rows1_ref
  15.4 2.6 %collective-permute-start.5 = (f32[64,128]{1,0:T(8,128)S(1)}, f32[64,128]{1,0:T(8,128)S(1)}, u32[]{:S(2)}, u32[]{:S(2)}) collective-permute-start(f32[64,128]{1,0:T(8,128)S(1)} %get-tuple-element.60), channel_id=1, source_target_pairs={{0,1},{1,0},{2,3},{3,2},{4,5},{5,4},{6,7},{7,6},{8,9},{9,8},{10,11... | collective-permute-start | bytes 98312 | tf_op jit(solution)/shard_map/ppermute | solution.py:641
  18.0 0.7 %collective-permute-start.6 = (f32[64,128]{1,0:T(8,128)S(1)}, f32[64,128]{1,0:T(8,128)S(1)}, u32[]{:S(2)}, u32[]{:S(2)}) collective-permute-start(f32[64,128]{1,0:T(8,128)S(1)} %get-tuple-element.61), channel_id=1, source_target_pairs={{1,2},{2,1},{3,4},{4,3},{5,6},{6,5},{9,10},{10,9},{11,12},{12,11},... | collective-permute-start | bytes 98312 | tf_op jit(solution)/shard_map/ppermute | solution.py:641
  18.7 0.0 copy-done.3
  18.7 0.0 copy-done.4
  18.7 3.0 %own.1 = (f32[32,24,128]{2,1,0:T(8,128)S(1)}, f32[32,24,128]{2,1,0:T(8,128)S(1)}, f32[32,24,128]{2,1,0:T(8,128)S(1)}, f32[32,24,128]{2,1,0:T(8,128)S(1)}, f32[32...) custom-call(f32[2,2,8,128]{3,2,1,0:T(8,128)S(1)} %get-tuple-element., ...), custom_call_target="tpu_custom_call" | custom-call | bytes 3145728 | tf_op jit(solution)/shard_map/own/pallas_call | solution.py:442
  21.7 0.0 collective-permute-done.5.packed1_ref
  21.7 0.0 collective-permute-done.6.packed2_ref
  21.7 1.4 %sweeps.1 = (f32[32,16,128]{2,1,0:T(8,128)S(1)}, f32[32,1,128]{2,1,0:T(1,128)}) custom-call(f32[64,128]{1,0:T(8,128)S(1)} %collective-permute-done.5.packed1_ref, f32[64,128]{1,0:T(8,128)S(1)} %collective-permute-done.6.packed2_ref, f32[264,128]{1,0:T(8,128)S(1)} %collective-permute-done.planes1_ref, f32[264,128]{1,0:T(8,128)S(1)} %collective-permute-done.1.planes2_ref, ...), custom_call_target="tpu_custom_call" | custom-call | tf_op jit(solution)/shard_map/sweeps/pallas_call | solution.py:548
  23.1 0.9 %collective-permute-start.7 = (f32[32,16,128]{2,1,0:T(8,128)S(1)}, f32[32,16,128]{2,1,0:T(8,128)S(1)}, u32[]{:S(2)}, u32[]{:S(2)}) collective-permute-start(f32[32,16,128]{2,1,0:T(8,128)S(1)} %get-tuple-element.76.rest_0_), channel_id=1, source_target_pairs={{0,16},{8,24},{16,0},{24,8},{1,17},{9,25},{17,1},{25,9},{2,18},{10... | collective-permute-start | bytes 786440 | tf_op jit(solution)/shard_map/ppermute | solution.py:632
  24.0 6.9 %all-to-all-start = ((f32[32,1,128]{2,1,0:T(1,128)}), f32[32,1,128]{2,1,0:T(1,128)S(1)}, u32[]{:S(2)}, u32[]{:S(2)}) async-start(f32[32,1,128]{2,1,0:T(1,128)} %get-tuple-element.75), calls=%async_computation | async-start | bytes 32768 | tf_op jit(solution)/shard_map/all_to_all | solution.py:667
  30.9 0.3 collective-permute-start.8
  31.2 6.7 %all-to-all-done.most_ref = f32[32,1,128]{2,1,0:T(1,128)S(1)} async-done(((f32[32,1,128]{2,1,0:T(1,128)}), f32[32,1,128]{2,1,0:T(1,128)S(1)}, u32[]{:S(2)}, u32[]{:S(2)}) %all-to-all-start) | async-done | bytes 16416 | tf_op jit(solution)/shard_map/all_to_all | solution.py:667
  38.0 0.0 collective-permute-done.7.rest_1_
  38.0 0.0 collective-permute-start.9
  38.0 0.0 collective-permute-done.8.rest_2_
  38.0 1.1 %settle.1 = (f32[32,64,128]{2,1,0:T(8,128)}, f32[8,128]{1,0:T(8,128)S(1)}) custom-call(f32[32,1,128]{2,1,0:T(1,128)S(1)} %all-to-all-done.most_ref, f32[32,64,128]{2,1,0:T(8,128)S(1)} %copy-done.1, f32[32,16,128]{2,1,0:T(8,128)S(1)} %get-tuple-element.76.rest_0_, f32[32,16,128]{2,1,0:T(8,128)S(1)} %collective-permute-done.7.rest_1_, ...), custom_call_target="tpu_custom_call" | custom-call | bytes 3145728 | tf_op jit(solution)/shard_map/settle/pallas_call | solution.py:601
  39.1 0.4 %collective-permute-done.9.rest_0_ = f32[32,16,128]{2,1,0:T(8,128)S(1)} collective-permute-done((f32[32,16,128]{2,1,0:T(8,128)S(1)}, f32[32,16,128]{2,1,0:T(8,128)S(1)}, u32[]{:S(2)}, u32[]{:S(2)}) %collective-permute-start.9) | collective-permute-done | bytes 262176 | tf_op jit(solution)/shard_map/ppermute | solution.py:632
  39.5 0.7 %settle_more.1 = f32[32,64,128]{2,1,0:T(8,128)} custom-call(f32[8,128]{1,0:T(8,128)S(1)} %get-tuple-element.78.scale_ref, f32[32,64,128]{2,1,0:T(8,128)S(1)} %copy-done.1, f32[32,16,128]{2,1,0:T(8,128)S(1)} %collective-permute-done.9.rest_0_, f32[32,64,128]{2,1,0:T(8,128)} %get-tuple-element.80.rest_1_), custom_call_target="tpu_custom_call", output_to_operand_aliasing={{}: (3, {})} | custom-call | tf_op jit(solution)/shard_map/settle_more/pallas_call | solution.py:611
  (1 shorter events, 0.0 us)
Async XLA Ops:
  0.0 5.3 %copy-start.5 = (f32[1,2,2,1024]{3,2,1,0:T(2,128)S(1)}, f32[1,2,2,1024]{3,2,1,0:T(2,128)}, u32[]{:S(2)}) copy-start(f32[1,2,2,1024]{3,2,1,0:T(2,128)} %param.7) | copy-start | bytes 49156
  0.0 6.1 %copy-start = (f32[1,2,2,1024,1024]{4,3,2,1,0:T(8,128)S(1)}, f32[1,2,2,1024,1024]{4,3,2,1,0:T(8,128)}, u32[]{:S(2)}) copy-start(f32[1,2,2,1024,1024]{4,3,2,1,0:T(8,128)} %param.6) | copy-start | bytes 50331652
  0.0 11.7 %copy-start.1 = (f32[32,64,128]{2,1,0:T(8,128)S(1)}, f32[32,64,128]{2,1,0:T(8,128)}, u32[]{:S(2)}) copy-start(f32[32,64,128]{2,1,0:T(8,128)} %old_ref.7) | copy-start | bytes 3145732
  0.0 11.7 %copy-start.2 = (s32[32,64,128]{2,1,0:T(8,128)S(1)}, s32[32,64,128]{2,1,0:T(8,128)}, u32[]{:S(2)}) copy-start(s32[32,64,128]{2,1,0:T(8,128)} %mesh_ref.3) | copy-start | bytes 3145732
  0.0 18.7 %copy-start.3 = (s32[32,16,128]{2,1,0:T(8,128)S(1)}, s32[32,16,128]{2,1,0:T(8,128)}, u32[]{:S(2)}) copy-start(s32[32,16,128]{2,1,0:T(8,128)} %regions_ref.3) | copy-start | bytes 786436
  0.0 18.7 %copy-start.4 = (f32[32,16,128]{2,1,0:T(8,128)S(1)}, f32[32,16,128]{2,1,0:T(8,128)}, u32[]{:S(2)}) copy-start(f32[32,16,128]{2,1,0:T(8,128)} %dopant_ref.3) | copy-start | bytes 786436
  1.4 9.5 %collective-permute-start = (f32[264,128]{1,0:T(8,128)S(1)}, f32[264,128]{1,0:T(8,128)S(1)}, u32[]{:S(2)}, u32[]{:S(2)}) collective-permute-start(f32[264,128]{1,0:T(8,128)S(1)} %get-tuple-element.47), channel_id=1, source_target_pairs={{0,1},{1,0},{2,3},{3,2},{4,5},{5,4},{6,7},{7,6},{8,9},{9,8},{10,11... | collective-permute-start | bytes 405512 | tf_op jit(solution)/shard_map/ppermute | solution.py:641
  4.5 6.5 %collective-permute-start.1 = (f32[264,128]{1,0:T(8,128)S(1)}, f32[264,128]{1,0:T(8,128)S(1)}, u32[]{:S(2)}, u32[]{:S(2)}) collective-permute-start(f32[264,128]{1,0:T(8,128)S(1)} %get-tuple-element.48), channel_id=1, source_target_pairs={{1,2},{2,1},{3,4},{4,3},{5,6},{6,5},{9,10},{10,9},{11,12},{12,11},... | collective-permute-start | bytes 405512 | tf_op jit(solution)/shard_map/ppermute | solution.py:641
  8.5 6.8 %collective-permute-start.4 = (f32[224,128]{1,0:T(8,128)S(1)}, f32[224,128]{1,0:T(8,128)S(1)}, u32[]{:S(2)}, u32[]{:S(2)}) collective-permute-start(f32[224,128]{1,0:T(8,128)S(1)} %get-tuple-element.50), channel_id=1, source_target_pairs={{0,24},{8,16},{16,8},{24,0},{1,25},{9,17},{17,9},{25,1},{2,26},{10... | collective-permute-start | bytes 344072 | tf_op jit(solution)/shard_map/ppermute | solution.py:632
  11.0 4.4 %collective-permute-start.2 = (f32[224,128]{1,0:T(8,128)S(1)}, f32[224,128]{1,0:T(8,128)S(1)}, u32[]{:S(2)}, u32[]{:S(2)}) collective-permute-start(f32[224,128]{1,0:T(8,128)S(1)} %get-tuple-element.49), channel_id=1, source_target_pairs={{0,8},{8,0},{16,24},{24,16},{1,9},{9,1},{17,25},{25,17},{2,10},{10... | collective-permute-start | bytes 344072 | tf_op jit(solution)/shard_map/ppermute | solution.py:632
  11.6 3.7 %collective-permute-start.3 = (f32[2,2,8,128]{3,2,1,0:T(8,128)S(1)}, f32[2,2,8,128]{3,2,1,0:T(8,128)S(1)}, u32[]{:S(2)}, u32[]{:S(2)}) collective-permute-start(f32[2,2,8,128]{3,2,1,0:T(8,128)S(1)} %get-tuple-element.56.refs_0_), channel_id=1, source_target_pairs={{0,16},{8,24},{16,0},{24,8},{1,17},{9,25},{17,1},{25,9},{2,18},{10... | collective-permute-start | bytes 49160 | tf_op jit(solution)/shard_map/ppermute | solution.py:632
  15.4 6.3 %collective-permute-start.5 = (f32[64,128]{1,0:T(8,128)S(1)}, f32[64,128]{1,0:T(8,128)S(1)}, u32[]{:S(2)}, u32[]{:S(2)}) collective-permute-start(f32[64,128]{1,0:T(8,128)S(1)} %get-tuple-element.60), channel_id=1, source_target_pairs={{0,1},{1,0},{2,3},{3,2},{4,5},{5,4},{6,7},{7,6},{8,9},{9,8},{10,11... | collective-permute-start | bytes 98312 | tf_op jit(solution)/shard_map/ppermute | solution.py:641
  18.0 3.7 %collective-permute-start.6 = (f32[64,128]{1,0:T(8,128)S(1)}, f32[64,128]{1,0:T(8,128)S(1)}, u32[]{:S(2)}, u32[]{:S(2)}) collective-permute-start(f32[64,128]{1,0:T(8,128)S(1)} %get-tuple-element.61), channel_id=1, source_target_pairs={{1,2},{2,1},{3,4},{4,3},{5,6},{6,5},{9,10},{10,9},{11,12},{12,11},... | collective-permute-start | bytes 98312 | tf_op jit(solution)/shard_map/ppermute | solution.py:641
  23.1 14.9 %collective-permute-start.7 = (f32[32,16,128]{2,1,0:T(8,128)S(1)}, f32[32,16,128]{2,1,0:T(8,128)S(1)}, u32[]{:S(2)}, u32[]{:S(2)}) collective-permute-start(f32[32,16,128]{2,1,0:T(8,128)S(1)} %get-tuple-element.76.rest_0_), channel_id=1, source_target_pairs={{0,16},{8,24},{16,0},{24,8},{1,17},{9,25},{17,1},{25,9},{2,18},{10... | collective-permute-start | bytes 786440 | tf_op jit(solution)/shard_map/ppermute | solution.py:632
  24.0 13.9 %all-to-all-start = ((f32[32,1,128]{2,1,0:T(1,128)}), f32[32,1,128]{2,1,0:T(1,128)S(1)}, u32[]{:S(2)}, u32[]{:S(2)}) async-start(f32[32,1,128]{2,1,0:T(1,128)} %get-tuple-element.75), calls=%async_computation | async-start | bytes 32768 | tf_op jit(solution)/shard_map/all_to_all | solution.py:667
  30.9 7.0 %collective-permute-start.8 = (f32[32,16,128]{2,1,0:T(8,128)S(1)}, f32[32,16,128]{2,1,0:T(8,128)S(1)}, u32[]{:S(2)}, u32[]{:S(2)}) collective-permute-start(f32[32,16,128]{2,1,0:T(8,128)S(1)} %get-tuple-element.76.rest_0_), channel_id=1, source_target_pairs={{0,8},{8,0},{16,24},{24,16},{1,9},{9,1},{17,25},{25,17},{2,10},{10... | collective-permute-start | bytes 786440 | tf_op jit(solution)/shard_map/ppermute | solution.py:632
  38.0 1.5 %collective-permute-start.9 = (f32[32,16,128]{2,1,0:T(8,128)S(1)}, f32[32,16,128]{2,1,0:T(8,128)S(1)}, u32[]{:S(2)}, u32[]{:S(2)}) collective-permute-start(f32[32,16,128]{2,1,0:T(8,128)S(1)} %collective-permute-done.7.rest_1_), channel_id=1, source_target_pairs={{0,8},{8,0},{16,24},{24,16},{1,9},{9,1},{17,25},{25,17},{2,10},{10... | collective-permute-start | bytes 786440 | tf_op jit(solution)/shard_map/ppermute | solution.py:632
